TPU v7x, 32 devices: a whole 2x2x4 slice. The times are simulated.
32 devices in a mesh: groups: 2 (over x), dp: 16 (over z, y, core).
Axes of the slice: x: 2, y: 2, z: 4, core: 2. Of those that a mesh axis runs over, the one named last changes fastest.
Arguments:
- features: bfloat16 [4096, 6144], P(('groups', 'dp')), parts along dimension 0, may hold values from -6 to 6
- grads: bfloat16 [4096, 16384], P(('groups', 'dp')), parts along dimension 0, may hold values from -6 to 6
- routes: int32 [4096, 2], P(('groups', 'dp')), parts along dimension 0, may hold values from 0 to 7, all different within a row; in each aligned block of 128 rows (0 to 127, 128 to 255, ...) at most 48 rows name the same one
- proj_in: bfloat16 [64, 49152], P(None, 'dp'), may hold values from -0.078125 to 0.078125
- proj_out: bfloat16 [64, 131072], P(None, 'dp'), may hold values from -0.046875 to 0.046875
- fisher_inverse: bfloat16 [4096, 4096], P(None, 'dp'), as said below
Outputs:
- preconditioned: float32 [32, 8, 4096], P(('groups', 'dp')), parts along dimension 0
There are 2 independent parts, one for each index of `groups`. A program takes and returns all parts, laid end to end along the dimension named above; an argument that names none is the same for every part. Nothing has to cross between parts.
Inputs may be any that keep to these rules, and one draw needn't show every extreme that they name: `routes`: the two experts of a token differ; among the 128 rows of one device no expert is named more than 48 times, and in every draw some expert is named exactly 48 times by the rows of some device. `fisher_inverse`: the matrix is symmetric.
All inputs are finite; a program needn't handle non-finite values.
Results may differ from a plain program's by a relative error of at most 0.0029.
Values may be sent and summed in bfloat16 or wider, within the bound.
No kernel may reach another device: no remote copies, remote signals or barrier semaphores. Data moves between devices by JAX's collectives and lax.ppermute only.
A program may use at most 128 MiB of HBM per device.

v0:
```python
import jax
import jax.numpy as jnp
from jax import lax
from jax.sharding import PartitionSpec as P

EXPERTS = 8
PROJ = 64
TOK_EX = 128
CAP = 48


def shards(features, grads, routes, proj_in, proj_out, fisher_inverse):
    n_dev = lax.axis_size("dp")
    slices = n_dev // EXPERTS
    tok = features.shape[0]
    width = features.shape[1]
    hidden = grads.shape[1]
    onehot = (routes[:, :, None] == jnp.arange(EXPERTS, dtype=jnp.int32)[None, None, :]).astype(
        jnp.int32
    )
    flat_hot = onehot.reshape(tok * 2, EXPERTS)
    ranks = jnp.cumsum(flat_hot, axis=0) - 1
    slot = jnp.sum(ranks * flat_hot, axis=1).reshape(tok, 2)
    position = routes * CAP + slot
    token_ids = jnp.repeat(jnp.arange(tok, dtype=jnp.int32), 2)
    owner = jnp.full((EXPERTS * CAP,), tok, jnp.int32).at[position.reshape(-1)].set(token_ids)
    owner = owner.reshape(EXPERTS, CAP)
    pick = owner[:, None, :] * slices + jnp.arange(slices, dtype=jnp.int32)[None, :, None]
    pick = pick.reshape(-1)
    send_in = jnp.take(
        features.reshape(tok * slices, width // slices), pick, axis=0, mode="fill", fill_value=0
    )
    send_in = send_in.reshape(EXPERTS * slices, CAP, width // slices)
    send_out = jnp.take(
        grads.reshape(tok * slices, hidden // slices), pick, axis=0, mode="fill", fill_value=0
    )
    send_out = send_out.reshape(EXPERTS * slices, CAP, hidden // slices)
    rows_in = lax.all_to_all(send_in, "dp", split_axis=0, concat_axis=0, tiled=True)
    rows_out = lax.all_to_all(send_out, "dp", split_axis=0, concat_axis=0, tiled=True)
    left = jnp.einsum("sid,pd->sip", rows_in, proj_in, preferred_element_type=jnp.float32)
    right = jnp.einsum("sif,pf->sip", rows_out, proj_out, preferred_element_type=jnp.float32)
    both = jnp.concatenate([left, right], axis=-1)
    back = lax.all_to_all(both, "dp", split_axis=0, concat_axis=0, tiled=True)
    projected = jnp.sum(back.reshape(EXPERTS, slices, CAP, 2 * PROJ), axis=1)
    per_token = jnp.take(projected.reshape(EXPERTS * CAP, 2 * PROJ), position.reshape(-1), axis=0)
    per_token = per_token.reshape(tok, 2, 2 * PROJ)
    dense = jnp.einsum(
        "tke,tkp->tep", onehot.astype(jnp.float32), per_token, precision=lax.Precision.HIGHEST
    )
    grouped = dense.reshape(tok // TOK_EX, TOK_EX, EXPERTS, 2 * PROJ)
    grams = jnp.einsum(
        "xtep,xteq->xepq", grouped[..., :PROJ], grouped[..., PROJ:], precision=lax.Precision.HIGHEST
    )
    grams = (
        (grams * TOK_EX ** (-0.5))
        .astype(jnp.bfloat16)
        .reshape(tok // TOK_EX * EXPERTS, PROJ * PROJ)
    )
    columns = jnp.dot(
        lax.all_gather(grams, "dp", axis=0, tiled=True),
        fisher_inverse,
        preferred_element_type=jnp.float32,
    )
    result = lax.all_to_all(columns, "dp", split_axis=0, concat_axis=1, tiled=True)
    return result.reshape(tok // TOK_EX, EXPERTS, PROJ * PROJ)


def solution(mesh):
    in_specs = (
        P(("groups", "dp"), None),
        P(("groups", "dp"), None),
        P(("groups", "dp"), None),
        P(None, "dp"),
        P(None, "dp"),
        P(None, "dp"),
    )
    out_specs = P(("groups", "dp"), None, None)
    return jax.shard_map(shards, mesh=mesh, in_specs=in_specs, out_specs=out_specs, check_vma=False)
```

profile of v0, /device:TPU:0, one launch (start us, length us, event | category | flops | bytes accessed | tf_op | source)
XLA Modules:
  0.0 506.0 jit_solution(18269640342623949914)
XLA Ops:
  6.5 0.0 copy-start
  6.5 0.9 copy.18
  7.5 0.1 eq.39
  7.6 0.1 eq.35
  7.8 0.6 reduce-window.6
  8.4 0.2 slice_reduce_fusion
  8.6 0.1 fusion.14
  8.7 0.1 reshape.167
  8.9 0.1 copy.21
  8.9 0.7 compare_and_fusion.1
  9.6 0.1 copy.23
  9.7 0.1 reshape.168
  9.9 0.1 reshape.207
  10.0 1.4 scatter_custom_fusion
  11.5 0.1 mul.35
  11.6 0.1 add.97
  11.7 3.5 reshape.170
  15.2 11.3 %gather_fusion = bf16[768,3072]{1,0:T(8,128)(2,1)} fusion(bf16[256,3072]{1,0:T(8,128)(2,1)} %reshape.170, s32[1024]{0:T(1024)S(1)} %pad_clamp_fusion.1), kind=kCustom, calls=%fused_computation | custom fusion | bytes 9440256 | tf_op jit(solution)/shard_map/jit(_take)/gather | solution.py:30
  26.5 4.8 broadcast_select_fusion.1
  31.3 7.4 %all-to-all-start = ((bf16[16,48,3072]{2,1,0:T(8,128)(2,1)}), bf16[16,48,3072]{2,1,0:T(8,128)(2,1)}, u32[]{:S(2)}, u32[]{:S(2)}) async-start(bf16[16,48,3072]{2,1,0:T(8,128)(2,1)} %broadcast_select_fusion.1), calls=%async_computation | async-start | bytes 9437184 | tf_op jit(solution)/shard_map/all_to_all | solution.py:38
  38.8 7.3 %reshape.171 = bf16[256,8192]{1,0:T(8,128)(2,1)} reshape(bf16[128,16384]{1,0:T(8,128)(2,1)} %param.7) | data formatting | bytes 8388608 | tf_op jit(solution)/shard_map/reshape | solution.py:35
  46.0 24.7 %gather_fusion.1 = bf16[768,8192]{1,0:T(8,128)(2,1)} fusion(bf16[256,8192]{1,0:T(8,128)(2,1)} %reshape.171, s32[1024]{0:T(1024)S(1)} %pad_clamp_fusion.1), kind=kCustom, calls=%fused_computation.1 | custom fusion | bytes 25168896 | tf_op jit(solution)/shard_map/jit(_take)/gather | solution.py:34
  70.7 10.7 %broadcast_select_fusion = bf16[16,48,8192]{2,1,0:T(8,128)(2,1)} fusion(bf16[16,48,8192]{2,1,0:T(8,128)(2,1)} %bitcast.35, pred[16,48]{1,0:T(8,128)(4,1)S(1)} %compare_and_fusion), kind=kLoop, calls=%fused_computation.4 | loop fusion | flops 6291456 | bytes 25166592 | tf_op jit(solution)/shard_map/jit(_take)/select_n | solution.py:34
  81.4 0.0 copy-start.1
  81.4 44.2 %all-to-all-done = bf16[16,48,3072]{2,1,0:T(8,128)(2,1)} async-done(((bf16[16,48,3072]{2,1,0:T(8,128)(2,1)}), bf16[16,48,3072]{2,1,0:T(8,128)(2,1)}, u32[]{:S(2)}, u32[]{:S(2)}) %all-to-all-start) | async-done | bytes 4718624 | tf_op jit(solution)/shard_map/all_to_all | solution.py:38
  125.6 21.8 %all-to-all-start.1 = ((bf16[16,48,8192]{2,1,0:T(8,128)(2,1)}), bf16[16,48,8192]{2,1,0:T(8,128)(2,1)}, u32[]{:S(2)}, u32[]{:S(2)}) async-start(bf16[16,48,8192]{2,1,0:T(8,128)(2,1)} %broadcast_select_fusion), calls=%async_computation.1 | async-start | bytes 25165824 | tf_op jit(solution)/shard_map/all_to_all | solution.py:39
  147.4 0.0 copy-done.1
  147.4 3.7 fusion.5
  151.1 220.0 %all-to-all-done.1 = bf16[16,48,8192]{2,1,0:T(8,128)(2,1)} async-done(((bf16[16,48,8192]{2,1,0:T(8,128)(2,1)}), bf16[16,48,8192]{2,1,0:T(8,128)(2,1)}, u32[]{:S(2)}, u32[]{:S(2)}) %all-to-all-start.1) | async-done | bytes 12582944 | tf_op jit(solution)/shard_map/all_to_all | solution.py:39
  371.1 6.7 %fusion.1 = f32[16,48,64]{2,1,0:T(8,128)S(1)} fusion(bf16[16,48,8192]{2,1,0:T(8,128)(2,1)} %all-to-all-done.1, bf16[64,8192]{1,0:T(8,128)(2,1)} %param.10), kind=kOutput, calls=%fused_computation.10 | convolution fusion | flops 805306368 | bytes 13828096 | tf_op jit(solution)/shard_map/sif,pf->sip/dot_general | solution.py:41
  377.8 0.9 pad_maximum_fusion
  378.7 53.3 %all-to-all-start.2 = ((f32[16,48,128]{2,1,0:T(8,128)}), f32[16,48,128]{2,1,0:T(8,128)S(1)}, u32[]{:S(2)}, u32[]{:S(2)}) async-start(f32[16,48,128]{2,1,0:T(8,128)} %pad_maximum_fusion), calls=%async_computation.2 | async-start | bytes 786432 | tf_op jit(solution)/shard_map/all_to_all | solution.py:43
  432.1 0.3 all-gather.2.cloned.1.call-start
  432.4 0.1 copy.22
  432.5 11.8 %all-to-all-done.2 = f32[16,48,128]{2,1,0:T(8,128)S(1)} async-done(((f32[16,48,128]{2,1,0:T(8,128)}), f32[16,48,128]{2,1,0:T(8,128)S(1)}, u32[]{:S(2)}, u32[]{:S(2)}) %all-to-all-start.2) | async-done | bytes 393248 | tf_op jit(solution)/shard_map/all_to_all | solution.py:43
  444.3 0.7 gather_fusion.2
  445.0 1.4 convolution_bitcast_fusion
  446.5 0.2 slice_bitcast_fusion.1
  446.7 1.0 fusion
  447.7 0.8 reshape.177
  448.5 0.0 all-gather.2.cloned.1.call-update
  448.5 36.9 %all-gather.2.cloned.1.call-done = bf16[128,4096]{1,0:T(8,128)(2,1)} async-done(((bf16[8,4096]{1,0:T(8,128)(2,1)}), bf16[128,4096]{1,0:T(8,128)(2,1)}) %all-gather.2.cloned.1.call-update) | async-done | bytes 1048592 | tf_op jit(solution)/shard_map/all_gather | solution.py:60
  485.5 0.0 copy-done
  485.5 1.7 convolution_bitcast_fusion.1
  487.2 11.4 %all_to_all.31 = f32[16,8,256]{2,1,0:T(8,128)S(1)} all-to-all(f32[16,8,256]{2,1,0:T(8,128)S(1)} %convolution_bitcast_fusion.1), channel_id=1, replica_groups=mesh['groups'=2,'dp'=16] {'dp'}, dimensions={0} | all-to-all | bytes 262144 | tf_op jit(solution)/shard_map/all_to_all | solution.py:64
  498.5 0.7 copy.31
  (12 shorter events, 0.1 us)
Async XLA Ops:
  6.5 479.0 %copy-start = (bf16[4096,256]{1,0:T(8,128)(2,1)S(1)}, bf16[4096,256]{1,0:T(8,128)(2,1)}, u32[]{:S(2)}) copy-start(bf16[4096,256]{1,0:T(8,128)(2,1)} %param.11) | copy-start | bytes 6291460
  31.3 94.2 %all-to-all-start = ((bf16[16,48,3072]{2,1,0:T(8,128)(2,1)}), bf16[16,48,3072]{2,1,0:T(8,128)(2,1)}, u32[]{:S(2)}, u32[]{:S(2)}) async-start(bf16[16,48,3072]{2,1,0:T(8,128)(2,1)} %broadcast_select_fusion.1), calls=%async_computation | async-start | bytes 9437184 | tf_op jit(solution)/shard_map/all_to_all | solution.py:38
  81.4 66.0 %copy-start.1 = (bf16[64,3072]{1,0:T(8,128)(2,1)S(1)}, bf16[64,3072]{1,0:T(8,128)(2,1)}, u32[]{:S(2)}) copy-start(bf16[64,3072]{1,0:T(8,128)(2,1)} %param.9) | copy-start | bytes 1179652
  125.6 245.5 %all-to-all-start.1 = ((bf16[16,48,8192]{2,1,0:T(8,128)(2,1)}), bf16[16,48,8192]{2,1,0:T(8,128)(2,1)}, u32[]{:S(2)}, u32[]{:S(2)}) async-start(bf16[16,48,8192]{2,1,0:T(8,128)(2,1)} %broadcast_select_fusion), calls=%async_computation.1 | async-start | bytes 25165824 | tf_op jit(solution)/shard_map/all_to_all | solution.py:39
  378.7 65.5 %all-to-all-start.2 = ((f32[16,48,128]{2,1,0:T(8,128)}), f32[16,48,128]{2,1,0:T(8,128)S(1)}, u32[]{:S(2)}, u32[]{:S(2)}) async-start(f32[16,48,128]{2,1,0:T(8,128)} %pad_maximum_fusion), calls=%async_computation.2 | async-start | bytes 786432 | tf_op jit(solution)/shard_map/all_to_all | solution.py:43
  432.1 53.4 %all-gather.2.cloned.1.call-start = ((), (), s32[]{:S(2)}) async-start(), calls=%async_computation.4 | async-start | bytes 1114112 | tf_op jit(solution)/shard_map/all_gather | solution.py:60
Sparse Core Ops, SparseCore 0:
  448.7 36.7 all-gather.1
where the time goes:
time: 507 us; the launch traced here: 506 us
  waiting for transfers between devices  313 us (62%)
  starting transfers between devices  82.8 us (16%)
  local copies, waits for them, and re-layouts  52.9 us (10%)
  other arithmetic  17.9 us (4%)
  matrix products  14.5 us (3%)
  between operations  13.6 us (3%)
  blocking collectives  11.4 us (2%)
    all_to_all x1, waiting for transfers between devices, shards(): lax.all_to_all(send_out, 'dp', split_axis=0, concat_axis=0, tiled=True)  220 us
    all_to_all x1, starting transfers between devices, shards(): back = lax.all_to_all(both, 'dp', split_axis=0, concat_axis=0, tiled=True)  53.3 us
    all_to_all x1, waiting for transfers between devices, shards(): lax.all_to_all(send_in, 'dp', split_axis=0, concat_axis=0, tiled=True)  44.2 us
    all_gather x1, waiting for transfers between devices, shards(): lax.all_gather(grams, 'dp', axis=0, tiled=True)  36.9 us
    gather x1, local copies, waits for them, and re-layouts, shards(): jnp.take(grads.reshape(tok * slices, hidden // slices), pick, axis=0, mod...  24.7 us
    all_to_all x1, starting transfers between devices, shards(): lax.all_to_all(send_out, 'dp', split_axis=0, concat_axis=0, tiled=True)  21.8 us
    all_to_all x1, waiting for transfers between devices, shards(): back = lax.all_to_all(both, 'dp', split_axis=0, concat_axis=0, tiled=True)  11.8 us
    all_to_all x1, blocking collectives, shards(): lax.all_to_all(columns, 'dp', split_axis=0, concat_axis=1, tiled=True)  11.4 us
  transfers between devices with their start and end apart: 4, of which 4 were waited for; matrix products, arithmetic and copies ran while one was open for 9% of the time, Pallas kernels for 0%

commit v1 on v0

v1 whole, which is shorter than its diff:
```python
import math

import jax
import jax.numpy as jnp
from jax import lax
from jax.experimental import pallas as pl
from jax.experimental.pallas import tpu as pltpu
from jax.sharding import PartitionSpec as P

EXPERTS = 8
PROJ = 64
TOK = 128
LANES = 128
VMEM = 48 * 1024 * 1024
AXES = ("groups", "dp")


def project_kernel(n_pieces, sub, n_in, n_a, n_k, eid_ref, *refs):
    toks = refs[: 4 * sub]
    w_a = refs[4 * sub : 4 * sub + n_pieces]
    w_b = refs[4 * sub + n_pieces : 4 * sub + 2 * n_pieces]
    routes_ref, out_ref, left, right = refs[4 * sub + 2 * n_pieces :]
    step = pl.program_id(0)

    @pl.when(step == 0)
    def _():
        left[...] = jnp.zeros_like(left)
        right[...] = jnp.zeros_like(right)

    def add(weights, total):
        table = jnp.concatenate([w[...] for w in weights], axis=0)
        for a in range(sub):
            rows = jnp.concatenate([toks[a * 4 + b][...] for b in range(4)], axis=0)
            total[a] += lax.dot_general(
                rows, table, (((1,), (1,)), ((), ())), preferred_element_type=jnp.float32
            )

    @pl.when(step < n_in)
    def _():
        add(w_a, left)

    @pl.when((step >= n_in) & (step < n_a))
    def _():
        add(w_a, right)

    @pl.when(step >= n_a)
    def _():
        add(w_b, right)

    @pl.when(step == n_k - 1)
    def _():
        low = lax.broadcasted_iota(jnp.int32, (TOK, LANES), 1) < PROJ
        for b in range(4):
            for k in range(2):
                own = routes_ref[b * TOK : (b + 1) * TOK, k : k + 1]
                picked = [jnp.zeros((TOK, LANES), jnp.float32) for _ in range(2)]
                for a in range(sub):
                    for pair in range(n_pieces // 2):
                        wanted = jnp.where(
                            low,
                            jnp.where(eid_ref[1, 2 * pair] == a, eid_ref[0, 2 * pair], -1),
                            jnp.where(eid_ref[1, 2 * pair + 1] == a, eid_ref[0, 2 * pair + 1], -1),
                        )
                        mask = own == wanted
                        for side, total in enumerate((left, right)):
                            block = total[a, b * TOK : (b + 1) * TOK, pair * LANES : (pair + 1) * LANES]
                            picked[side] += jnp.where(mask, block, 0.0)
                both = [x + pltpu.roll(x, PROJ, 1) for x in picked]
                out_ref[b, :, k * LANES : (k + 1) * LANES] = jnp.where(low, both[0], both[1])


def project(toks, pieces_a, pieces_b, routes, eid, sub, n_in, n_a, n_k, width):
    n_pieces = len(pieces_a)
    n_b = n_k - n_a

    def tok_spec(a):
        return pl.BlockSpec((TOK, width), lambda k, a=a: (0, a * n_k + k))

    specs = [pl.BlockSpec(memory_space=pltpu.SMEM)]
    operands = [eid]
    for a in range(sub):
        for tok in toks:
            specs.append(tok_spec(a))
            operands.append(tok)
    for piece in pieces_a:
        specs.append(pl.BlockSpec((PROJ, width), lambda k: (0, jnp.minimum(k, n_a - 1))))
        operands.append(piece)
    for piece in pieces_b:
        specs.append(pl.BlockSpec((PROJ, width), lambda k: (0, jnp.maximum(k - n_a, 0))))
        operands.append(piece)
    specs.append(pl.BlockSpec((4 * TOK, 2), lambda k: (0, 0)))
    operands.append(routes)
    total = pltpu.VMEM((sub, 4 * TOK, n_pieces * PROJ), jnp.float32)
    return pl.pallas_call(
        lambda *refs: project_kernel(n_pieces, sub, n_in, n_a, n_k, *refs),
        grid=(n_k,),
        in_specs=specs,
        out_specs=pl.BlockSpec((4, TOK, 4 * PROJ), lambda k: (0, 0, 0)),
        out_shape=jax.ShapeDtypeStruct((4, TOK, 4 * PROJ), jnp.float32),
        scratch_shapes=[total, total],
        compiler_params=pltpu.CompilerParams(vmem_limit_bytes=VMEM),
        name="project",
    )(*operands)


def gram_kernel(p0, p1, p2, p3, routes_ref, out_ref, flat):
    total = (p0[...] + p1[...]) + (p2[...] + p3[...])
    first, second = total[:, :LANES], total[:, LANES:]
    left = jnp.concatenate([jnp.transpose(first)[:PROJ], jnp.transpose(second)[:PROJ]], axis=1)
    right = jnp.concatenate([first, second], axis=0)
    named = routes_ref[...]
    rows = jnp.concatenate([jnp.where(named == e, left, 0.0) for e in range(EXPERTS)], axis=0)
    grams = lax.dot_general(
        rows,
        right,
        (((1,), (0,)), ((), ())),
        precision=lax.Precision.HIGHEST,
        preferred_element_type=jnp.float32,
    )
    grams = grams * (TOK**-0.5)
    low = lax.broadcasted_iota(jnp.int32, (PROJ // 2, LANES), 1) < PROJ
    for e in range(EXPERTS):
        top = grams[e * PROJ : e * PROJ + PROJ // 2]
        bottom = grams[e * PROJ + PROJ // 2 : (e + 1) * PROJ]
        flat[:, e, :] = jnp.where(low, pltpu.roll(top, PROJ, 1), bottom)
    out_ref[...] = flat[...].reshape(PROJ // 4, 2 * EXPERTS, LANES).astype(jnp.bfloat16)


def gram(parts, routes):
    return pl.pallas_call(
        gram_kernel,
        out_shape=jax.ShapeDtypeStruct((PROJ // 4, 2 * EXPERTS, LANES), jnp.bfloat16),
        scratch_shapes=[pltpu.VMEM((PROJ // 2, EXPERTS, LANES), jnp.float32)],
        name="gram",
    )(*parts, routes)


def fisher_kernel(n, order_ref, *refs):
    own, other = refs[: n // 2], refs[n // 2]
    fisher, out_ref = refs[n // 2 + 1 :]
    total = jnp.zeros((n * EXPERTS, fisher.shape[1]), jnp.float32)
    for i in range(PROJ // 4):
        tiles = [x[i] for x in own] + [other[j, i] for j in range(n // 2)]
        rows = jnp.concatenate([x.astype(jnp.float32).reshape(1, 2, EXPERTS, LANES) for x in tiles], axis=0)
        for h in range(2):
            p = 2 * i + h
            table = jnp.concatenate(
                [
                    fisher[p * PROJ : (p + 1) * PROJ, :],
                    fisher[(PROJ // 2 + p) * PROJ : (PROJ // 2 + p + 1) * PROJ, :],
                ],
                axis=0,
            )
            lhs = rows[:, h].reshape(n * EXPERTS, LANES).astype(jnp.bfloat16)
            total += jnp.dot(lhs, table, preferred_element_type=jnp.float32)
    for j in range(n):
        out_ref[order_ref[j]] = total[j * EXPERTS : (j + 1) * EXPERTS]


def precondition(own, other, fisher, order):
    n = 2 * len(own)
    vmem = pl.BlockSpec(memory_space=pltpu.VMEM)
    return pl.pallas_call(
        lambda *refs: fisher_kernel(n, *refs),
        in_specs=[pl.BlockSpec(memory_space=pltpu.SMEM)] + [vmem] * (n // 2 + 2),
        out_specs=vmem,
        out_shape=jax.ShapeDtypeStruct((n, EXPERTS, fisher.shape[1]), jnp.float32),
        compiler_params=pltpu.CompilerParams(vmem_limit_bytes=VMEM),
        name="precondition",
    )(order, *own, other, fisher)


def shards(features, grads, routes, proj_in, proj_out, fisher_inverse):
    groups, n = lax.axis_size("groups"), lax.axis_size("dp")
    chips = n // 2
    slices = n // EXPERTS
    sub = slices // 2
    y_size = 2 if groups == 2 else 1
    z_size = chips // y_size
    group, place = lax.axis_index("groups"), lax.axis_index("dp")
    core, chip, half = place % 2, place // 2, group % 2
    z, y = chip // y_size, chip % y_size

    def move(x, to):
        pairs = []
        for g in range(groups):
            for d in range(n):
                tg, td = to(g, d)
                pairs.append((g * n + d, tg * n + td))
        return lax.ppermute(x, AXES, pairs)

    def to_core(g, d):
        return g, d ^ 1

    def to_x(g, d):
        return g ^ 1, d

    def to_x_core(g, d):
        return g ^ 1, d ^ 1

    def to_y(g, d):
        return g, d ^ 2

    def to_z(g, d):
        return g, (d + 2 * y_size) % n

    quarter_in, quarter_out = proj_in.shape[1] // 2, proj_out.shape[1] // 2

    def token_columns(c, h):
        parts = []
        for a in range(sub):
            at = (a * 2 + c) * 2 + h
            parts.append(lax.dynamic_slice_in_dim(features, at * quarter_in, quarter_in, 1))
            parts.append(lax.dynamic_slice_in_dim(grads, at * quarter_out, quarter_out, 1))
        return jnp.concatenate(parts, axis=1)

    table = jnp.concatenate(
        [
            lax.dynamic_slice_in_dim(proj_in, half * quarter_in, quarter_in, 1),
            lax.dynamic_slice_in_dim(proj_out, half * quarter_out, quarter_out, 1),
        ],
        axis=1,
    )
    width = math.gcd(quarter_in, quarter_out)
    n_k = (quarter_in + quarter_out) // width
    n_in = quarter_in // width
    n_a = max(n_in, (n_k + 1) // 2)
    first = [table[:, : n_a * width]]
    second = [table[:, n_a * width :]]

    tok_x = move(token_columns(core, 1 - half), to_x)
    tok_x_core = move(token_columns(1 - core, 1 - half), to_x_core)
    for _ in range(z_size - 1):
        first.append(move(first[-1], to_z))
        second.append(move(second[-1], to_z))
    chip_ids = [((z - k) % z_size) * y_size + y for k in range(z_size)]
    if y_size == 2:
        for k in range(z_size):
            first.append(move(first[k], to_y))
            second.append(move(second[k], to_y))
            chip_ids.append(((z - k) % z_size) * y_size + (1 - y))
    tok_core = move(token_columns(1 - core, half), to_core)
    tok_own = token_columns(core, half)
    pair_routes = jnp.concatenate([routes, move(routes, to_core)], axis=0)
    all_routes = jnp.concatenate([pair_routes, move(pair_routes, to_x)], axis=0)
    chip_ids = jnp.stack(chip_ids).astype(jnp.int32)
    eid = jnp.stack([2 * chip_ids // slices, 2 * chip_ids % slices // 2])

    partial = project(
        [tok_own, tok_core, tok_x, tok_x_core], first, second, all_routes, eid, sub, n_in, n_a, n_k, width
    )
    sums = [partial[0], move(partial[1], to_core), move(partial[2], to_x), move(partial[3], to_x_core)]
    mine = gram(sums, routes.T.reshape(1, -1))

    own = [mine]
    for k in range(1, chips):
        own.append(move(mine, lambda g, d, k=k: (g, d ^ (2 * k))))
    other = move(jnp.stack(own), to_core)
    steps = jnp.arange(chips, dtype=jnp.int32)
    order = jnp.concatenate([(chip ^ steps) * 2 + core, (chip ^ steps) * 2 + (1 - core)])
    columns = precondition(own, other, fisher_inverse, order.astype(jnp.int32))
    result = lax.all_to_all(columns, "dp", split_axis=0, concat_axis=0, tiled=True)
    return jnp.transpose(result, (1, 0, 2)).reshape(1, EXPERTS, PROJ * PROJ)


def solution(mesh):
    in_specs = (
        P(AXES, None),
        P(AXES, None),
        P(AXES, None),
        P(None, "dp"),
        P(None, "dp"),
        P(None, "dp"),
    )
    out_specs = P(AXES, None, None)
    return jax.shard_map(shards, mesh=mesh, in_specs=in_specs, out_specs=out_specs, check_vma=False)
```

time: 507 us -> 169 us (0.33)
  waiting for transfers between devices: 313 us -> 86.4 us
  starting transfers between devices: 82.8 us -> 31.9 us
  local copies, waits for them, and re-layouts: 52.9 us -> 16.6 us
  Pallas kernels: 0 us -> 15.4 us
  matrix products: 14.5 us -> 0 us
  between operations: 13.6 us -> 0.19 us
  other arithmetic: 17.9 us -> 5.13 us
    all_to_all x3 -> x0, waiting for transfers between devices: 276 us -> none  [the longest x1 220 us: shards(): lax.all_to_all(send_out, 'dp', split_axis=0, concat_axis=0, tiled=True)]
    ppermute x0 -> x30, waiting for transfers between devices: none -> 86.4 us  [move(): return lax.ppermute(x, AXES, pairs)]
    all_to_all x3 -> x0, starting transfers between devices: 82.6 us -> none  [the longest x1 53.3 us: shards(): back = lax.all_to_all(both, 'dp', split_axis=0, concat_axis=0, tiled=True)]
    all_gather x1 -> x0, waiting for transfers between devices: 36.9 us -> none  [shards(): lax.all_gather(grams, 'dp', axis=0, tiled=True)]
    gather x3 -> x0, local copies, waits for them, and re-layouts: 36.7 us -> none  [the longest x1 24.7 us: shards(): jnp.take(grads.reshape(tok * slices, hidden // slices), pick, axis=0, mod...]
    ppermute x0 -> x30, starting transfers between devices: none -> 31.9 us  [move(): return lax.ppermute(x, AXES, pairs)]
    select_n x4 -> x2, other arithmetic: 15.5 us -> 0.02 us  [shards(): eid = jnp.stack([2 * chip_ids // slices, 2 * chip_ids % slices // 2])]
    pallas_call x0 -> x3, Pallas kernels: none -> 15.4 us  [the longest x1 11.7 us: project(): pl.pallas_call(lambda *refs: project_kernel(n_pieces, sub, n_in, n_a, n_k...]
  transfers between devices with their start and end apart: 4 -> 30, of which waited for: 4 -> 14; matrix products, arithmetic and copies ran while one was open for 9% -> 5% of each run, Pallas kernels for 0% -> 0%
where the time goes in v1:
time: 169 us; the launch traced here: 168 us
  waiting for transfers between devices  86.4 us (51%)
  starting transfers between devices  31.9 us (19%)
  local copies, waits for them, and re-layouts  16.6 us (10%)
  Pallas kernels  15.4 us (9%)
  blocking collectives  12.7 us (8%)
  other arithmetic  5.13 us (3%)
    ppermute x30, waiting for transfers between devices, move(): return lax.ppermute(x, AXES, pairs)  86.4 us
    ppermute x30, starting transfers between devices, move(): return lax.ppermute(x, AXES, pairs)  31.9 us
    all_to_all x1, blocking collectives, shards(): lax.all_to_all(columns, 'dp', split_axis=0, concat_axis=0, tiled=True)  12.7 us
    pallas_call x1, Pallas kernels, project(): pl.pallas_call(lambda *refs: project_kernel(n_pieces, sub, n_in, n_a, n_k...  11.7 us
    unnamed x40, local copies, waits for them, and re-layouts  10.5 us
    concatenate x4, other arithmetic, token_columns(): return jnp.concatenate(parts, axis=1)  4.97 us
  transfers between devices with their start and end apart: 30, of which 14 were waited for; matrix products, arithmetic and copies ran while one was open for 5% of the time, Pallas kernels for 0%

profile of v1, /device:TPU:0, one launch (start us, length us, event | category | flops | bytes accessed | tf_op | source)
XLA Modules:
  0.0 168.2 jit_solution(4094344214939669690)
XLA Ops:
  0.0 1.2 copy-done
  1.3 0.9 constant_dynamic-slice_fusion.2
  2.3 3.1 %collective-permute-start.3 = (bf16[64,3072]{1,0:T(8,128)(2,1)S(1)}, bf16[64,3072]{1,0:T(8,128)(2,1)S(1)}, u32[]{:S(2)}, u32[]{:S(2)}) collective-permute-start(bf16[64,3072]{1,0:T(8,128)(2,1)S(1)} %pad_maximum_fusion.4.refs_5_), channel_id=1, source_target_pairs={{0,4},{1,5},{2,6},{3,7},{4,8},{5,9},{6,10},{7,11},{8,12},{9,13},{1... | collective-permute-start | bytes 1179656 | tf_op jit(solution)/shard_map/ppermute | solution.py:190
  5.3 1.5 collective-permute-start.6
  6.9 1.6 collective-permute-start.10
  8.5 0.5 collective-permute-start.13
  9.0 2.8 %constant_dynamic-slice_fusion.3 = (bf16[128,4096]{1,0:T(8,128)(2,1)S(1)}, bf16[128,4096]{1,0:T(8,128)(2,1)S(1)}, bf16[128,4096]{1,0:T(8,128)(2,1)S(1)}, bf16[128,4096]{1,0:T(8,128)(2,1)S(1)}) fusion(bf16[128,16384]{1,0:T(8,128)(2,1)} %param.7, s32[]{:T(128)S(6)} %select_n.130, s32[]{:T(128)S(6)} %select_n.126, s32[]{:T(128)S(6)} %select_n.124, s32[]{:T(128)S(6)} %select_n.128), kind=kLoop, calls=%fused_computation.21 | loop fusion | bytes 8388624 | tf_op jit(solution)/shard_map/dynamic_slice | solution.py:214
  11.8 0.1 constant_dynamic-slice_fusion.4
  11.9 1.2 pad_maximum_fusion.1
  13.2 1.5 collective-permute-start.18
  14.7 8.8 %collective-permute-done.10.refs_14_ = bf16[64,2560]{1,0:T(8,128)(2,1)S(1)} collective-permute-done((bf16[64,2560]{1,0:T(8,128)(2,1)S(1)}, bf16[64,2560]{1,0:T(8,128)(2,1)S(1)}, u32[]{:S(2)}, u32[]{:S(2)}) %collective-permute-start.10) | collective-permute-done | bytes 327712 | tf_op jit(solution)/shard_map/ppermute | solution.py:190
  23.5 1.3 pad_maximum_fusion.2
  24.8 1.5 collective-permute-start.14
  26.3 1.3 collective-permute-start.4
  27.6 0.5 collective-permute-start.7
  28.1 7.8 %collective-permute-done.11.refs_15_ = bf16[64,2560]{1,0:T(8,128)(2,1)S(1)} collective-permute-done((bf16[64,2560]{1,0:T(8,128)(2,1)S(1)}, bf16[64,2560]{1,0:T(8,128)(2,1)S(1)}, u32[]{:S(2)}, u32[]{:S(2)}) %collective-permute-start.11) | collective-permute-done | bytes 327712 | tf_op jit(solution)/shard_map/ppermute | solution.py:190
  36.0 1.6 collective-permute-start.15
  37.5 1.2 pad_maximum_fusion.3
  38.8 0.7 copy-done.7
  39.5 4.9 %collective-permute-done.4.refs_7_ = bf16[64,3072]{1,0:T(8,128)(2,1)S(1)} collective-permute-done((bf16[64,3072]{1,0:T(8,128)(2,1)S(1)}, bf16[64,3072]{1,0:T(8,128)(2,1)S(1)}, u32[]{:S(2)}, u32[]{:S(2)}) %collective-permute-start.4) | collective-permute-done | bytes 393248 | tf_op jit(solution)/shard_map/ppermute | solution.py:190
  44.4 1.5 collective-permute-start.1
  45.9 0.7 copy-done.3
  46.6 3.1 %collective-permute-done.12.refs_16_ = bf16[64,2560]{1,0:T(8,128)(2,1)} collective-permute-done((bf16[64,2560]{1,0:T(8,128)(2,1)S(1)}, bf16[64,2560]{1,0:T(8,128)(2,1)}, u32[]{:S(2)}, u32[]{:S(2)}) %collective-permute-start.12) | collective-permute-done | bytes 327712 | tf_op jit(solution)/shard_map/ppermute | solution.py:190
  49.8 0.7 copy-done.9
  50.5 1.3 collective-permute-start.8
  51.7 1.3 pad_maximum_fusion.refs_1_
  53.0 0.1 stack.67
  53.1 7.9 %collective-permute-done.5.refs_8_ = bf16[64,3072]{1,0:T(8,128)(2,1)} collective-permute-done((bf16[64,3072]{1,0:T(8,128)(2,1)S(1)}, bf16[64,3072]{1,0:T(8,128)(2,1)}, u32[]{:S(2)}, u32[]{:S(2)}) %collective-permute-start.5) | collective-permute-done | bytes 393248 | tf_op jit(solution)/shard_map/ppermute | solution.py:190
  61.0 1.0 collective-permute-start.16
  62.1 1.0 collective-permute-start.9
  63.1 0.1 copy.10.refs_21_
  63.3 8.7 %collective-permute-done.16.refs_20_ = bf16[64,2560]{1,0:T(8,128)(2,1)} collective-permute-done((bf16[64,2560]{1,0:T(8,128)(2,1)}, bf16[64,2560]{1,0:T(8,128)(2,1)}, u32[]{:S(2)}, u32[]{:S(2)}) %collective-permute-start.16) | collective-permute-done | bytes 327712 | tf_op jit(solution)/shard_map/ppermute | solution.py:190
  72.0 7.2 %collective-permute-done.1.refs_3_ = bf16[128,5632]{1,0:T(8,128)(2,1)} collective-permute-done((bf16[128,5632]{1,0:T(8,128)(2,1)}, bf16[128,5632]{1,0:T(8,128)(2,1)}, u32[]{:S(2)}, u32[]{:S(2)}) %collective-permute-start.1) | collective-permute-done | bytes 1441824 | tf_op jit(solution)/shard_map/ppermute | solution.py:190
  79.2 25.0 %collective-permute-done.2.refs_4_ = bf16[128,5632]{1,0:T(8,128)(2,1)} collective-permute-done((bf16[128,5632]{1,0:T(8,128)(2,1)}, bf16[128,5632]{1,0:T(8,128)(2,1)}, u32[]{:S(2)}, u32[]{:S(2)}) %collective-permute-start.2) | collective-permute-done | bytes 1441824 | tf_op jit(solution)/shard_map/ppermute | solution.py:190
  104.2 1.0 copy-done.4
  105.2 1.0 copy-done.6
  106.2 1.0 copy-done.8
  107.1 1.0 copy-done.10
  108.1 11.7 %project.1 = f32[4,128,256]{2,1,0:T(8,128)} custom-call(s32[2,8]{1,0:T(2,128)S(1)} %pad_add_fusion.2.refs_0_, bf16[128,5632]{1,0:T(8,128)(2,1)} %pad_maximum_fusion.refs_1_, bf16[128,5632]{1,0:T(8,128)(2,1)} %collective-permute-done.refs_2_, bf16[128,5632]{1,0:T(8,128)(2,1)} %collective-permute-done.1.refs_3_, ...), custom_call_target="tpu_custom_call" | custom-call | tf_op jit(solution)/shard_map/project/pallas_call | solution.py:94
  119.8 1.9 %slice_bitcast_fusion = (f32[128,256]{1,0:T(8,128)S(1)}, f32[128,256]{1,0:T(8,128)S(1)}, f32[128,256]{1,0:T(8,128)S(1)}, f32[128,256]{1,0:T(8,128)}) fusion(f32[4,128,256]{2,1,0:T(8,128)} %project.1), kind=kLoop, calls=%fused_computation.5 | loop fusion | bytes 1048576 | tf_op jit(solution)/shard_map/squeeze | solution.py:252
  121.7 1.3 collective-permute-start.19
  123.1 1.0 collective-permute-start.20
  124.0 0.4 collective-permute-start.21
  124.4 5.0 %collective-permute-done.20.p2 = f32[128,256]{1,0:T(8,128)S(1)} collective-permute-done((f32[128,256]{1,0:T(8,128)S(1)}, f32[128,256]{1,0:T(8,128)S(1)}, u32[]{:S(2)}, u32[]{:S(2)}) %collective-permute-start.20) | collective-permute-done | bytes 131104 | tf_op jit(solution)/shard_map/ppermute | solution.py:190
  129.4 0.9 collective-permute-done.21.p3
  130.3 0.6 copy-done.14
  131.0 2.4 %gram.1.refs_1_ = bf16[16,16,128]{2,1,0:T(8,128)(2,1)} custom-call(f32[128,256]{1,0:T(8,128)} %get-tuple-element.18.p0, f32[128,256]{1,0:T(8,128)} %copy-done.12, f32[128,256]{1,0:T(8,128)} %copy-done.13, f32[128,256]{1,0:T(8,128)} %copy-done.14, s32[1,256]{1,0:T(1,128)} %bitcast.39), custom_call_target="tpu_custom_call" | custom-call | tf_op jit(solution)/shard_map/gram/pallas_call | solution.py:130
  133.4 1.0 collective-permute-start.22
  134.4 2.4 %collective-permute-start.24 = (bf16[16,16,128]{2,1,0:T(8,128)(2,1)}, bf16[16,16,128]{2,1,0:T(8,128)(2,1)S(1)}, u32[]{:S(2)}, u32[]{:S(2)}) collective-permute-start(bf16[16,16,128]{2,1,0:T(8,128)(2,1)} %gram.1.refs_1_), channel_id=1, source_target_pairs={{0,6},{1,7},{2,4},{3,5},{4,2},{5,3},{6,0},{7,1},{8,14},{9,15},{10,... | collective-permute-start | bytes 196616 | tf_op jit(solution)/shard_map/ppermute | solution.py:190
  136.9 1.4 collective-permute-start.25
  138.2 2.0 %collective-permute-start.26 = (bf16[16,16,128]{2,1,0:T(8,128)(2,1)}, bf16[16,16,128]{2,1,0:T(8,128)(2,1)S(1)}, u32[]{:S(2)}, u32[]{:S(2)}) collective-permute-start(bf16[16,16,128]{2,1,0:T(8,128)(2,1)} %gram.1.refs_1_), channel_id=1, source_target_pairs={{0,10},{1,11},{2,8},{3,9},{4,14},{5,15},{6,12},{7,13},{8,2},{9,3},... | collective-permute-start | bytes 196616 | tf_op jit(solution)/shard_map/ppermute | solution.py:190
  140.3 0.9 bitcast_dynamic-update-slice_fusion.7
  141.2 2.3 %collective-permute-start.27 = (bf16[16,16,128]{2,1,0:T(8,128)(2,1)}, bf16[16,16,128]{2,1,0:T(8,128)(2,1)S(1)}, u32[]{:S(2)}, u32[]{:S(2)}) collective-permute-start(bf16[16,16,128]{2,1,0:T(8,128)(2,1)} %gram.1.refs_1_), channel_id=1, source_target_pairs={{0,12},{1,13},{2,14},{3,15},{4,8},{5,9},{6,10},{7,11},{8,4},{9,5},... | collective-permute-start | bytes 196616 | tf_op jit(solution)/shard_map/ppermute | solution.py:190
  143.5 2.0 %collective-permute-start.28 = (bf16[16,16,128]{2,1,0:T(8,128)(2,1)}, bf16[16,16,128]{2,1,0:T(8,128)(2,1)S(1)}, u32[]{:S(2)}, u32[]{:S(2)}) collective-permute-start(bf16[16,16,128]{2,1,0:T(8,128)(2,1)} %gram.1.refs_1_), channel_id=1, source_target_pairs={{0,14},{1,15},{2,12},{3,13},{4,10},{5,11},{6,8},{7,9},{8,6},{9,7},... | collective-permute-start | bytes 196616 | tf_op jit(solution)/shard_map/ppermute | solution.py:190
  145.5 0.7 collective-permute-done.25.refs_5_
  146.2 2.9 %collective-permute-done.26.refs_6_ = bf16[16,16,128]{2,1,0:T(8,128)(2,1)S(1)} collective-permute-done((bf16[16,16,128]{2,1,0:T(8,128)(2,1)}, bf16[16,16,128]{2,1,0:T(8,128)(2,1)S(1)}, u32[]{:S(2)}, u32[]{:S(2)}) %collective-permute-start.26) | collective-permute-done | bytes 65568 | tf_op jit(solution)/shard_map/ppermute | solution.py:190
  149.1 1.7 collective-permute-done.28.refs_8_
  150.8 0.1 collective-permute-start.29
  150.9 0.1 pad_add_fusion.3.refs_0_
  151.0 1.8 %collective-permute-done.29.refs_9_ = bf16[8,16,16,128]{3,2,1,0:T(8,128)(2,1)S(1)} collective-permute-done((bf16[8,16,16,128]{3,2,1,0:T(8,128)(2,1)S(1)}, bf16[8,16,16,128]{3,2,1,0:T(8,128)(2,1)S(1)}, u32[]{:S(2)}, u32[]{:S(2)}) %collective-permute-start.29) | collective-permute-done | bytes 524320 | tf_op jit(solution)/shard_map/ppermute | solution.py:190
  152.8 0.8 copy-done.2
  153.6 1.2 precondition.1
  154.9 12.7 %all_to_all.5 = f32[16,8,256]{2,1,0:T(8,128)S(1)} all-to-all(f32[16,8,256]{2,1,0:T(8,128)S(1)} %precondition.1), channel_id=1, replica_groups=mesh['groups'=2,'dp'=16] {'dp'}, dimensions={0} | all-to-all | bytes 262144 | tf_op jit(solution)/shard_map/all_to_all | solution.py:262
  167.6 0.7 copy.19
  (61 shorter events, 0.3 us)
Async XLA Ops:
  0.0 1.2 copy-start
  1.2 7.8 %copy-start.15 = (s32[128,2]{0,1:T(2,128)S(1)}, s32[128,2]{0,1:T(2,128)}, u32[]{:S(2)}) copy-start(s32[128,2]{0,1:T(2,128)} %param.8) | copy-start | bytes 3076
  2.3 24.1 %collective-permute-start.3 = (bf16[64,3072]{1,0:T(8,128)(2,1)S(1)}, bf16[64,3072]{1,0:T(8,128)(2,1)S(1)}, u32[]{:S(2)}, u32[]{:S(2)}) collective-permute-start(bf16[64,3072]{1,0:T(8,128)(2,1)S(1)} %pad_maximum_fusion.4.refs_5_), channel_id=1, source_target_pairs={{0,4},{1,5},{2,6},{3,7},{4,8},{5,9},{6,10},{7,11},{8,12},{9,13},{1... | collective-permute-start | bytes 1179656 | tf_op jit(solution)/shard_map/ppermute | solution.py:190
  5.3 30.6 %collective-permute-start.6 = (bf16[64,3072]{1,0:T(8,128)(2,1)S(1)}, bf16[64,3072]{1,0:T(8,128)(2,1)S(1)}, u32[]{:S(2)}, u32[]{:S(2)}) collective-permute-start(bf16[64,3072]{1,0:T(8,128)(2,1)S(1)} %pad_maximum_fusion.4.refs_5_), channel_id=1, source_target_pairs={{0,2},{1,3},{2,0},{3,1},{4,6},{5,7},{6,4},{7,5},{8,10},{9,11},{10,... | collective-permute-start | bytes 1179656 | tf_op jit(solution)/shard_map/ppermute | solution.py:190
  6.9 16.6 %collective-permute-start.10 = (bf16[64,2560]{1,0:T(8,128)(2,1)S(1)}, bf16[64,2560]{1,0:T(8,128)(2,1)S(1)}, u32[]{:S(2)}, u32[]{:S(2)}) collective-permute-start(bf16[64,2560]{1,0:T(8,128)(2,1)S(1)} %constant_dynamic-slice_fusion.refs_13_), channel_id=1, source_target_pairs={{0,4},{1,5},{2,6},{3,7},{4,8},{5,9},{6,10},{7,11},{8,12},{9,13},{1... | collective-permute-start | bytes 983048 | tf_op jit(solution)/shard_map/ppermute | solution.py:190
  8.5 19.1 %collective-permute-start.13 = (bf16[64,2560]{1,0:T(8,128)(2,1)S(1)}, bf16[64,2560]{1,0:T(8,128)(2,1)}, u32[]{:S(2)}, u32[]{:S(2)}) collective-permute-start(bf16[64,2560]{1,0:T(8,128)(2,1)S(1)} %constant_dynamic-slice_fusion.refs_13_), channel_id=1, source_target_pairs={{0,2},{1,3},{2,0},{3,1},{4,6},{5,7},{6,4},{7,5},{8,10},{9,11},{10,... | collective-permute-start | bytes 983048 | tf_op jit(solution)/shard_map/ppermute | solution.py:190
  9.0 4.1 %collective-permute-start.17 = (s32[128,2]{0,1:T(2,128)S(1)}, s32[128,2]{0,1:T(2,128)S(1)}, u32[]{:S(2)}, u32[]{:S(2)}) collective-permute-start(s32[128,2]{0,1:T(2,128)S(1)} %copy-done.15), channel_id=1, source_target_pairs={{0,1},{1,0},{2,3},{3,2},{4,5},{5,4},{6,7},{7,6},{8,9},{9,8},{10,11... | collective-permute-start | bytes 3080 | tf_op jit(solution)/shard_map/ppermute | solution.py:190
  9.0 2.8 %copy-start.11 = (bf16[128,6144]{1,0:T(8,128)(2,1)S(1)}, bf16[128,6144]{1,0:T(8,128)(2,1)}, u32[]{:S(2)}) copy-start(bf16[128,6144]{1,0:T(8,128)(2,1)} %param.6) | copy-start | bytes 4718596
  13.2 11.6 %collective-permute-start.18 = (s32[256,2]{0,1:T(2,128)S(1)}, s32[256,2]{0,1:T(2,128)S(1)}, u32[]{:S(2)}, u32[]{:S(2)}) collective-permute-start(s32[256,2]{0,1:T(2,128)S(1)} %pad_add_fusion.1), channel_id=1, source_target_pairs={{0,16},{1,17},{2,18},{3,19},{4,20},{5,21},{6,22},{7,23},{8,24},{9,... | collective-permute-start | bytes 6152 | tf_op jit(solution)/shard_map/ppermute | solution.py:190
  23.5 12.4 %collective-permute-start.11 = (bf16[64,2560]{1,0:T(8,128)(2,1)S(1)}, bf16[64,2560]{1,0:T(8,128)(2,1)S(1)}, u32[]{:S(2)}, u32[]{:S(2)}) collective-permute-start(bf16[64,2560]{1,0:T(8,128)(2,1)S(1)} %collective-permute-done.10.refs_14_), channel_id=1, source_target_pairs={{0,4},{1,5},{2,6},{3,7},{4,8},{5,9},{6,10},{7,11},{8,12},{9,13},{1... | collective-permute-start | bytes 983048 | tf_op jit(solution)/shard_map/ppermute | solution.py:190
  24.8 14.0 %collective-permute-start.14 = (bf16[64,2560]{1,0:T(8,128)(2,1)S(1)}, bf16[64,2560]{1,0:T(8,128)(2,1)S(1)}, u32[]{:S(2)}, u32[]{:S(2)}) collective-permute-start(bf16[64,2560]{1,0:T(8,128)(2,1)S(1)} %collective-permute-done.10.refs_14_), channel_id=1, source_target_pairs={{0,2},{1,3},{2,0},{3,1},{4,6},{5,7},{6,4},{7,5},{8,10},{9,11},{10,... | collective-permute-start | bytes 983048 | tf_op jit(solution)/shard_map/ppermute | solution.py:190
  26.3 18.1 %collective-permute-start.4 = (bf16[64,3072]{1,0:T(8,128)(2,1)S(1)}, bf16[64,3072]{1,0:T(8,128)(2,1)S(1)}, u32[]{:S(2)}, u32[]{:S(2)}) collective-permute-start(bf16[64,3072]{1,0:T(8,128)(2,1)S(1)} %collective-permute-done.3.refs_6_), channel_id=1, source_target_pairs={{0,4},{1,5},{2,6},{3,7},{4,8},{5,9},{6,10},{7,11},{8,12},{9,13},{1... | collective-permute-start | bytes 1179656 | tf_op jit(solution)/shard_map/ppermute | solution.py:190
  27.6 18.3 %collective-permute-start.7 = (bf16[64,3072]{1,0:T(8,128)(2,1)S(1)}, bf16[64,3072]{1,0:T(8,128)(2,1)S(1)}, u32[]{:S(2)}, u32[]{:S(2)}) collective-permute-start(bf16[64,3072]{1,0:T(8,128)(2,1)S(1)} %collective-permute-done.3.refs_6_), channel_id=1, source_target_pairs={{0,2},{1,3},{2,0},{3,1},{4,6},{5,7},{6,4},{7,5},{8,10},{9,11},{10,... | collective-permute-start | bytes 1179656 | tf_op jit(solution)/shard_map/ppermute | solution.py:190
  35.9 2.8 %copy-start.5 = (bf16[64,2560]{1,0:T(8,128)(2,1)}, bf16[64,2560]{1,0:T(8,128)(2,1)S(1)}, u32[]{:S(2)}) copy-start(bf16[64,2560]{1,0:T(8,128)(2,1)S(1)} %collective-permute-done.11.refs_15_) | copy-start | bytes 983044
  35.9 13.8 %collective-permute-start.12 = (bf16[64,2560]{1,0:T(8,128)(2,1)S(1)}, bf16[64,2560]{1,0:T(8,128)(2,1)}, u32[]{:S(2)}, u32[]{:S(2)}) collective-permute-start(bf16[64,2560]{1,0:T(8,128)(2,1)S(1)} %collective-permute-done.11.refs_15_), channel_id=1, source_target_pairs={{0,4},{1,5},{2,6},{3,7},{4,8},{5,9},{6,10},{7,11},{8,12},{9,13},{1... | collective-permute-start | bytes 983048 | tf_op jit(solution)/shard_map/ppermute | solution.py:190
  36.0 13.8 %collective-permute-start.15 = (bf16[64,2560]{1,0:T(8,128)(2,1)S(1)}, bf16[64,2560]{1,0:T(8,128)(2,1)S(1)}, u32[]{:S(2)}, u32[]{:S(2)}) collective-permute-start(bf16[64,2560]{1,0:T(8,128)(2,1)S(1)} %collective-permute-done.11.refs_15_), channel_id=1, source_target_pairs={{0,2},{1,3},{2,0},{3,1},{4,6},{5,7},{6,4},{7,5},{8,10},{9,11},{10,... | collective-permute-start | bytes 983048 | tf_op jit(solution)/shard_map/ppermute | solution.py:190
  38.8 0.7 copy-start.7
  39.5 32.5 %collective-permute-start = (bf16[128,5632]{1,0:T(8,128)(2,1)}, bf16[128,5632]{1,0:T(8,128)(2,1)}, u32[]{:S(2)}, u32[]{:S(2)}) collective-permute-start(bf16[128,5632]{1,0:T(8,128)(2,1)} %pad_maximum_fusion.1), channel_id=1, source_target_pairs={{0,1},{1,0},{2,3},{3,2},{4,5},{5,4},{6,7},{7,6},{8,9},{9,8},{10,11... | collective-permute-start | bytes 4325384 | tf_op jit(solution)/shard_map/ppermute | solution.py:190
  44.4 34.8 %collective-permute-start.1 = (bf16[128,5632]{1,0:T(8,128)(2,1)}, bf16[128,5632]{1,0:T(8,128)(2,1)}, u32[]{:S(2)}, u32[]{:S(2)}) collective-permute-start(bf16[128,5632]{1,0:T(8,128)(2,1)} %pad_maximum_fusion.2), channel_id=1, source_target_pairs={{0,16},{1,17},{2,18},{3,19},{4,20},{5,21},{6,22},{7,23},{8,24},{9,... | collective-permute-start | bytes 4325384 | tf_op jit(solution)/shard_map/ppermute | solution.py:190
  45.9 0.7 copy-start.3
  46.6 57.6 %collective-permute-start.2 = (bf16[128,5632]{1,0:T(8,128)(2,1)}, bf16[128,5632]{1,0:T(8,128)(2,1)}, u32[]{:S(2)}, u32[]{:S(2)}) collective-permute-start(bf16[128,5632]{1,0:T(8,128)(2,1)} %pad_maximum_fusion.3), channel_id=1, source_target_pairs={{0,17},{1,16},{2,19},{3,18},{4,21},{5,20},{6,23},{7,22},{8,25},{9,... | collective-permute-start | bytes 4325384 | tf_op jit(solution)/shard_map/ppermute | solution.py:190
  49.7 11.3 %collective-permute-start.5 = (bf16[64,3072]{1,0:T(8,128)(2,1)S(1)}, bf16[64,3072]{1,0:T(8,128)(2,1)}, u32[]{:S(2)}, u32[]{:S(2)}) collective-permute-start(bf16[64,3072]{1,0:T(8,128)(2,1)S(1)} %collective-permute-done.4.refs_7_), channel_id=1, source_target_pairs={{0,4},{1,5},{2,6},{3,7},{4,8},{5,9},{6,10},{7,11},{8,12},{9,13},{1... | collective-permute-start | bytes 1179656 | tf_op jit(solution)/shard_map/ppermute | solution.py:190
  49.8 0.7 copy-start.9
  50.5 11.6 %collective-permute-start.8 = (bf16[64,3072]{1,0:T(8,128)(2,1)S(1)}, bf16[64,3072]{1,0:T(8,128)(2,1)}, u32[]{:S(2)}, u32[]{:S(2)}) collective-permute-start(bf16[64,3072]{1,0:T(8,128)(2,1)S(1)} %collective-permute-done.4.refs_7_), channel_id=1, source_target_pairs={{0,2},{1,3},{2,0},{3,1},{4,6},{5,7},{6,4},{7,5},{8,10},{9,11},{10,... | collective-permute-start | bytes 1179656 | tf_op jit(solution)/shard_map/ppermute | solution.py:190
  61.0 11.0 %collective-permute-start.16 = (bf16[64,2560]{1,0:T(8,128)(2,1)}, bf16[64,2560]{1,0:T(8,128)(2,1)}, u32[]{:S(2)}, u32[]{:S(2)}) collective-permute-start(bf16[64,2560]{1,0:T(8,128)(2,1)} %collective-permute-done.12.refs_16_), channel_id=1, source_target_pairs={{0,2},{1,3},{2,0},{3,1},{4,6},{5,7},{6,4},{7,5},{8,10},{9,11},{10,... | collective-permute-start | bytes 983048 | tf_op jit(solution)/shard_map/ppermute | solution.py:190
  62.1 42.1 %collective-permute-start.9 = (bf16[64,3072]{1,0:T(8,128)(2,1)}, bf16[64,3072]{1,0:T(8,128)(2,1)}, u32[]{:S(2)}, u32[]{:S(2)}) collective-permute-start(bf16[64,3072]{1,0:T(8,128)(2,1)} %collective-permute-done.5.refs_8_), channel_id=1, source_target_pairs={{0,2},{1,3},{2,0},{3,1},{4,6},{5,7},{6,4},{7,5},{8,10},{9,11},{10,... | collective-permute-start | bytes 1179656 | tf_op jit(solution)/shard_map/ppermute | solution.py:190
  104.2 1.0 copy-start.4
  105.2 1.0 copy-start.6
  106.2 1.0 copy-start.8
  107.1 1.0 copy-start.10
  119.8 33.0 %copy-start.1 = (bf16[4096,256]{1,0:T(8,128)(2,1)S(1)}, bf16[4096,256]{1,0:T(8,128)(2,1)}, u32[]{:S(2)}) copy-start(bf16[4096,256]{1,0:T(8,128)(2,1)} %refs_10_.1) | copy-start | bytes 6291460
  121.7 2.7 %collective-permute-start.19 = (f32[128,256]{1,0:T(8,128)S(1)}, f32[128,256]{1,0:T(8,128)S(1)}, u32[]{:S(2)}, u32[]{:S(2)}) collective-permute-start(f32[128,256]{1,0:T(8,128)S(1)} %get-tuple-element.17), channel_id=1, source_target_pairs={{0,1},{1,0},{2,3},{3,2},{4,5},{5,4},{6,7},{7,6},{8,9},{9,8},{10,11... | collective-permute-start | bytes 393224 | tf_op jit(solution)/shard_map/ppermute | solution.py:190
  123.1 6.4 %collective-permute-start.20 = (f32[128,256]{1,0:T(8,128)S(1)}, f32[128,256]{1,0:T(8,128)S(1)}, u32[]{:S(2)}, u32[]{:S(2)}) collective-permute-start(f32[128,256]{1,0:T(8,128)S(1)} %get-tuple-element.16), channel_id=1, source_target_pairs={{0,16},{1,17},{2,18},{3,19},{4,20},{5,21},{6,22},{7,23},{8,24},{9,... | collective-permute-start | bytes 393224 | tf_op jit(solution)/shard_map/ppermute | solution.py:190
  124.0 6.3 %collective-permute-start.21 = (f32[128,256]{1,0:T(8,128)S(1)}, f32[128,256]{1,0:T(8,128)S(1)}, u32[]{:S(2)}, u32[]{:S(2)}) collective-permute-start(f32[128,256]{1,0:T(8,128)S(1)} %get-tuple-element.15), channel_id=1, source_target_pairs={{0,17},{1,16},{2,19},{3,18},{4,21},{5,20},{6,23},{7,22},{8,25},{9,... | collective-permute-start | bytes 393224 | tf_op jit(solution)/shard_map/ppermute | solution.py:190
  124.4 5.9 %copy-start.12 = (f32[128,256]{1,0:T(8,128)}, f32[128,256]{1,0:T(8,128)S(1)}, u32[]{:S(2)}) copy-start(f32[128,256]{1,0:T(8,128)S(1)} %collective-permute-done.19.p1) | copy-start | bytes 393220
  129.4 0.9 copy-start.13
  130.3 0.7 copy-start.14
  133.4 7.8 %collective-permute-start.22 = (bf16[16,16,128]{2,1,0:T(8,128)(2,1)}, bf16[16,16,128]{2,1,0:T(8,128)(2,1)S(1)}, u32[]{:S(2)}, u32[]{:S(2)}) collective-permute-start(bf16[16,16,128]{2,1,0:T(8,128)(2,1)} %gram.1.refs_1_), channel_id=1, source_target_pairs={{0,2},{1,3},{2,0},{3,1},{4,6},{5,7},{6,4},{7,5},{8,10},{9,11},{10,... | collective-permute-start | bytes 196616 | tf_op jit(solution)/shard_map/ppermute | solution.py:190
  134.4 9.0 %collective-permute-start.23 = (bf16[16,16,128]{2,1,0:T(8,128)(2,1)}, bf16[16,16,128]{2,1,0:T(8,128)(2,1)S(1)}, u32[]{:S(2)}, u32[]{:S(2)}) collective-permute-start(bf16[16,16,128]{2,1,0:T(8,128)(2,1)} %gram.1.refs_1_), channel_id=1, source_target_pairs={{0,4},{1,5},{2,6},{3,7},{4,0},{5,1},{6,2},{7,3},{8,12},{9,13},{10,... | collective-permute-start | bytes 196616 | tf_op jit(solution)/shard_map/ppermute | solution.py:190
  134.4 11.1 %collective-permute-start.24 = (bf16[16,16,128]{2,1,0:T(8,128)(2,1)}, bf16[16,16,128]{2,1,0:T(8,128)(2,1)S(1)}, u32[]{:S(2)}, u32[]{:S(2)}) collective-permute-start(bf16[16,16,128]{2,1,0:T(8,128)(2,1)} %gram.1.refs_1_), channel_id=1, source_target_pairs={{0,6},{1,7},{2,4},{3,5},{4,2},{5,3},{6,0},{7,1},{8,14},{9,15},{10,... | collective-permute-start | bytes 196616 | tf_op jit(solution)/shard_map/ppermute | solution.py:190
  136.9 9.3 %collective-permute-start.25 = (bf16[16,16,128]{2,1,0:T(8,128)(2,1)}, bf16[16,16,128]{2,1,0:T(8,128)(2,1)S(1)}, u32[]{:S(2)}, u32[]{:S(2)}) collective-permute-start(bf16[16,16,128]{2,1,0:T(8,128)(2,1)} %gram.1.refs_1_), channel_id=1, source_target_pairs={{0,8},{1,9},{2,10},{3,11},{4,12},{5,13},{6,14},{7,15},{8,0},{9,1},... | collective-permute-start | bytes 196616 | tf_op jit(solution)/shard_map/ppermute | solution.py:190
  138.2 10.9 %collective-permute-start.26 = (bf16[16,16,128]{2,1,0:T(8,128)(2,1)}, bf16[16,16,128]{2,1,0:T(8,128)(2,1)S(1)}, u32[]{:S(2)}, u32[]{:S(2)}) collective-permute-start(bf16[16,16,128]{2,1,0:T(8,128)(2,1)} %gram.1.refs_1_), channel_id=1, source_target_pairs={{0,10},{1,11},{2,8},{3,9},{4,14},{5,15},{6,12},{7,13},{8,2},{9,3},... | collective-permute-start | bytes 196616 | tf_op jit(solution)/shard_map/ppermute | solution.py:190
  141.2 7.9 %collective-permute-start.27 = (bf16[16,16,128]{2,1,0:T(8,128)(2,1)}, bf16[16,16,128]{2,1,0:T(8,128)(2,1)S(1)}, u32[]{:S(2)}, u32[]{:S(2)}) collective-permute-start(bf16[16,16,128]{2,1,0:T(8,128)(2,1)} %gram.1.refs_1_), channel_id=1, source_target_pairs={{0,12},{1,13},{2,14},{3,15},{4,8},{5,9},{6,10},{7,11},{8,4},{9,5},... | collective-permute-start | bytes 196616 | tf_op jit(solution)/shard_map/ppermute | solution.py:190
  143.5 7.3 %collective-permute-start.28 = (bf16[16,16,128]{2,1,0:T(8,128)(2,1)}, bf16[16,16,128]{2,1,0:T(8,128)(2,1)S(1)}, u32[]{:S(2)}, u32[]{:S(2)}) collective-permute-start(bf16[16,16,128]{2,1,0:T(8,128)(2,1)} %gram.1.refs_1_), channel_id=1, source_target_pairs={{0,14},{1,15},{2,12},{3,13},{4,10},{5,11},{6,8},{7,9},{8,6},{9,7},... | collective-permute-start | bytes 196616 | tf_op jit(solution)/shard_map/ppermute | solution.py:190
  150.8 2.0 %collective-permute-start.29 = (bf16[8,16,16,128]{3,2,1,0:T(8,128)(2,1)S(1)}, bf16[8,16,16,128]{3,2,1,0:T(8,128)(2,1)S(1)}, u32[]{:S(2)}, u32[]{:S(2)}) collective-permute-start(bf16[8,16,16,128]{3,2,1,0:T(8,128)(2,1)S(1)} %bitcast_dynamic-update-slice_fusion), channel_id=1, source_target_pairs={{0,1},{1,0},{2,3},{3,2},{4,5},{5,4},{6,7},{7,6},{8,9},{9,8},{10,11... | collective-permute-start | bytes 1572872 | tf_op jit(solution)/shard_map/ppermute | solution.py:190
  152.8 0.8 copy-start.2

commit v2 on v1

v2 whole, which is shorter than its diff:
```python
import functools

import jax
import jax.numpy as jnp
from jax import lax
from jax.experimental import pallas as pl
from jax.experimental.pallas import tpu as pltpu
from jax.sharding import PartitionSpec as P

EXPERTS = 8
PROJ = 64
TOK = 128
LANES = 128
VMEM = 28 * 1024 * 1024
AXES = ("groups", "dp")


def nt(rows, table):
    return lax.dot_general(rows, table, (((1,), (1,)), ((), ())), preferred_element_type=jnp.float32)


def pick(total, routes, eid_ref, first, pieces, sub):
    low = lax.broadcasted_iota(jnp.int32, (TOK, LANES), 1) < PROJ
    out = []
    for k in range(2):
        picked = jnp.zeros((TOK, LANES), jnp.float32)
        for a in range(sub):
            for pair in range(pieces // 2):
                even, odd = first + 2 * pair, first + 2 * pair + 1
                wanted = jnp.where(
                    low,
                    jnp.where(eid_ref[1, even] == a, eid_ref[0, even], -1),
                    jnp.where(eid_ref[1, odd] == a, eid_ref[0, odd], -1),
                ).astype(jnp.float32)
                picked += jnp.where(routes[:, k : k + 1] == wanted, total(a, pair), 0.0)
        out.append(picked + pltpu.roll(picked, PROJ, 1))
    return out


def right_sums(sub, width, toks, pieces):
    table = jnp.concatenate([p[:, :width] for p in pieces], axis=0)
    return [nt(toks[:, a * width : (a + 1) * width], table) for a in range(sub)]


def left_sums(sub, width, toks, pieces):
    table = jnp.concatenate([p[:, width:] for p in pieces], axis=0)
    at, size = sub * width, table.shape[1]
    return [nt(toks[:, at + a * size : at + (a + 1) * size], table) for a in range(sub)]


def picks(rows, tables, width, first, eid_ref, sub):
    toks = jnp.concatenate(rows, axis=0)
    right, left = right_sums(sub, width, toks, tables), left_sums(sub, width, toks, tables)
    low = lax.broadcasted_iota(jnp.int32, (TOK, LANES), 1) < PROJ
    picked = []
    for b in range(len(rows)):
        here = slice(b * TOK, (b + 1) * TOK)
        named = toks[here, -LANES:].astype(jnp.float32)

        def pick_of(sums):
            return pick(
                lambda a, pair: sums[a][here, pair * LANES : (pair + 1) * LANES], named, eid_ref, first, len(tables), sub
            )

        picked.append([jnp.where(low, x, y) for x, y in zip(pick_of(left), pick_of(right))])
    return picked


def early_kernel(sub, width, eid_ref, own, other, x, *refs):
    rows = [own[...], other[...], x[...]]
    for b, slots in enumerate(picks(rows, refs[:-1], width, 0, eid_ref, sub)):
        for k, got in enumerate(slots):
            refs[-1][b, :, k * LANES : (k + 1) * LANES] = got


def last_kernel(sub, width, n_pieces, eid_ref, own, other, x, xc, *refs):
    pieces, early_ref, outs = refs[:n_pieces], refs[n_pieces], refs[n_pieces + 1 :]
    rows = [own[...], other[...], x[...]]
    for b, slots in enumerate(picks(rows, pieces[-2:], width, n_pieces - 2, eid_ref, sub)):
        for k, got in enumerate(slots):
            lanes = slice(k * LANES, (k + 1) * LANES)
            outs[b][:, lanes] = early_ref[b, :, lanes] + got
    for k, got in enumerate(picks([xc[...]], pieces, width, 0, eid_ref, sub)[0]):
        outs[3][:, k * LANES : (k + 1) * LANES] = got


def pack_kernel(outputs, place_ref, *refs):
    n_outs = sum(len(cuts) for _, cuts in outputs)
    n_blocks = sum(len(blocks) for blocks, _ in outputs)
    ins, outs = refs[:n_blocks], refs[n_blocks : n_blocks + n_outs]
    buffers, in_sems, out_sems = refs[n_blocks + n_outs : -2], refs[-2], refs[-1]
    copies, i = [], 0
    for (blocks, _), buffer in zip(outputs, buffers):
        at, group = 0, []
        for _, width, place, scale, offset in blocks:
            start = pl.multiple_of((place_ref[place] * scale + offset) * width, LANES)
            group.append(
                pltpu.make_async_copy(ins[i].at[:, pl.ds(start, width)], buffer.at[:, at : at + width], in_sems.at[i])
            )
            at, i = at + width, i + 1
        copies.append(group)
    for group in copies:
        for copy in group:
            copy.start()
    back, i = [], 0
    for (_, cuts), buffer, group in zip(outputs, buffers, copies):
        for copy in group:
            copy.wait()
        at = 0
        for width in cuts:
            copy = pltpu.make_async_copy(buffer.at[:, at : at + width], outs[i], out_sems.at[i])
            copy.start()
            back.append(copy)
            at, i = at + width, i + 1
    for copy in back:
        copy.wait()


def pack(places, outputs, name):
    blocks = [b for out, _ in outputs for b in out]
    shapes = [(out[0][0].shape[0], width) for out, cuts in outputs for width in cuts]
    hbm = pl.BlockSpec(memory_space=pl.ANY)
    plain = [([(None,) + b[1:] for b in out], cuts) for out, cuts in outputs]
    return pl.pallas_call(
        functools.partial(pack_kernel, plain),
        in_specs=[pl.BlockSpec(memory_space=pltpu.SMEM)] + [hbm] * len(blocks),
        out_specs=[hbm] * len(shapes),
        out_shape=[jax.ShapeDtypeStruct(x, jnp.bfloat16) for x in shapes],
        scratch_shapes=[pltpu.VMEM((out[0][0].shape[0], sum(cuts)), jnp.bfloat16) for out, cuts in outputs]
        + [pltpu.SemaphoreType.DMA((len(blocks),)), pltpu.SemaphoreType.DMA((len(shapes),))],
        compiler_params=pltpu.CompilerParams(vmem_limit_bytes=2 * VMEM),
        name=name,
    )(places, *[b[0] for b in blocks])


def local(kernel, name, out_shape, operands, smem=0):
    vmem = pl.BlockSpec(memory_space=pltpu.VMEM)
    return pl.pallas_call(
        kernel,
        in_specs=[pl.BlockSpec(memory_space=pltpu.SMEM)] * smem + [vmem] * (len(operands) - smem),
        out_specs=jax.tree.map(lambda _: vmem, out_shape),
        out_shape=out_shape,
        compiler_params=pltpu.CompilerParams(vmem_limit_bytes=VMEM),
        name=name,
    )(*operands)


def gram_kernel(p0, p1, p2, p3, routes_ref, out_ref, flat):
    total = (p0[...] + p1[...]) + (p2[...] + p3[...])
    first, second = total[:, :LANES], total[:, LANES:]
    left = jnp.concatenate([jnp.transpose(first)[:PROJ], jnp.transpose(second)[:PROJ]], axis=1)
    right = jnp.concatenate([first, second], axis=0)
    named = routes_ref[...]
    rows = jnp.concatenate([jnp.where(named == e, left, 0.0) for e in range(EXPERTS)], axis=0)
    grams = lax.dot_general(
        rows,
        right,
        (((1,), (0,)), ((), ())),
        precision=lax.Precision.HIGHEST,
        preferred_element_type=jnp.float32,
    )
    grams = grams * (TOK**-0.5)
    low = lax.broadcasted_iota(jnp.int32, (PROJ // 2, LANES), 1) < PROJ
    for e in range(EXPERTS):
        top = grams[e * PROJ : e * PROJ + PROJ // 2]
        bottom = grams[e * PROJ + PROJ // 2 : (e + 1) * PROJ]
        flat[:, e, :] = jnp.where(low, pltpu.roll(top, PROJ, 1), bottom)
    out_ref[...] = flat[...].reshape(PROJ // 4, 2 * EXPERTS, LANES).astype(jnp.bfloat16)


def gram(parts, routes):
    return pl.pallas_call(
        gram_kernel,
        out_shape=jax.ShapeDtypeStruct((PROJ // 4, 2 * EXPERTS, LANES), jnp.bfloat16),
        scratch_shapes=[pltpu.VMEM((PROJ // 2, EXPERTS, LANES), jnp.float32)],
        name="gram",
    )(*parts, routes)


def fisher_kernel(n, order_ref, *refs):
    own, other = refs[: n // 2], refs[n // 2]
    fisher, out_ref = refs[n // 2 + 1 :]
    total = jnp.zeros((n * EXPERTS, fisher.shape[1]), jnp.float32)
    for i in range(PROJ // 4):
        tiles = [x[i] for x in own] + [other[j, i] for j in range(n // 2)]
        rows = jnp.concatenate([x.astype(jnp.float32).reshape(1, 2, EXPERTS, LANES) for x in tiles], axis=0)
        for h in range(2):
            p = 2 * i + h
            table = jnp.concatenate(
                [
                    fisher[p * PROJ : (p + 1) * PROJ, :],
                    fisher[(PROJ // 2 + p) * PROJ : (PROJ // 2 + p + 1) * PROJ, :],
                ],
                axis=0,
            )
            lhs = rows[:, h].reshape(n * EXPERTS, LANES).astype(jnp.bfloat16)
            total += jnp.dot(lhs, table, preferred_element_type=jnp.float32)
    for j in range(n):
        out_ref[order_ref[j]] = total[j * EXPERTS : (j + 1) * EXPERTS]


def precondition(own, other, fisher, order):
    n = 2 * len(own)
    vmem = pl.BlockSpec(memory_space=pltpu.VMEM)
    return pl.pallas_call(
        lambda *refs: fisher_kernel(n, *refs),
        in_specs=[pl.BlockSpec(memory_space=pltpu.SMEM)] + [vmem] * (n // 2 + 2),
        out_specs=vmem,
        out_shape=jax.ShapeDtypeStruct((n, EXPERTS, fisher.shape[1]), jnp.float32),
        compiler_params=pltpu.CompilerParams(vmem_limit_bytes=VMEM),
        name="precondition",
    )(order, *own, other, fisher)


def shards(features, grads, routes, proj_in, proj_out, fisher_inverse):
    groups, n = lax.axis_size("groups"), lax.axis_size("dp")
    chips = n // 2
    slices = n // EXPERTS
    sub = slices // 2
    y_size = 2 if groups == 2 else 1
    z_size = chips // y_size
    group, place = lax.axis_index("groups"), lax.axis_index("dp")
    core, chip, half = place % 2, place // 2, group % 2
    z, y = chip // y_size, chip % y_size

    def move(x, to):
        pairs = []
        for g in range(groups):
            for d in range(n):
                tg, td = to(g, d)
                pairs.append((g * n + d, tg * n + td))
        return lax.ppermute(x, AXES, pairs)

    def to_core(g, d):
        return g, d ^ 1

    def to_x(g, d):
        return g ^ 1, d

    def to_x_core(g, d):
        return g ^ 1, d ^ 1

    def to_y(g, d):
        return g, d ^ 2

    def to_z(g, d):
        return g, (d + 2 * y_size) % n

    def from_z(g, d):
        return g, (d - 2 * y_size) % n

    quarter_in, quarter_out = proj_in.shape[1] // 2, proj_out.shape[1] // 2

    def after(x, *others):
        return lax.optimization_barrier((x, *others))[0]

    def part(c, h):
        return c * 2 + h

    places = jnp.stack([part(core, 1 - half), part(1 - core, 1 - half), part(core, half), part(1 - core, half), half])
    places = places.astype(jnp.int32)
    named = jnp.pad(routes.astype(jnp.bfloat16), ((0, 0), (0, LANES - 2)))
    width = sub * (quarter_in + quarter_out) + LANES

    def whole(place):
        return (
            [(grads, quarter_out, place, 1, 4 * a) for a in range(sub)]
            + [(features, quarter_in, place, 1, 4 * a) for a in range(sub)]
            + [(named, LANES, 0, 0, 0)]
        )

    tables = [(proj_out, quarter_out, 4, 1, 0), (proj_in, quarter_in, 4, 1, 0)]
    table, send_other, send_x = pack(
        places, [(tables, [quarter_out + quarter_in]), (whole(3), [width]), (whole(0), [width])], "pack_first"
    )
    send_xc, own = pack(after(places, send_x), [(whole(1), [width]), (whole(2), [width])], "pack_second")
    other = move(send_other, to_core)
    x, xc = move(send_x, to_x), move(send_xc, to_x_core)

    blocks, ids = [table], [0]
    ups, downs = z_size // 2, (z_size - 1) // 2
    up = down = table
    facing = move(table, to_y) if y_size == 2 else table
    for k in range(1, ups + 1):
        up = move(after(up, facing, other) if k == 2 else up, to_z)
        blocks.append(up)
        ids.append(-k)
        if k <= downs:
            down = move(down, from_z)
            blocks.append(down)
            ids.append(k)
    pieces, chip_ids = [], []
    for i, block in enumerate(blocks):
        for across in range(y_size):
            if across:
                if i == 1:
                    block = after(block, facing)
                if i == len(blocks) - 1:
                    block = after(block, x, pieces[3])
                block = move(block, to_y) if i else facing
            pieces.append(block)
            chip_ids.append(((z + ids[i]) % z_size) * y_size + (1 - y if across else y))

    chip_ids = jnp.stack(chip_ids).astype(jnp.int32)
    eid = jnp.stack([2 * chip_ids // slices, 2 * chip_ids % slices // 2])

    f32 = jnp.float32
    early = local(
        functools.partial(early_kernel, sub, quarter_out),
        "project_early",
        jax.ShapeDtypeStruct((3, TOK, 2 * LANES), f32),
        [eid, own, other, x] + pieces[:-2],
        smem=1,
    )
    partial = local(
        functools.partial(last_kernel, sub, quarter_out, chips),
        "project_last",
        [jax.ShapeDtypeStruct((TOK, 2 * LANES), f32)] * 4,
        [eid, own, other, x, xc] + pieces + [early],
        smem=1,
    )
    sums = [partial[0], move(partial[1], to_core), move(partial[2], to_x), move(partial[3], to_x_core)]
    mine = gram(sums, routes.T.reshape(1, -1))

    own = [mine]
    for k in range(1, chips):
        own.append(move(mine, lambda g, d, k=k: (g, d ^ (2 * k))))
    other = move(jnp.stack(own), to_core)
    steps = jnp.arange(chips, dtype=jnp.int32)
    order = jnp.concatenate([(chip ^ steps) * 2 + core, (chip ^ steps) * 2 + (1 - core)])
    columns = precondition(own, other, fisher_inverse, order.astype(jnp.int32))
    result = lax.all_to_all(columns, "dp", split_axis=0, concat_axis=0, tiled=True)
    return jnp.transpose(result, (1, 0, 2)).reshape(1, EXPERTS, PROJ * PROJ)


def solution(mesh):
    in_specs = (
        P(AXES, None),
        P(AXES, None),
        P(AXES, None),
        P(None, "dp"),
        P(None, "dp"),
        P(None, "dp"),
    )
    out_specs = P(AXES, None, None)
    return jax.shard_map(shards, mesh=mesh, in_specs=in_specs, out_specs=out_specs, check_vma=False)
```

time: 169 us -> 136 us (0.80)
  waiting for transfers between devices: 86.4 us -> 58.2 us
  Pallas kernels: 15.4 us -> 20.6 us
  other arithmetic: 5.13 us -> 0.8 us
  starting transfers between devices: 31.9 us -> 28.4 us
    ppermute x30 -> x21, waiting for transfers between devices: 86.4 us -> 58.2 us  [move(): return lax.ppermute(x, AXES, pairs)]
    pallas_call x1 -> x4, Pallas kernels: 11.7 us -> 16.9 us  [the longest x2 9.11 us: local(): pl.pallas_call(kernel, in_specs=[pl.BlockSpec(memory_space=pltpu.SMEM)] *...]
    concatenate x7 -> x0, other arithmetic: 5.01 us -> none  [the longest x4 4.97 us: token_columns(): return jnp.concatenate(parts, axis=1)]
    dynamic_slice x4 -> x0, local copies, waits for them, and re-layouts: 3.88 us -> none  [the longest x1 2.78 us: token_columns(): lax.dynamic_slice_in_dim(grads, at * quarter_out, quarter_out, 1)]
    ppermute x30 -> x21, starting transfers between devices: 31.9 us -> 28.4 us  [move(): return lax.ppermute(x, AXES, pairs)]
    unnamed x40 -> x38, local copies, waits for them, and re-layouts: 10.5 us -> 13.8 us
    squeeze x1 -> x0, local copies, waits for them, and re-layouts: 1.93 us -> none  [shards(): partial[3]]
  transfers between devices with their start and end apart: 30 -> 21, of which waited for: 14 -> 9; matrix products, arithmetic and copies ran while one was open for 5% -> 1% of each run, Pallas kernels for 0% -> 6%
where the time goes in v2:
time: 136 us; the launch traced here: 135 us
  waiting for transfers between devices  58.2 us (43%)
  starting transfers between devices  28.4 us (21%)
  Pallas kernels  20.6 us (15%)
  local copies, waits for them, and re-layouts  15.2 us (11%)
  blocking collectives  11.8 us (9%)
    ppermute x21, waiting for transfers between devices, move(): return lax.ppermute(x, AXES, pairs)  58.2 us
    ppermute x21, starting transfers between devices, move(): return lax.ppermute(x, AXES, pairs)  28.4 us
    unnamed x38, local copies, waits for them, and re-layouts  13.8 us
    all_to_all x1, blocking collectives, shards(): lax.all_to_all(columns, 'dp', split_axis=0, concat_axis=0, tiled=True)  11.8 us
    pallas_call x2, Pallas kernels, local(): pl.pallas_call(kernel, in_specs=[pl.BlockSpec(memory_space=pltpu.SMEM)] *...  9.11 us
    pallas_call x2, Pallas kernels, pack(): pl.pallas_call(functools.partial(pack_kernel, plain), in_specs=[pl.BlockS...  7.83 us
  transfers between devices with their start and end apart: 21, of which 9 were waited for; matrix products, arithmetic and copies ran while one was open for 1% of the time, Pallas kernels for 6%

profile of v2, /device:TPU:0, one launch (start us, length us, event | category | flops | bytes accessed | tf_op | source)
XLA Modules:
  0.0 135.2 jit_solution(4835633149672289765)
XLA Ops:
  0.0 0.7 convert_element_type.5
  0.7 0.1 copy.8
  0.8 0.6 pad.4.refs_4_.refs_7_.refs_2_.refs_5_
  1.4 0.6 stack.92.place_ref
  2.0 3.9 %pack_first.1 = (bf16[64,5632]{1,0:T(8,128)(2,1)}, bf16[128,5760]{1,0:T(8,128)(2,1)}, bf16[128,5760]{1,0:T(8,128)(2,1)}) custom-call(s32[5]{0:T(128)} %stack.92.place_ref, bf16[64,8192]{1,0:T(8,128)(2,1)} %refs_0_.2, bf16[64,3072]{1,0:T(8,128)(2,1)} %refs_1_.2, bf16[128,16384]{1,0:T(8,128)(2,1)} %refs_3_.3, bf16[128,6144]{1,0:T(8,128)(2,1)} %refs_4_.1, ...), custom_call_target="tpu_custom_call" | custom-call | tf_op jit(solution)/shard_map/pack_first/pallas_call | solution.py:124
  5.9 1.0 collective-permute-start
  7.0 2.6 %collective-permute-start.1 = (bf16[128,5760]{1,0:T(8,128)(2,1)}, bf16[128,5760]{1,0:T(8,128)(2,1)S(1)}, u32[]{:S(2)}, u32[]{:S(2)}) collective-permute-start(bf16[128,5760]{1,0:T(8,128)(2,1)} %get-tuple-element.18), channel_id=1, source_target_pairs={{0,16},{1,17},{2,18},{3,19},{4,20},{5,21},{6,22},{7,23},{8,24},{9,... | collective-permute-start | bytes 4423688 | tf_op jit(solution)/shard_map/ppermute | solution.py:232
  9.5 1.5 %collective-permute-start.3 = (bf16[64,5632]{1,0:T(8,128)(2,1)}, bf16[64,5632]{1,0:T(8,128)(2,1)S(1)}, u32[]{:S(2)}, u32[]{:S(2)}) collective-permute-start(bf16[64,5632]{1,0:T(8,128)(2,1)} %get-tuple-element.23.refs_0_), channel_id=1, source_target_pairs={{0,2},{1,3},{2,0},{3,1},{4,6},{5,7},{6,4},{7,5},{8,10},{9,11},{10,... | collective-permute-start | bytes 2162696 | tf_op jit(solution)/shard_map/ppermute | solution.py:232
  11.1 1.6 %collective-permute-start.4 = (bf16[64,5632]{1,0:T(8,128)(2,1)}, bf16[64,5632]{1,0:T(8,128)(2,1)S(1)}, u32[]{:S(2)}, u32[]{:S(2)}) collective-permute-start(bf16[64,5632]{1,0:T(8,128)(2,1)} %get-tuple-element.23.refs_0_), channel_id=1, source_target_pairs={{0,4},{1,5},{2,6},{3,7},{4,8},{5,9},{6,10},{7,11},{8,12},{9,13},{1... | collective-permute-start | bytes 2162696 | tf_op jit(solution)/shard_map/ppermute | solution.py:232
  12.6 3.9 %pack_second.1 = (bf16[128,5760]{1,0:T(8,128)(2,1)}, bf16[128,5760]{1,0:T(8,128)(2,1)}) custom-call(s32[5]{0:T(128)} %stack.92.place_ref, bf16[128,16384]{1,0:T(8,128)(2,1)} %refs_3_.3, bf16[128,6144]{1,0:T(8,128)(2,1)} %refs_4_.1, bf16[128,128]{1,0:T(8,128)(2,1)} %pad.4.refs_4_.refs_7_.refs_2_.refs_5_, bf16[128,16384]{1,0:T(8,128)(2,1)} %refs_3_.3, ...), custom_call_target="tpu_custom_call" | custom-call | tf_op jit(solution)/shard_map/pack_second/pallas_call | solution.py:124
  16.6 0.1 collective-permute-start.2
  16.7 11.3 %collective-permute-done.3.refs_1_ = bf16[64,5632]{1,0:T(8,128)(2,1)S(1)} collective-permute-done((bf16[64,5632]{1,0:T(8,128)(2,1)}, bf16[64,5632]{1,0:T(8,128)(2,1)S(1)}, u32[]{:S(2)}, u32[]{:S(2)}) %collective-permute-start.3) | collective-permute-done | bytes 720928 | tf_op jit(solution)/shard_map/ppermute | solution.py:232
  28.0 0.9 copy-done.3
  28.8 3.6 %collective-permute-start.6 = (bf16[64,5632]{1,0:T(8,128)(2,1)S(1)}, bf16[64,5632]{1,0:T(8,128)(2,1)}, u32[]{:S(2)}, u32[]{:S(2)}) collective-permute-start(bf16[64,5632]{1,0:T(8,128)(2,1)S(1)} %copy-done.1), channel_id=1, source_target_pairs={{0,12},{1,13},{2,14},{3,15},{4,0},{5,1},{6,2},{7,3},{8,4},{9,5},{1... | collective-permute-start | bytes 2162696 | tf_op jit(solution)/shard_map/ppermute | solution.py:232
  32.4 0.0 collective-permute-done.4.refs_2_
  32.4 1.5 %collective-permute-start.5 = (bf16[64,5632]{1,0:T(8,128)(2,1)S(1)}, bf16[64,5632]{1,0:T(8,128)(2,1)S(1)}, u32[]{:S(2)}, u32[]{:S(2)}) collective-permute-start(bf16[64,5632]{1,0:T(8,128)(2,1)S(1)} %collective-permute-done.4.refs_2_), channel_id=1, source_target_pairs={{0,2},{1,3},{2,0},{3,1},{4,6},{5,7},{6,4},{7,5},{8,10},{9,11},{10,... | collective-permute-start | bytes 2162696 | tf_op jit(solution)/shard_map/ppermute | solution.py:232
  34.0 0.0 collective-permute-done.other
  34.0 0.0 collective-permute-start.8
  34.0 0.9 copy-done.5
  34.9 14.2 %collective-permute-done.6.refs_4_ = bf16[64,5632]{1,0:T(8,128)(2,1)} collective-permute-done((bf16[64,5632]{1,0:T(8,128)(2,1)S(1)}, bf16[64,5632]{1,0:T(8,128)(2,1)}, u32[]{:S(2)}, u32[]{:S(2)}) %collective-permute-start.6) | collective-permute-done | bytes 720928 | tf_op jit(solution)/shard_map/ppermute | solution.py:232
  49.0 1.5 %collective-permute-start.7 = (bf16[64,5632]{1,0:T(8,128)(2,1)}, bf16[64,5632]{1,0:T(8,128)(2,1)}, u32[]{:S(2)}, u32[]{:S(2)}) collective-permute-start(bf16[64,5632]{1,0:T(8,128)(2,1)} %collective-permute-done.6.refs_4_), channel_id=1, source_target_pairs={{0,2},{1,3},{2,0},{3,1},{4,6},{5,7},{6,4},{7,5},{8,10},{9,11},{10,... | collective-permute-start | bytes 2162696 | tf_op jit(solution)/shard_map/ppermute | solution.py:232
  50.6 0.9 copy-done.7
  51.4 0.0 collective-permute-done.1.x
  51.4 12.4 %collective-permute-done.8.refs_6_ = bf16[64,5632]{1,0:T(8,128)(2,1)} collective-permute-done((bf16[64,5632]{1,0:T(8,128)(2,1)S(1)}, bf16[64,5632]{1,0:T(8,128)(2,1)}, u32[]{:S(2)}, u32[]{:S(2)}) %collective-permute-start.8) | collective-permute-done | bytes 720928 | tf_op jit(solution)/shard_map/ppermute | solution.py:232
  63.8 1.5 %collective-permute-start.9 = (bf16[64,5632]{1,0:T(8,128)(2,1)}, bf16[64,5632]{1,0:T(8,128)(2,1)}, u32[]{:S(2)}, u32[]{:S(2)}) collective-permute-start(bf16[64,5632]{1,0:T(8,128)(2,1)} %collective-permute-done.8.refs_6_), channel_id=1, source_target_pairs={{0,2},{1,3},{2,0},{3,1},{4,6},{5,7},{6,4},{7,5},{8,10},{9,11},{10,... | collective-permute-start | bytes 2162696 | tf_op jit(solution)/shard_map/ppermute | solution.py:232
  65.3 0.1 stack.85
  65.5 0.0 collective-permute-done.7.refs_5_
  65.5 1.4 %copy-done = bf16[128,5760]{1,0:T(8,128)(2,1)S(1)} copy-done((bf16[128,5760]{1,0:T(8,128)(2,1)S(1)}, bf16[128,5760]{1,0:T(8,128)(2,1)}, u32[]{:S(2)}) %copy-start) | copy-done | bytes 1474584
  66.8 1.1 copy-done.2
  68.0 1.1 copy-done.4
  69.1 1.1 copy-done.6
  70.2 1.1 copy-done.8
  71.3 3.8 %project_early.1.refs_8_ = f32[3,128,256]{2,1,0:T(8,128)S(1)} custom-call(s32[2,8]{1,0:T(2,128)S(1)} %pad_add_fusion.eid_ref, bf16[128,5760]{1,0:T(8,128)(2,1)S(1)} %copy-done, bf16[128,5760]{1,0:T(8,128)(2,1)S(1)} %collective-permute-done.other, bf16[128,5760]{1,0:T(8,128)(2,1)S(1)} %collective-permute-done.1.x, bf16[64,5632]{1,0:T(8,128)(2,1)S(1)} %copy-done.2, ...), custom_call_target="tpu_custom_call" | custom-call | tf_op jit(solution)/shard_map/project_early/pallas_call | solution.py:138
  75.1 5.5 %collective-permute-done.9.refs_7_ = bf16[64,5632]{1,0:T(8,128)(2,1)} collective-permute-done((bf16[64,5632]{1,0:T(8,128)(2,1)}, bf16[64,5632]{1,0:T(8,128)(2,1)}, u32[]{:S(2)}, u32[]{:S(2)}) %collective-permute-start.9) | collective-permute-done | bytes 720928 | tf_op jit(solution)/shard_map/ppermute | solution.py:232
  80.6 5.3 %project_last.1 = (f32[128,256]{1,0:T(8,128)S(1)}, f32[128,256]{1,0:T(8,128)S(1)}, f32[128,256]{1,0:T(8,128)S(1)}, f32[128,256]{1,0:T(8,128)S(1)}) custom-call(s32[2,8]{1,0:T(2,128)S(1)} %pad_add_fusion.eid_ref, bf16[128,5760]{1,0:T(8,128)(2,1)S(1)} %copy-done, bf16[128,5760]{1,0:T(8,128)(2,1)S(1)} %collective-permute-done.other, ...), custom_call_target="tpu_custom_call" | custom-call | tf_op jit(solution)/shard_map/project_last/pallas_call | solution.py:138
  85.9 0.0 copy-start.11
  85.9 0.6 copy-done.11
  86.5 0.3 collective-permute-start.11
  86.8 1.6 %collective-permute-start.12 = (f32[128,256]{1,0:T(8,128)S(1)}, f32[128,256]{1,0:T(8,128)S(1)}, u32[]{:S(2)}, u32[]{:S(2)}) collective-permute-start(f32[128,256]{1,0:T(8,128)S(1)} %get-tuple-element.30), channel_id=1, source_target_pairs={{0,17},{1,16},{2,19},{3,18},{4,21},{5,20},{6,23},{7,22},{8,25},{9,... | collective-permute-start | bytes 393224 | tf_op jit(solution)/shard_map/ppermute | solution.py:232
  88.4 0.0 collective-permute-done.10.p1
  88.4 4.4 %collective-permute-done.11.p2 = f32[128,256]{1,0:T(8,128)S(1)} collective-permute-done((f32[128,256]{1,0:T(8,128)S(1)}, f32[128,256]{1,0:T(8,128)S(1)}, u32[]{:S(2)}, u32[]{:S(2)}) %collective-permute-start.11) | collective-permute-done | bytes 131104 | tf_op jit(solution)/shard_map/ppermute | solution.py:232
  92.8 2.0 %collective-permute-done.12.p3 = f32[128,256]{1,0:T(8,128)S(1)} collective-permute-done((f32[128,256]{1,0:T(8,128)S(1)}, f32[128,256]{1,0:T(8,128)S(1)}, u32[]{:S(2)}, u32[]{:S(2)}) %collective-permute-start.12) | collective-permute-done | bytes 131104 | tf_op jit(solution)/shard_map/ppermute | solution.py:232
  94.9 0.7 copy-done.14
  95.5 2.4 %gram.1.refs_1_ = bf16[16,16,128]{2,1,0:T(8,128)(2,1)} custom-call(f32[128,256]{1,0:T(8,128)} %copy-done.11, f32[128,256]{1,0:T(8,128)} %copy-done.12, f32[128,256]{1,0:T(8,128)} %copy-done.13, f32[128,256]{1,0:T(8,128)} %copy-done.14, s32[1,256]{1,0:T(1,128)} %bitcast.36), custom_call_target="tpu_custom_call" | custom-call | tf_op jit(solution)/shard_map/gram/pallas_call | solution.py:172
  98.0 1.5 %collective-permute-start.13 = (bf16[16,16,128]{2,1,0:T(8,128)(2,1)}, bf16[16,16,128]{2,1,0:T(8,128)(2,1)S(1)}, u32[]{:S(2)}, u32[]{:S(2)}) collective-permute-start(bf16[16,16,128]{2,1,0:T(8,128)(2,1)} %gram.1.refs_1_), channel_id=1, source_target_pairs={{0,2},{1,3},{2,0},{3,1},{4,6},{5,7},{6,4},{7,5},{8,10},{9,11},{10,... | collective-permute-start | bytes 196616 | tf_op jit(solution)/shard_map/ppermute | solution.py:232
  99.5 1.7 %collective-permute-start.14 = (bf16[16,16,128]{2,1,0:T(8,128)(2,1)}, bf16[16,16,128]{2,1,0:T(8,128)(2,1)S(1)}, u32[]{:S(2)}, u32[]{:S(2)}) collective-permute-start(bf16[16,16,128]{2,1,0:T(8,128)(2,1)} %gram.1.refs_1_), channel_id=1, source_target_pairs={{0,4},{1,5},{2,6},{3,7},{4,0},{5,1},{6,2},{7,3},{8,12},{9,13},{10,... | collective-permute-start | bytes 196616 | tf_op jit(solution)/shard_map/ppermute | solution.py:232
  101.2 0.3 collective-permute-start.15
  101.4 3.0 %collective-permute-start.16 = (bf16[16,16,128]{2,1,0:T(8,128)(2,1)}, bf16[16,16,128]{2,1,0:T(8,128)(2,1)S(1)}, u32[]{:S(2)}, u32[]{:S(2)}) collective-permute-start(bf16[16,16,128]{2,1,0:T(8,128)(2,1)} %gram.1.refs_1_), channel_id=1, source_target_pairs={{0,8},{1,9},{2,10},{3,11},{4,12},{5,13},{6,14},{7,15},{8,0},{9,1},... | collective-permute-start | bytes 196616 | tf_op jit(solution)/shard_map/ppermute | solution.py:232
  104.5 0.9 collective-permute-start.17
  105.3 0.9 bitcast_dynamic-update-slice_fusion.7
  106.2 0.0 collective-permute-done.13.refs_2_
  106.2 3.5 %collective-permute-start.18 = (bf16[16,16,128]{2,1,0:T(8,128)(2,1)}, bf16[16,16,128]{2,1,0:T(8,128)(2,1)S(1)}, u32[]{:S(2)}, u32[]{:S(2)}) collective-permute-start(bf16[16,16,128]{2,1,0:T(8,128)(2,1)} %gram.1.refs_1_), channel_id=1, source_target_pairs={{0,12},{1,13},{2,14},{3,15},{4,8},{5,9},{6,10},{7,11},{8,4},{9,5},... | collective-permute-start | bytes 196616 | tf_op jit(solution)/shard_map/ppermute | solution.py:232
  109.7 0.6 collective-permute-start.19
  110.4 0.0 collective-permute-done.15.refs_4_
  110.4 3.2 %collective-permute-done.17.refs_6_ = bf16[16,16,128]{2,1,0:T(8,128)(2,1)S(1)} collective-permute-done((bf16[16,16,128]{2,1,0:T(8,128)(2,1)}, bf16[16,16,128]{2,1,0:T(8,128)(2,1)S(1)}, u32[]{:S(2)}, u32[]{:S(2)}) %collective-permute-start.17) | collective-permute-done | bytes 65568 | tf_op jit(solution)/shard_map/ppermute | solution.py:232
  113.7 3.3 %collective-permute-done.19.refs_8_ = bf16[16,16,128]{2,1,0:T(8,128)(2,1)S(1)} collective-permute-done((bf16[16,16,128]{2,1,0:T(8,128)(2,1)}, bf16[16,16,128]{2,1,0:T(8,128)(2,1)S(1)}, u32[]{:S(2)}, u32[]{:S(2)}) %collective-permute-start.19) | collective-permute-done | bytes 65568 | tf_op jit(solution)/shard_map/ppermute | solution.py:232
  117.1 0.1 collective-permute-start.20
  117.2 0.1 pad_add_fusion.1.refs_0_
  117.2 1.8 %collective-permute-done.20.refs_9_ = bf16[8,16,16,128]{3,2,1,0:T(8,128)(2,1)S(1)} collective-permute-done((bf16[8,16,16,128]{3,2,1,0:T(8,128)(2,1)S(1)}, bf16[8,16,16,128]{3,2,1,0:T(8,128)(2,1)S(1)}, u32[]{:S(2)}, u32[]{:S(2)}) %collective-permute-start.20) | collective-permute-done | bytes 524320 | tf_op jit(solution)/shard_map/ppermute | solution.py:232
  119.0 1.6 %copy-done.9 = bf16[4096,256]{1,0:T(8,128)(2,1)S(1)} copy-done((bf16[4096,256]{1,0:T(8,128)(2,1)S(1)}, bf16[4096,256]{1,0:T(8,128)(2,1)}, u32[]{:S(2)}) %copy-start.9) | copy-done | bytes 2097176
  120.6 0.8 copy-done.10
  121.5 1.2 precondition.1
  122.7 11.8 %all_to_all.5 = f32[16,8,256]{2,1,0:T(8,128)S(1)} all-to-all(f32[16,8,256]{2,1,0:T(8,128)S(1)} %precondition.1), channel_id=1, replica_groups=mesh['groups'=2,'dp'=16] {'dp'}, dimensions={0} | all-to-all | bytes 262144 | tf_op jit(solution)/shard_map/all_to_all | solution.py:332
  134.5 0.7 copy.17
  (34 shorter events, 0.2 us)
Async XLA Ops:
  5.9 28.0 %collective-permute-start = (bf16[128,5760]{1,0:T(8,128)(2,1)}, bf16[128,5760]{1,0:T(8,128)(2,1)S(1)}, u32[]{:S(2)}, u32[]{:S(2)}) collective-permute-start(bf16[128,5760]{1,0:T(8,128)(2,1)} %get-tuple-element.21), channel_id=1, source_target_pairs={{0,1},{1,0},{2,3},{3,2},{4,5},{5,4},{6,7},{7,6},{8,9},{9,8},{10,11... | collective-permute-start | bytes 4423688 | tf_op jit(solution)/shard_map/ppermute | solution.py:232
  7.0 44.5 %collective-permute-start.1 = (bf16[128,5760]{1,0:T(8,128)(2,1)}, bf16[128,5760]{1,0:T(8,128)(2,1)S(1)}, u32[]{:S(2)}, u32[]{:S(2)}) collective-permute-start(bf16[128,5760]{1,0:T(8,128)(2,1)} %get-tuple-element.18), channel_id=1, source_target_pairs={{0,16},{1,17},{2,18},{3,19},{4,20},{5,21},{6,22},{7,23},{8,24},{9,... | collective-permute-start | bytes 4423688 | tf_op jit(solution)/shard_map/ppermute | solution.py:232
  9.5 19.3 %copy-start.1 = (bf16[64,5632]{1,0:T(8,128)(2,1)S(1)}, bf16[64,5632]{1,0:T(8,128)(2,1)}, u32[]{:S(2)}) copy-start(bf16[64,5632]{1,0:T(8,128)(2,1)} %get-tuple-element.23.refs_0_) | copy-start | bytes 2162692
  9.5 18.4 %collective-permute-start.3 = (bf16[64,5632]{1,0:T(8,128)(2,1)}, bf16[64,5632]{1,0:T(8,128)(2,1)S(1)}, u32[]{:S(2)}, u32[]{:S(2)}) collective-permute-start(bf16[64,5632]{1,0:T(8,128)(2,1)} %get-tuple-element.23.refs_0_), channel_id=1, source_target_pairs={{0,2},{1,3},{2,0},{3,1},{4,6},{5,7},{6,4},{7,5},{8,10},{9,11},{10,... | collective-permute-start | bytes 2162696 | tf_op jit(solution)/shard_map/ppermute | solution.py:232
  11.1 21.4 %collective-permute-start.4 = (bf16[64,5632]{1,0:T(8,128)(2,1)}, bf16[64,5632]{1,0:T(8,128)(2,1)S(1)}, u32[]{:S(2)}, u32[]{:S(2)}) collective-permute-start(bf16[64,5632]{1,0:T(8,128)(2,1)} %get-tuple-element.23.refs_0_), channel_id=1, source_target_pairs={{0,4},{1,5},{2,6},{3,7},{4,8},{5,9},{6,10},{7,11},{8,12},{9,13},{1... | collective-permute-start | bytes 2162696 | tf_op jit(solution)/shard_map/ppermute | solution.py:232
  16.6 58.5 %collective-permute-start.2 = (bf16[128,5760]{1,0:T(8,128)(2,1)}, bf16[128,5760]{1,0:T(8,128)(2,1)}, u32[]{:S(2)}, u32[]{:S(2)}) collective-permute-start(bf16[128,5760]{1,0:T(8,128)(2,1)} %get-tuple-element.22), channel_id=1, source_target_pairs={{0,17},{1,16},{2,19},{3,18},{4,21},{5,20},{6,23},{7,22},{8,25},{9,... | collective-permute-start | bytes 4423688 | tf_op jit(solution)/shard_map/ppermute | solution.py:232
  28.0 0.9 copy-start.3
  28.8 20.2 %collective-permute-start.6 = (bf16[64,5632]{1,0:T(8,128)(2,1)S(1)}, bf16[64,5632]{1,0:T(8,128)(2,1)}, u32[]{:S(2)}, u32[]{:S(2)}) collective-permute-start(bf16[64,5632]{1,0:T(8,128)(2,1)S(1)} %copy-done.1), channel_id=1, source_target_pairs={{0,12},{1,13},{2,14},{3,15},{4,0},{5,1},{6,2},{7,3},{8,4},{9,5},{1... | collective-permute-start | bytes 2162696 | tf_op jit(solution)/shard_map/ppermute | solution.py:232
  32.4 18.1 %collective-permute-start.5 = (bf16[64,5632]{1,0:T(8,128)(2,1)S(1)}, bf16[64,5632]{1,0:T(8,128)(2,1)S(1)}, u32[]{:S(2)}, u32[]{:S(2)}) collective-permute-start(bf16[64,5632]{1,0:T(8,128)(2,1)S(1)} %collective-permute-done.4.refs_2_), channel_id=1, source_target_pairs={{0,2},{1,3},{2,0},{3,1},{4,6},{5,7},{6,4},{7,5},{8,10},{9,11},{10,... | collective-permute-start | bytes 2162696 | tf_op jit(solution)/shard_map/ppermute | solution.py:232
  34.0 29.8 %collective-permute-start.8 = (bf16[64,5632]{1,0:T(8,128)(2,1)S(1)}, bf16[64,5632]{1,0:T(8,128)(2,1)}, u32[]{:S(2)}, u32[]{:S(2)}) collective-permute-start(bf16[64,5632]{1,0:T(8,128)(2,1)S(1)} %collective-permute-done.4.refs_2_), channel_id=1, source_target_pairs={{0,4},{1,5},{2,6},{3,7},{4,8},{5,9},{6,10},{7,11},{8,12},{9,13},{1... | collective-permute-start | bytes 2162696 | tf_op jit(solution)/shard_map/ppermute | solution.py:232
  34.0 0.9 copy-start.5
  49.0 16.4 %collective-permute-start.7 = (bf16[64,5632]{1,0:T(8,128)(2,1)}, bf16[64,5632]{1,0:T(8,128)(2,1)}, u32[]{:S(2)}, u32[]{:S(2)}) collective-permute-start(bf16[64,5632]{1,0:T(8,128)(2,1)} %collective-permute-done.6.refs_4_), channel_id=1, source_target_pairs={{0,2},{1,3},{2,0},{3,1},{4,6},{5,7},{6,4},{7,5},{8,10},{9,11},{10,... | collective-permute-start | bytes 2162696 | tf_op jit(solution)/shard_map/ppermute | solution.py:232
  50.6 0.9 copy-start.7
  63.8 16.8 %collective-permute-start.9 = (bf16[64,5632]{1,0:T(8,128)(2,1)}, bf16[64,5632]{1,0:T(8,128)(2,1)}, u32[]{:S(2)}, u32[]{:S(2)}) collective-permute-start(bf16[64,5632]{1,0:T(8,128)(2,1)} %collective-permute-done.8.refs_6_), channel_id=1, source_target_pairs={{0,2},{1,3},{2,0},{3,1},{4,6},{5,7},{6,4},{7,5},{8,10},{9,11},{10,... | collective-permute-start | bytes 2162696 | tf_op jit(solution)/shard_map/ppermute | solution.py:232
  65.5 1.4 %copy-start = (bf16[128,5760]{1,0:T(8,128)(2,1)S(1)}, bf16[128,5760]{1,0:T(8,128)(2,1)}, u32[]{:S(2)}) copy-start(bf16[128,5760]{1,0:T(8,128)(2,1)} %get-tuple-element.20.own) | copy-start | bytes 4423684
  66.8 1.1 copy-start.2
  68.0 1.1 copy-start.4
  69.1 1.1 copy-start.6
  70.2 1.1 copy-start.8
  85.9 0.7 copy-start.11
  86.5 1.9 %collective-permute-start.10 = (f32[128,256]{1,0:T(8,128)S(1)}, f32[128,256]{1,0:T(8,128)S(1)}, u32[]{:S(2)}, u32[]{:S(2)}) collective-permute-start(f32[128,256]{1,0:T(8,128)S(1)} %get-tuple-element.28), channel_id=1, source_target_pairs={{0,1},{1,0},{2,3},{3,2},{4,5},{5,4},{6,7},{7,6},{8,9},{9,8},{10,11... | collective-permute-start | bytes 393224 | tf_op jit(solution)/shard_map/ppermute | solution.py:232
  86.5 6.3 %collective-permute-start.11 = (f32[128,256]{1,0:T(8,128)S(1)}, f32[128,256]{1,0:T(8,128)S(1)}, u32[]{:S(2)}, u32[]{:S(2)}) collective-permute-start(f32[128,256]{1,0:T(8,128)S(1)} %get-tuple-element.29), channel_id=1, source_target_pairs={{0,16},{1,17},{2,18},{3,19},{4,20},{5,21},{6,22},{7,23},{8,24},{9,... | collective-permute-start | bytes 393224 | tf_op jit(solution)/shard_map/ppermute | solution.py:232
  86.8 8.1 %collective-permute-start.12 = (f32[128,256]{1,0:T(8,128)S(1)}, f32[128,256]{1,0:T(8,128)S(1)}, u32[]{:S(2)}, u32[]{:S(2)}) collective-permute-start(f32[128,256]{1,0:T(8,128)S(1)} %get-tuple-element.30), channel_id=1, source_target_pairs={{0,17},{1,16},{2,19},{3,18},{4,21},{5,20},{6,23},{7,22},{8,25},{9,... | collective-permute-start | bytes 393224 | tf_op jit(solution)/shard_map/ppermute | solution.py:232
  88.4 6.5 %copy-start.12 = (f32[128,256]{1,0:T(8,128)}, f32[128,256]{1,0:T(8,128)S(1)}, u32[]{:S(2)}) copy-start(f32[128,256]{1,0:T(8,128)S(1)} %collective-permute-done.10.p1) | copy-start | bytes 393220
  92.8 2.0 %copy-start.13 = (f32[128,256]{1,0:T(8,128)}, f32[128,256]{1,0:T(8,128)S(1)}, u32[]{:S(2)}) copy-start(f32[128,256]{1,0:T(8,128)S(1)} %collective-permute-done.11.p2) | copy-start | bytes 393220
  94.9 0.7 copy-start.14
  98.0 8.3 %collective-permute-start.13 = (bf16[16,16,128]{2,1,0:T(8,128)(2,1)}, bf16[16,16,128]{2,1,0:T(8,128)(2,1)S(1)}, u32[]{:S(2)}, u32[]{:S(2)}) collective-permute-start(bf16[16,16,128]{2,1,0:T(8,128)(2,1)} %gram.1.refs_1_), channel_id=1, source_target_pairs={{0,2},{1,3},{2,0},{3,1},{4,6},{5,7},{6,4},{7,5},{8,10},{9,11},{10,... | collective-permute-start | bytes 196616 | tf_op jit(solution)/shard_map/ppermute | solution.py:232
  99.5 10.2 %collective-permute-start.14 = (bf16[16,16,128]{2,1,0:T(8,128)(2,1)}, bf16[16,16,128]{2,1,0:T(8,128)(2,1)S(1)}, u32[]{:S(2)}, u32[]{:S(2)}) collective-permute-start(bf16[16,16,128]{2,1,0:T(8,128)(2,1)} %gram.1.refs_1_), channel_id=1, source_target_pairs={{0,4},{1,5},{2,6},{3,7},{4,0},{5,1},{6,2},{7,3},{8,12},{9,13},{10,... | collective-permute-start | bytes 196616 | tf_op jit(solution)/shard_map/ppermute | solution.py:232
  101.2 9.2 %collective-permute-start.15 = (bf16[16,16,128]{2,1,0:T(8,128)(2,1)}, bf16[16,16,128]{2,1,0:T(8,128)(2,1)S(1)}, u32[]{:S(2)}, u32[]{:S(2)}) collective-permute-start(bf16[16,16,128]{2,1,0:T(8,128)(2,1)} %gram.1.refs_1_), channel_id=1, source_target_pairs={{0,6},{1,7},{2,4},{3,5},{4,2},{5,3},{6,0},{7,1},{8,14},{9,15},{10,... | collective-permute-start | bytes 196616 | tf_op jit(solution)/shard_map/ppermute | solution.py:232
  101.4 8.9 %collective-permute-start.16 = (bf16[16,16,128]{2,1,0:T(8,128)(2,1)}, bf16[16,16,128]{2,1,0:T(8,128)(2,1)S(1)}, u32[]{:S(2)}, u32[]{:S(2)}) collective-permute-start(bf16[16,16,128]{2,1,0:T(8,128)(2,1)} %gram.1.refs_1_), channel_id=1, source_target_pairs={{0,8},{1,9},{2,10},{3,11},{4,12},{5,13},{6,14},{7,15},{8,0},{9,1},... | collective-permute-start | bytes 196616 | tf_op jit(solution)/shard_map/ppermute | solution.py:232
  104.5 9.2 %collective-permute-start.17 = (bf16[16,16,128]{2,1,0:T(8,128)(2,1)}, bf16[16,16,128]{2,1,0:T(8,128)(2,1)S(1)}, u32[]{:S(2)}, u32[]{:S(2)}) collective-permute-start(bf16[16,16,128]{2,1,0:T(8,128)(2,1)} %gram.1.refs_1_), channel_id=1, source_target_pairs={{0,10},{1,11},{2,8},{3,9},{4,14},{5,15},{6,12},{7,13},{8,2},{9,3},... | collective-permute-start | bytes 196616 | tf_op jit(solution)/shard_map/ppermute | solution.py:232
  106.2 7.5 %collective-permute-start.18 = (bf16[16,16,128]{2,1,0:T(8,128)(2,1)}, bf16[16,16,128]{2,1,0:T(8,128)(2,1)S(1)}, u32[]{:S(2)}, u32[]{:S(2)}) collective-permute-start(bf16[16,16,128]{2,1,0:T(8,128)(2,1)} %gram.1.refs_1_), channel_id=1, source_target_pairs={{0,12},{1,13},{2,14},{3,15},{4,8},{5,9},{6,10},{7,11},{8,4},{9,5},... | collective-permute-start | bytes 196616 | tf_op jit(solution)/shard_map/ppermute | solution.py:232
  109.7 7.3 %collective-permute-start.19 = (bf16[16,16,128]{2,1,0:T(8,128)(2,1)}, bf16[16,16,128]{2,1,0:T(8,128)(2,1)S(1)}, u32[]{:S(2)}, u32[]{:S(2)}) collective-permute-start(bf16[16,16,128]{2,1,0:T(8,128)(2,1)} %gram.1.refs_1_), channel_id=1, source_target_pairs={{0,14},{1,15},{2,12},{3,13},{4,10},{5,11},{6,8},{7,9},{8,6},{9,7},... | collective-permute-start | bytes 196616 | tf_op jit(solution)/shard_map/ppermute | solution.py:232
  117.1 2.0 %collective-permute-start.20 = (bf16[8,16,16,128]{3,2,1,0:T(8,128)(2,1)S(1)}, bf16[8,16,16,128]{3,2,1,0:T(8,128)(2,1)S(1)}, u32[]{:S(2)}, u32[]{:S(2)}) collective-permute-start(bf16[8,16,16,128]{3,2,1,0:T(8,128)(2,1)S(1)} %bitcast_dynamic-update-slice_fusion), channel_id=1, source_target_pairs={{0,1},{1,0},{2,3},{3,2},{4,5},{5,4},{6,7},{7,6},{8,9},{9,8},{10,11... | collective-permute-start | bytes 1572872 | tf_op jit(solution)/shard_map/ppermute | solution.py:232
  119.0 1.6 %copy-start.9 = (bf16[4096,256]{1,0:T(8,128)(2,1)S(1)}, bf16[4096,256]{1,0:T(8,128)(2,1)}, u32[]{:S(2)}) copy-start(bf16[4096,256]{1,0:T(8,128)(2,1)} %refs_10_.1) | copy-start | bytes 6291460
  120.6 0.8 copy-start.10

commit v3 on v2

v3 whole, which is shorter than its diff:
```python
import functools

import jax
import jax.numpy as jnp
from jax import lax
from jax.experimental import pallas as pl
from jax.experimental.pallas import tpu as pltpu
from jax.sharding import PartitionSpec as P

EXPERTS = 8
PROJ = 64
TOK = 128
LANES = 128
VMEM = 28 * 1024 * 1024
AXES = ("groups", "dp")


def position():
    place = lax.axis_index("dp")
    return lax.rem(place, 2), lax.div(place, 2), lax.rem(lax.axis_index("groups"), 2)


def piece_of(at, sizes):
    z_size, y_size, slices = sizes
    _, chip, _ = position()
    z, y = lax.div(chip, y_size), lax.rem(chip, y_size)
    step, across = at
    first = 2 * (lax.rem(z + (step + z_size), z_size) * y_size + (1 - y if across else y))
    return lax.div(first, slices), lax.div(lax.rem(first, slices), 2)


def nt(rows, table):
    return lax.dot_general(rows, table, (((1,), (1,)), ((), ())), preferred_element_type=jnp.float32)


def pick(total, routes, experts, sub):
    low = lax.broadcasted_iota(jnp.int32, (TOK, LANES), 1) < PROJ
    out = []
    for k in range(2):
        picked = jnp.zeros((TOK, LANES), jnp.float32)
        for a in range(sub):
            for pair in range(len(experts) // 2):
                even, odd = experts[2 * pair], experts[2 * pair + 1]
                wanted = jnp.where(
                    low,
                    jnp.where(even[1] == a, even[0], -1),
                    jnp.where(odd[1] == a, odd[0], -1),
                ).astype(jnp.float32)
                picked += jnp.where(routes[:, k : k + 1] == wanted, total(a, pair), 0.0)
        out.append(picked + pltpu.roll(picked, PROJ, 1))
    return out


def right_sums(sub, width, toks, pieces):
    table = jnp.concatenate([p[:, :width] for p in pieces], axis=0)
    return [nt(toks[:, a * width : (a + 1) * width], table) for a in range(sub)]


def left_sums(sub, width, toks, pieces):
    table = jnp.concatenate([p[:, width:] for p in pieces], axis=0)
    at, size = sub * width, table.shape[1]
    return [nt(toks[:, at + a * size : at + (a + 1) * size], table) for a in range(sub)]


def picks(rows, tables, experts, width, sub):
    toks = jnp.concatenate(rows, axis=0)
    right, left = right_sums(sub, width, toks, tables), left_sums(sub, width, toks, tables)
    low = lax.broadcasted_iota(jnp.int32, (TOK, LANES), 1) < PROJ
    picked = []
    for b in range(len(rows)):
        here = slice(b * TOK, (b + 1) * TOK)
        named = toks[here, -LANES:].astype(jnp.float32)

        def pick_of(sums):
            return pick(lambda a, pair: sums[a][here, pair * LANES : (pair + 1) * LANES], named, experts, sub)

        picked.append([jnp.where(low, x, y) for x, y in zip(pick_of(left), pick_of(right))])
    return picked


def early_kernel(sub, width, ids, sizes, own, other, x, *refs):
    experts = [piece_of(at, sizes) for at in ids]
    rows = [own[...], other[...], x[...]]
    for b, slots in enumerate(picks(rows, refs[:-1], experts, width, sub)):
        for k, got in enumerate(slots):
            refs[-1][b, :, k * LANES : (k + 1) * LANES] = got


def mid_kernel(sub, width, ids, sizes, xc, *refs):
    experts = [piece_of(at, sizes) for at in ids]
    for k, got in enumerate(picks([xc[...]], refs[:-1], experts, width, sub)[0]):
        refs[-1][:, k * LANES : (k + 1) * LANES] = got


def last_kernel(sub, width, ids, sizes, own, other, x, xc, piece0, piece1, early_ref, mid_ref, *outs):
    experts = [piece_of(at, sizes) for at in ids]
    rows = [own[...], other[...], x[...], xc[...]]
    for b, slots in enumerate(picks(rows, (piece0, piece1), experts, width, sub)):
        for k, got in enumerate(slots):
            lanes = slice(k * LANES, (k + 1) * LANES)
            outs[b][:, lanes] = (early_ref[b, :, lanes] if b < 3 else mid_ref[:, lanes]) + got


def pack_kernel(outputs, routes_ref, *refs):
    core, _, half = position()
    n_blocks = sum(len(blocks) for blocks in outputs)
    ins, outs = refs[:n_blocks], refs[n_blocks : n_blocks + len(outputs)]
    buffers, in_sems, out_sems = refs[n_blocks + len(outputs) : -2], refs[-2], refs[-1]
    copies, i = [], 0
    for blocks, buffer in zip(outputs, buffers):
        at, group = 0, []
        for width, place, offset in blocks:
            start = pl.multiple_of((place(core, half) + offset) * width, LANES)
            copy = pltpu.make_async_copy(
                ins[i].at[:, pl.ds(start, width)], buffer.at[:, at : at + width], in_sems.at[i]
            )
            copy.start()
            group.append(copy)
            at, i = at + width, i + 1
        copies.append(group)
    row = lax.broadcasted_iota(jnp.int32, (TOK, LANES), 0)
    routes = routes_ref[...].astype(jnp.float32)
    named = jnp.where(row == 0, routes[0:1], jnp.where(row == 1, routes[1:2], 0.0))
    named = jnp.transpose(named).astype(jnp.bfloat16)
    back = []
    for i, (blocks, buffer, group) in enumerate(zip(outputs, buffers, copies)):
        size = sum(block[0] for block in blocks)
        if buffer.shape[1] > size:
            buffer[:, size:] = named
        for copy in group:
            copy.wait()
        copy = pltpu.make_async_copy(buffer, outs[i], out_sems.at[i])
        copy.start()
        back.append(copy)
    for copy in back:
        copy.wait()


def pack(routes, outputs, name):
    blocks = [b for out in outputs for b in out]
    shapes = []
    for out in outputs:
        rows = out[0][0].shape[0]
        shapes.append((rows, sum(b[1] for b in out) + (LANES if rows == TOK else 0)))
    hbm = pl.BlockSpec(memory_space=pl.ANY)
    return pl.pallas_call(
        functools.partial(pack_kernel, [[b[1:] for b in out] for out in outputs]),
        in_specs=[pl.BlockSpec(memory_space=pltpu.VMEM)] + [hbm] * len(blocks),
        out_specs=[hbm] * len(shapes),
        out_shape=[jax.ShapeDtypeStruct(x, jnp.bfloat16) for x in shapes],
        scratch_shapes=[pltpu.VMEM(x, jnp.bfloat16) for x in shapes]
        + [pltpu.SemaphoreType.DMA((len(blocks),)), pltpu.SemaphoreType.DMA((len(shapes),))],
        compiler_params=pltpu.CompilerParams(vmem_limit_bytes=2 * VMEM),
        name=name,
    )(routes, *[b[0] for b in blocks])


def local(kernel, name, out_shape, operands):
    vmem = pl.BlockSpec(memory_space=pltpu.VMEM)
    return pl.pallas_call(
        kernel,
        in_specs=[vmem] * len(operands),
        out_specs=jax.tree.map(lambda _: vmem, out_shape),
        out_shape=out_shape,
        compiler_params=pltpu.CompilerParams(vmem_limit_bytes=VMEM),
        name=name,
    )(*operands)


def gram_kernel(p0, p1, p2, p3, routes_ref, out_ref, flat):
    total = (p0[...] + p1[...]) + (p2[...] + p3[...])
    first, second = total[:, :LANES], total[:, LANES:]
    left = jnp.concatenate([jnp.transpose(first)[:PROJ], jnp.transpose(second)[:PROJ]], axis=1)
    right = jnp.concatenate([first, second], axis=0)
    named = routes_ref[...]
    rows = jnp.concatenate([jnp.where(named == e, left, 0.0) for e in range(EXPERTS)], axis=0)
    grams = lax.dot_general(
        rows,
        right,
        (((1,), (0,)), ((), ())),
        precision=lax.Precision.HIGHEST,
        preferred_element_type=jnp.float32,
    )
    grams = grams * (TOK**-0.5)
    low = lax.broadcasted_iota(jnp.int32, (PROJ // 2, LANES), 1) < PROJ
    for e in range(EXPERTS):
        top = grams[e * PROJ : e * PROJ + PROJ // 2]
        bottom = grams[e * PROJ + PROJ // 2 : (e + 1) * PROJ]
        flat[:, e, :] = jnp.where(low, pltpu.roll(top, PROJ, 1), bottom)
    mine = flat[...].reshape(PROJ // 4, 2 * EXPERTS, LANES).astype(jnp.bfloat16)
    for j in range(out_ref.shape[0]):
        out_ref[j] = mine


def gram(parts, routes, copies):
    return pl.pallas_call(
        gram_kernel,
        out_shape=jax.ShapeDtypeStruct((copies, PROJ // 4, 2 * EXPERTS, LANES), jnp.bfloat16),
        scratch_shapes=[pltpu.VMEM((PROJ // 2, EXPERTS, LANES), jnp.float32)],
        compiler_params=pltpu.CompilerParams(vmem_limit_bytes=2 * VMEM),
        name="gram",
    )(*parts, routes)


def fisher_kernel(own, other, fisher, out_ref):
    n = 2 * own.shape[0]
    core, _, _ = position()
    total = jnp.zeros((n * EXPERTS, fisher.shape[1]), jnp.float32)
    for i in range(PROJ // 4):
        rows = jnp.concatenate([x[:, i].astype(jnp.float32) for x in (own, other)], axis=0)
        rows = rows.reshape(n, 2, EXPERTS, LANES)
        for h in range(2):
            p = 2 * i + h
            table = jnp.concatenate(
                [
                    fisher[p * PROJ : (p + 1) * PROJ, :],
                    fisher[(PROJ // 2 + p) * PROJ : (PROJ // 2 + p + 1) * PROJ, :],
                ],
                axis=0,
            )
            lhs = rows[:, h].reshape(n * EXPERTS, LANES).astype(jnp.bfloat16)
            total += jnp.dot(lhs, table, preferred_element_type=jnp.float32)
    for j in range(n // 2):
        out_ref[2 * j + core] = total[j * EXPERTS : (j + 1) * EXPERTS]
        out_ref[2 * j + 1 - core] = total[(n // 2 + j) * EXPERTS : (n // 2 + j + 1) * EXPERTS]


def shards(features, grads, routes, proj_in, proj_out, fisher_inverse):
    groups, n = lax.axis_size("groups"), lax.axis_size("dp")
    chips = n // 2
    slices = n // EXPERTS
    sub = slices // 2
    y_size = 2 if groups == 2 else 1
    z_size = chips // y_size
    def move(x, to):
        pairs = []
        for g in range(groups):
            for d in range(n):
                tg, td = to(g, d)
                pairs.append((g * n + d, tg * n + td))
        return lax.ppermute(x, AXES, pairs)

    def to_core(g, d):
        return g, d ^ 1

    def to_x(g, d):
        return g ^ 1, d

    def to_x_core(g, d):
        return g ^ 1, d ^ 1

    def to_y(g, d):
        return g, d ^ 2

    def to_z(g, d):
        return g, (d + 2 * y_size) % n

    def from_z(g, d):
        return g, (d - 2 * y_size) % n

    quarter_in, quarter_out = proj_in.shape[1] // 2, proj_out.shape[1] // 2

    def after(x, *others):
        return lax.optimization_barrier((x, *others))[0]

    def whole(place):
        return [(grads, quarter_out, place, 4 * a) for a in range(sub)] + [
            (features, quarter_in, place, 4 * a) for a in range(sub)
        ]

    def by_half(core, half):
        return half

    routes = routes.T
    table, send_other, send_x = pack(
        routes,
        [
            [(proj_out, quarter_out, by_half, 0), (proj_in, quarter_in, by_half, 0)],
            whole(lambda core, half: 2 * (1 - core) + half),
            whole(lambda core, half: 2 * core + 1 - half),
        ],
        "pack_first",
    )
    send_xc, own = pack(
        after(routes, send_x),
        [whole(lambda core, half: 2 * (1 - core) + 1 - half), whole(lambda core, half: 2 * core + half)],
        "pack_second",
    )

    facing = move(table, to_y) if y_size == 2 else table
    other, x = move(send_other, to_core), move(send_x, to_x)
    xc = move(after(send_xc, facing), to_x_core)
    blocks, ids = [table], [0]
    ups, downs = z_size // 2, (z_size - 1) // 2
    up = down = table
    for k in range(1, ups + 1):
        up = move(after(up, facing, other) if k == 2 else up, to_z)
        blocks.append(up)
        ids.append(-k)
        if k <= downs:
            down = move(down, from_z)
            blocks.append(down)
            ids.append(k)
    pieces, where = [], []
    for i, block in enumerate(blocks):
        for across in range(y_size):
            if across:
                if i == 1:
                    block = after(block, facing)
                if i == len(blocks) - 1:
                    block = after(block, x, pieces[3])
                block = move(block, to_y) if i else facing
            pieces.append(block)
            where.append((ids[i] % z_size, across))

    f32 = jnp.float32
    sizes = (z_size, y_size, slices)
    early = local(
        functools.partial(early_kernel, sub, quarter_out, where[:-2], sizes),
        "project_early",
        jax.ShapeDtypeStruct((3, TOK, 2 * LANES), f32),
        [own, other, x] + pieces[:-2],
    )
    mid = local(
        functools.partial(mid_kernel, sub, quarter_out, where[:-2], sizes),
        "project_mid",
        jax.ShapeDtypeStruct((TOK, 2 * LANES), f32),
        [after(xc, early)] + pieces[:-2],
    )
    partial = local(
        functools.partial(last_kernel, sub, quarter_out, where[-2:], sizes),
        "project_last",
        [jax.ShapeDtypeStruct((TOK, 2 * LANES), f32)] * 4,
        [own, other, x, xc] + pieces[-2:] + [early, mid],
    )
    sums = [partial[0], move(partial[1], to_core), move(partial[2], to_x), move(partial[3], to_x_core)]
    mine = gram(sums, routes.reshape(1, -1), chips)

    same_core = [list(range(c, n, 2)) for c in range(2)]
    grams = lax.all_to_all(mine, "dp", split_axis=0, concat_axis=0, axis_index_groups=same_core, tiled=True)
    columns = local(
        fisher_kernel,
        "precondition",
        jax.ShapeDtypeStruct((n, EXPERTS, fisher_inverse.shape[1]), f32),
        [grams, move(grams, to_core), fisher_inverse],
    )
    result = lax.all_to_all(columns, "dp", split_axis=0, concat_axis=0, tiled=True)
    return jnp.transpose(result, (1, 0, 2)).reshape(1, EXPERTS, PROJ * PROJ)


def solution(mesh):
    in_specs = (
        P(AXES, None),
        P(AXES, None),
        P(AXES, None),
        P(None, "dp"),
        P(None, "dp"),
        P(None, "dp"),
    )
    out_specs = P(AXES, None, None)
    return jax.shard_map(shards, mesh=mesh, in_specs=in_specs, out_specs=out_specs, check_vma=False)
```

time: 136 us -> 129 us (0.949)
  blocking collectives: 11.8 us -> 32 us
  local copies, waits for them, and re-layouts: 15.2 us -> 3.35 us
  starting transfers between devices: 28.4 us -> 17.2 us
  Pallas kernels: 20.6 us -> 16.6 us
  waiting for transfers between devices: 58.2 us -> 59.6 us
    all_to_all x0 -> x1, blocking collectives: none -> 20.5 us  [shards(): lax.all_to_all(mine, 'dp', split_axis=0, concat_axis=0, axis_index_groups...]
    ppermute x21 -> x14, starting transfers between devices: 28.4 us -> 17.2 us  [move(): return lax.ppermute(x, AXES, pairs)]
    unnamed x38 -> x17, local copies, waits for them, and re-layouts: 13.8 us -> 3.35 us
    pallas_call x6 -> x7, Pallas kernels: 20.6 us -> 16.6 us  [the longest x2 7.51 us: pack(): pl.pallas_call(functools.partial(pack_kernel, [[b[1:] for b in out] for o...]
    ppermute x21 -> x14, waiting for transfers between devices: 58.2 us -> 59.6 us  [move(): return lax.ppermute(x, AXES, pairs)]
  transfers between devices with their start and end apart: 21 -> 14, of which waited for: 9 -> 10; matrix products, arithmetic and copies ran while one was open for 1% -> 0% of each run, Pallas kernels for 6% -> 6%
where the time goes in v3:
time: 129 us
  waiting for transfers between devices  59.6 us (46%)
  blocking collectives  32 us (25%)
  starting transfers between devices  17.2 us (13%)
  Pallas kernels  16.6 us (13%)
  local copies, waits for them, and re-layouts  3.35 us (3%)
    ppermute x14, waiting for transfers between devices, move(): return lax.ppermute(x, AXES, pairs)  59.6 us
    all_to_all x1, blocking collectives, shards(): lax.all_to_all(mine, 'dp', split_axis=0, concat_axis=0, axis_index_groups...  20.5 us
    ppermute x14, starting transfers between devices, move(): return lax.ppermute(x, AXES, pairs)  17.2 us
    all_to_all x1, blocking collectives, shards(): lax.all_to_all(columns, 'dp', split_axis=0, concat_axis=0, tiled=True)  11.5 us
    pallas_call x2, Pallas kernels, pack(): pl.pallas_call(functools.partial(pack_kernel, [[b[1:] for b in out] for o...  7.51 us
    pallas_call x4, Pallas kernels, local(): pl.pallas_call(kernel, in_specs=[vmem] * len(operands), out_specs=jax.tre...  6.41 us
    unnamed x17, local copies, waits for them, and re-layouts  3.35 us
    pallas_call x1, Pallas kernels, gram(): pl.pallas_call(gram_kernel, out_shape=jax.ShapeDtypeStruct((copies, PROJ...  2.65 us
  transfers between devices with their start and end apart: 14, of which 10 were waited for; matrix products, arithmetic and copies ran while one was open for 0% of the time, Pallas kernels for 6%

profile of v3, /device:TPU:0, one launch (start us, length us, event | category | flops | bytes accessed | tf_op | source)
XLA Modules:
  0.0 128.8 jit_solution(14206433100116803566)
XLA Ops:
  0.0 3.9 %pack_first.1 = (bf16[64,5632]{1,0:T(8,128)(2,1)}, bf16[128,5760]{1,0:T(8,128)(2,1)}, bf16[128,5760]{1,0:T(8,128)(2,1)}) custom-call(s32[2,128]{1,0:T(2,128)} %bitcast.7, bf16[64,8192]{1,0:T(8,128)(2,1)} %refs_0_.2, bf16[64,3072]{1,0:T(8,128)(2,1)} %refs_1_.2, bf16[128,16384]{1,0:T(8,128)(2,1)} %refs_2_.3, bf16[128,6144]{1,0:T(8,128)(2,1)} %refs_3_.3, ...), custom_call_target="tpu_custom_call" | custom-call | tf_op jit(solution)/shard_map/pack_first/pallas_call | solution.py:146
  3.9 0.5 collective-permute-start
  4.4 2.6 %collective-permute-start.2 = (bf16[64,5632]{1,0:T(8,128)(2,1)}, bf16[64,5632]{1,0:T(8,128)(2,1)S(1)}, u32[]{:S(2)}, u32[]{:S(2)}) collective-permute-start(bf16[64,5632]{1,0:T(8,128)(2,1)} %get-tuple-element.25.refs_0_), channel_id=1, source_target_pairs={{0,2},{1,3},{2,0},{3,1},{4,6},{5,7},{6,4},{7,5},{8,10},{9,11},{10,... | collective-permute-start | bytes 2162696 | tf_op jit(solution)/shard_map/ppermute | solution.py:241
  7.0 0.0 copy-start.2
  7.0 1.5 %collective-permute-start.1 = (bf16[128,5760]{1,0:T(8,128)(2,1)}, bf16[128,5760]{1,0:T(8,128)(2,1)S(1)}, u32[]{:S(2)}, u32[]{:S(2)}) collective-permute-start(bf16[128,5760]{1,0:T(8,128)(2,1)} %get-tuple-element.20), channel_id=1, source_target_pairs={{0,16},{1,17},{2,18},{3,19},{4,20},{5,21},{6,22},{7,23},{8,24},{9,... | collective-permute-start | bytes 4423688 | tf_op jit(solution)/shard_map/ppermute | solution.py:241
  8.5 1.6 %collective-permute-start.4 = (bf16[64,5632]{1,0:T(8,128)(2,1)}, bf16[64,5632]{1,0:T(8,128)(2,1)S(1)}, u32[]{:S(2)}, u32[]{:S(2)}) collective-permute-start(bf16[64,5632]{1,0:T(8,128)(2,1)} %get-tuple-element.25.refs_0_), channel_id=1, source_target_pairs={{0,4},{1,5},{2,6},{3,7},{4,8},{5,9},{6,10},{7,11},{8,12},{9,13},{1... | collective-permute-start | bytes 2162696 | tf_op jit(solution)/shard_map/ppermute | solution.py:241
  10.1 3.6 %pack_second.1 = (bf16[128,5760]{1,0:T(8,128)(2,1)}, bf16[128,5760]{1,0:T(8,128)(2,1)}) custom-call(s32[2,128]{1,0:T(2,128)} %bitcast.8, bf16[128,16384]{1,0:T(8,128)(2,1)} %refs_2_.3, bf16[128,6144]{1,0:T(8,128)(2,1)} %refs_3_.3, bf16[128,16384]{1,0:T(8,128)(2,1)} %refs_2_.3, bf16[128,6144]{1,0:T(8,128)(2,1)} %refs_3_.3), custom_call_target="tpu_custom_call" | custom-call | tf_op jit(solution)/shard_map/pack_second/pallas_call | solution.py:146
  13.7 10.3 %collective-permute-done.2.refs_1_ = bf16[64,5632]{1,0:T(8,128)(2,1)S(1)} collective-permute-done((bf16[64,5632]{1,0:T(8,128)(2,1)}, bf16[64,5632]{1,0:T(8,128)(2,1)S(1)}, u32[]{:S(2)}, u32[]{:S(2)}) %collective-permute-start.2) | collective-permute-done | bytes 720928 | tf_op jit(solution)/shard_map/ppermute | solution.py:241
  24.0 1.0 collective-permute-start.3
  25.0 0.0 copy-done.2
  25.0 3.6 %collective-permute-start.8 = (bf16[64,5632]{1,0:T(8,128)(2,1)S(1)}, bf16[64,5632]{1,0:T(8,128)(2,1)S(1)}, u32[]{:S(2)}, u32[]{:S(2)}) collective-permute-start(bf16[64,5632]{1,0:T(8,128)(2,1)S(1)} %copy-done.2), channel_id=1, source_target_pairs={{0,12},{1,13},{2,14},{3,15},{4,0},{5,1},{6,2},{7,3},{8,4},{9,5},{1... | collective-permute-start | bytes 2162696 | tf_op jit(solution)/shard_map/ppermute | solution.py:241
  28.6 0.0 collective-permute-done.4.refs_2_
  28.6 1.5 %collective-permute-start.6 = (bf16[64,5632]{1,0:T(8,128)(2,1)S(1)}, bf16[64,5632]{1,0:T(8,128)(2,1)S(1)}, u32[]{:S(2)}, u32[]{:S(2)}) collective-permute-start(bf16[64,5632]{1,0:T(8,128)(2,1)S(1)} %collective-permute-done.4.refs_2_), channel_id=1, source_target_pairs={{0,2},{1,3},{2,0},{3,1},{4,6},{5,7},{6,4},{7,5},{8,10},{9,11},{10,... | collective-permute-start | bytes 2162696 | tf_op jit(solution)/shard_map/ppermute | solution.py:241
  30.1 0.0 collective-permute-done.other
  30.1 0.0 collective-permute-start.5
  30.1 15.0 %collective-permute-done.8.refs_4_ = bf16[64,5632]{1,0:T(8,128)(2,1)S(1)} collective-permute-done((bf16[64,5632]{1,0:T(8,128)(2,1)S(1)}, bf16[64,5632]{1,0:T(8,128)(2,1)S(1)}, u32[]{:S(2)}, u32[]{:S(2)}) %collective-permute-start.8) | collective-permute-done | bytes 720928 | tf_op jit(solution)/shard_map/ppermute | solution.py:241
  45.1 1.5 %collective-permute-start.9 = (bf16[64,5632]{1,0:T(8,128)(2,1)S(1)}, bf16[64,5632]{1,0:T(8,128)(2,1)S(1)}, u32[]{:S(2)}, u32[]{:S(2)}) collective-permute-start(bf16[64,5632]{1,0:T(8,128)(2,1)S(1)} %collective-permute-done.8.refs_4_), channel_id=1, source_target_pairs={{0,2},{1,3},{2,0},{3,1},{4,6},{5,7},{6,4},{7,5},{8,10},{9,11},{10,... | collective-permute-start | bytes 2162696 | tf_op jit(solution)/shard_map/ppermute | solution.py:241
  46.7 0.5 collective-permute-done.6.refs_3_
  47.2 0.0 collective-permute-done.1.x
  47.2 14.1 %collective-permute-done.5.piece0 = bf16[64,5632]{1,0:T(8,128)(2,1)S(1)} collective-permute-done((bf16[64,5632]{1,0:T(8,128)(2,1)S(1)}, bf16[64,5632]{1,0:T(8,128)(2,1)S(1)}, u32[]{:S(2)}, u32[]{:S(2)}) %collective-permute-start.5) | collective-permute-done | bytes 720928 | tf_op jit(solution)/shard_map/ppermute | solution.py:241
  61.3 1.5 %collective-permute-start.7 = (bf16[64,5632]{1,0:T(8,128)(2,1)S(1)}, bf16[64,5632]{1,0:T(8,128)(2,1)S(1)}, u32[]{:S(2)}, u32[]{:S(2)}) collective-permute-start(bf16[64,5632]{1,0:T(8,128)(2,1)S(1)} %collective-permute-done.5.piece0), channel_id=1, source_target_pairs={{0,2},{1,3},{2,0},{3,1},{4,6},{5,7},{6,4},{7,5},{8,10},{9,11},{10,... | collective-permute-start | bytes 2162696 | tf_op jit(solution)/shard_map/ppermute | solution.py:241
  62.8 0.2 collective-permute-done.9.refs_5_
  63.1 0.0 copy-start
  63.1 1.4 %copy-done = bf16[128,5760]{1,0:T(8,128)(2,1)S(1)} copy-done((bf16[128,5760]{1,0:T(8,128)(2,1)S(1)}, bf16[128,5760]{1,0:T(8,128)(2,1)}, u32[]{:S(2)}) %copy-start) | copy-done | bytes 1474584
  64.4 2.5 %project_early.1.early_ref = f32[3,128,256]{2,1,0:T(8,128)S(1)} custom-call(bf16[128,5760]{1,0:T(8,128)(2,1)S(1)} %copy-done, bf16[128,5760]{1,0:T(8,128)(2,1)S(1)} %collective-permute-done.other, bf16[128,5760]{1,0:T(8,128)(2,1)S(1)} %collective-permute-done.1.x, bf16[64,5632]{1,0:T(8,128)(2,1)S(1)} %copy-done.2, ...), custom_call_target="tpu_custom_call" | custom-call | tf_op jit(solution)/shard_map/project_early/pallas_call | solution.py:160
  66.9 0.0 copy-start.1
  66.9 5.5 %collective-permute-done.3.xc = bf16[128,5760]{1,0:T(8,128)(2,1)S(1)} collective-permute-done((bf16[128,5760]{1,0:T(8,128)(2,1)}, bf16[128,5760]{1,0:T(8,128)(2,1)S(1)}, u32[]{:S(2)}, u32[]{:S(2)}) %collective-permute-start.3) | collective-permute-done | bytes 1474592 | tf_op jit(solution)/shard_map/ppermute | solution.py:241
  72.4 1.4 %project_mid.1.mid_ref = f32[128,256]{1,0:T(8,128)S(1)} custom-call(bf16[128,5760]{1,0:T(8,128)(2,1)S(1)} %collective-permute-done.3.xc, bf16[64,5632]{1,0:T(8,128)(2,1)S(1)} %copy-done.2, bf16[64,5632]{1,0:T(8,128)(2,1)S(1)} %collective-permute-done.2.refs_1_, bf16[64,5632]{1,0:T(8,128)(2,1)S(1)} %collective-permute-done.4.refs_2_, ...), custom_call_target="tpu_custom_call" | custom-call | tf_op jit(solution)/shard_map/project_mid/pallas_call | solution.py:160
  73.8 5.6 %collective-permute-done.7.piece1 = bf16[64,5632]{1,0:T(8,128)(2,1)S(1)} collective-permute-done((bf16[64,5632]{1,0:T(8,128)(2,1)S(1)}, bf16[64,5632]{1,0:T(8,128)(2,1)S(1)}, u32[]{:S(2)}, u32[]{:S(2)}) %collective-permute-start.7) | collective-permute-done | bytes 720928 | tf_op jit(solution)/shard_map/ppermute | solution.py:241
  79.4 0.0 copy-done.1
  79.4 1.9 %project_last.1 = (f32[128,256]{1,0:T(8,128)S(1)}, f32[128,256]{1,0:T(8,128)S(1)}, f32[128,256]{1,0:T(8,128)S(1)}, f32[128,256]{1,0:T(8,128)S(1)}) custom-call(bf16[128,5760]{1,0:T(8,128)(2,1)S(1)} %copy-done.1, bf16[128,5760]{1,0:T(8,128)(2,1)S(1)} %collective-permute-done.other, bf16[128,5760]{1,0:T(8,128)(2,1)S(1)} %collective-permute-done.1.x, ...), custom_call_target="tpu_custom_call" | custom-call | tf_op jit(solution)/shard_map/project_last/pallas_call | solution.py:160
  81.2 0.0 copy-start.4
  81.2 0.6 copy-done.4
  81.9 0.0 copy-start.3
  81.9 0.0 collective-permute-start.10
  81.9 0.3 collective-permute-start.11
  82.2 1.5 %collective-permute-start.12 = (f32[128,256]{1,0:T(8,128)S(1)}, f32[128,256]{1,0:T(8,128)S(1)}, u32[]{:S(2)}, u32[]{:S(2)}) collective-permute-start(f32[128,256]{1,0:T(8,128)S(1)} %get-tuple-element.34), channel_id=1, source_target_pairs={{0,17},{1,16},{2,19},{3,18},{4,21},{5,20},{6,23},{7,22},{8,25},{9,... | collective-permute-start | bytes 393224 | tf_op jit(solution)/shard_map/ppermute | solution.py:241
  83.8 0.0 collective-permute-done.10.p1
  83.8 0.0 copy-start.5
  83.8 4.4 %collective-permute-done.11.p2 = f32[128,256]{1,0:T(8,128)S(1)} collective-permute-done((f32[128,256]{1,0:T(8,128)S(1)}, f32[128,256]{1,0:T(8,128)S(1)}, u32[]{:S(2)}, u32[]{:S(2)}) %collective-permute-start.11) | collective-permute-done | bytes 131104 | tf_op jit(solution)/shard_map/ppermute | solution.py:241
  88.2 0.0 copy-start.6
  88.2 2.0 %collective-permute-done.12.p3 = f32[128,256]{1,0:T(8,128)S(1)} collective-permute-done((f32[128,256]{1,0:T(8,128)S(1)}, f32[128,256]{1,0:T(8,128)S(1)}, u32[]{:S(2)}, u32[]{:S(2)}) %collective-permute-start.12) | collective-permute-done | bytes 131104 | tf_op jit(solution)/shard_map/ppermute | solution.py:241
  90.2 0.0 copy-start.7
  90.2 0.0 copy-done.5
  90.2 0.0 copy-done.6
  90.2 0.7 copy-done.7
  90.9 2.6 %gram.1 = bf16[8,16,16,128]{3,2,1,0:T(8,128)(2,1)} custom-call(f32[128,256]{1,0:T(8,128)} %copy-done.4, f32[128,256]{1,0:T(8,128)} %copy-done.5, f32[128,256]{1,0:T(8,128)} %copy-done.6, f32[128,256]{1,0:T(8,128)} %copy-done.7, s32[1,256]{1,0:T(1,128)} %bitcast.9), custom_call_target="tpu_custom_call" | custom-call | tf_op jit(solution)/shard_map/gram/pallas_call | solution.py:196
  93.5 20.5 %all_to_all.10.own = bf16[8,16,16,128]{3,2,1,0:T(8,128)(2,1)S(1)} all-to-all(bf16[8,16,16,128]{3,2,1,0:T(8,128)(2,1)} %gram.1), channel_id=1, replica_groups={{0,2,4,6,8,10,12,14},{1,3,5,7,9,11,13,15},{16,18,20,22,24,26,28,30},{17..., dimensions={0} | all-to-all | bytes 1048576 | tf_op jit(solution)/shard_map/all_to_all | solution.py:340
  114.0 0.0 collective-permute-start.13
  114.0 1.9 %collective-permute-done.13.other = bf16[8,16,16,128]{3,2,1,0:T(8,128)(2,1)S(1)} collective-permute-done((bf16[8,16,16,128]{3,2,1,0:T(8,128)(2,1)S(1)}, bf16[8,16,16,128]{3,2,1,0:T(8,128)(2,1)S(1)}, u32[]{:S(2)}, u32[]{:S(2)}) %collective-permute-start.13) | collective-permute-done | bytes 524320 | tf_op jit(solution)/shard_map/ppermute | solution.py:241
  115.9 0.0 copy-done.3
  116.0 0.7 precondition.1
  116.6 11.5 %all_to_all.11 = f32[16,8,256]{2,1,0:T(8,128)S(1)} all-to-all(f32[16,8,256]{2,1,0:T(8,128)S(1)} %precondition.1), channel_id=1, replica_groups=mesh['groups'=2,'dp'=16] {'dp'}, dimensions={0} | all-to-all | bytes 262144 | tf_op jit(solution)/shard_map/all_to_all | solution.py:347
  128.1 0.7 copy.8
Async XLA Ops:
  3.9 26.2 %collective-permute-start = (bf16[128,5760]{1,0:T(8,128)(2,1)}, bf16[128,5760]{1,0:T(8,128)(2,1)S(1)}, u32[]{:S(2)}, u32[]{:S(2)}) collective-permute-start(bf16[128,5760]{1,0:T(8,128)(2,1)} %get-tuple-element.23), channel_id=1, source_target_pairs={{0,1},{1,0},{2,3},{3,2},{4,5},{5,4},{6,7},{7,6},{8,9},{9,8},{10,11... | collective-permute-start | bytes 4423688 | tf_op jit(solution)/shard_map/ppermute | solution.py:241
  4.4 19.5 %collective-permute-start.2 = (bf16[64,5632]{1,0:T(8,128)(2,1)}, bf16[64,5632]{1,0:T(8,128)(2,1)S(1)}, u32[]{:S(2)}, u32[]{:S(2)}) collective-permute-start(bf16[64,5632]{1,0:T(8,128)(2,1)} %get-tuple-element.25.refs_0_), channel_id=1, source_target_pairs={{0,2},{1,3},{2,0},{3,1},{4,6},{5,7},{6,4},{7,5},{8,10},{9,11},{10,... | collective-permute-start | bytes 2162696 | tf_op jit(solution)/shard_map/ppermute | solution.py:241
  7.0 17.9 %copy-start.2 = (bf16[64,5632]{1,0:T(8,128)(2,1)S(1)}, bf16[64,5632]{1,0:T(8,128)(2,1)}, u32[]{:S(2)}) copy-start(bf16[64,5632]{1,0:T(8,128)(2,1)} %get-tuple-element.25.refs_0_) | copy-start | bytes 2162692
  7.0 40.2 %collective-permute-start.1 = (bf16[128,5760]{1,0:T(8,128)(2,1)}, bf16[128,5760]{1,0:T(8,128)(2,1)S(1)}, u32[]{:S(2)}, u32[]{:S(2)}) collective-permute-start(bf16[128,5760]{1,0:T(8,128)(2,1)} %get-tuple-element.20), channel_id=1, source_target_pairs={{0,16},{1,17},{2,18},{3,19},{4,20},{5,21},{6,22},{7,23},{8,24},{9,... | collective-permute-start | bytes 4423688 | tf_op jit(solution)/shard_map/ppermute | solution.py:241
  8.5 20.0 %collective-permute-start.4 = (bf16[64,5632]{1,0:T(8,128)(2,1)}, bf16[64,5632]{1,0:T(8,128)(2,1)S(1)}, u32[]{:S(2)}, u32[]{:S(2)}) collective-permute-start(bf16[64,5632]{1,0:T(8,128)(2,1)} %get-tuple-element.25.refs_0_), channel_id=1, source_target_pairs={{0,4},{1,5},{2,6},{3,7},{4,8},{5,9},{6,10},{7,11},{8,12},{9,13},{1... | collective-permute-start | bytes 2162696 | tf_op jit(solution)/shard_map/ppermute | solution.py:241
  24.0 48.5 %collective-permute-start.3 = (bf16[128,5760]{1,0:T(8,128)(2,1)}, bf16[128,5760]{1,0:T(8,128)(2,1)S(1)}, u32[]{:S(2)}, u32[]{:S(2)}) collective-permute-start(bf16[128,5760]{1,0:T(8,128)(2,1)} %get-tuple-element.26), channel_id=1, source_target_pairs={{0,17},{1,16},{2,19},{3,18},{4,21},{5,20},{6,23},{7,22},{8,25},{9,... | collective-permute-start | bytes 4423688 | tf_op jit(solution)/shard_map/ppermute | solution.py:241
  25.0 20.2 %collective-permute-start.8 = (bf16[64,5632]{1,0:T(8,128)(2,1)S(1)}, bf16[64,5632]{1,0:T(8,128)(2,1)S(1)}, u32[]{:S(2)}, u32[]{:S(2)}) collective-permute-start(bf16[64,5632]{1,0:T(8,128)(2,1)S(1)} %copy-done.2), channel_id=1, source_target_pairs={{0,12},{1,13},{2,14},{3,15},{4,0},{5,1},{6,2},{7,3},{8,4},{9,5},{1... | collective-permute-start | bytes 2162696 | tf_op jit(solution)/shard_map/ppermute | solution.py:241
  28.6 18.6 %collective-permute-start.6 = (bf16[64,5632]{1,0:T(8,128)(2,1)S(1)}, bf16[64,5632]{1,0:T(8,128)(2,1)S(1)}, u32[]{:S(2)}, u32[]{:S(2)}) collective-permute-start(bf16[64,5632]{1,0:T(8,128)(2,1)S(1)} %collective-permute-done.4.refs_2_), channel_id=1, source_target_pairs={{0,2},{1,3},{2,0},{3,1},{4,6},{5,7},{6,4},{7,5},{8,10},{9,11},{10,... | collective-permute-start | bytes 2162696 | tf_op jit(solution)/shard_map/ppermute | solution.py:241
  30.1 31.2 %collective-permute-start.5 = (bf16[64,5632]{1,0:T(8,128)(2,1)S(1)}, bf16[64,5632]{1,0:T(8,128)(2,1)S(1)}, u32[]{:S(2)}, u32[]{:S(2)}) collective-permute-start(bf16[64,5632]{1,0:T(8,128)(2,1)S(1)} %collective-permute-done.4.refs_2_), channel_id=1, source_target_pairs={{0,4},{1,5},{2,6},{3,7},{4,8},{5,9},{6,10},{7,11},{8,12},{9,13},{1... | collective-permute-start | bytes 2162696 | tf_op jit(solution)/shard_map/ppermute | solution.py:241
  45.1 17.9 %collective-permute-start.9 = (bf16[64,5632]{1,0:T(8,128)(2,1)S(1)}, bf16[64,5632]{1,0:T(8,128)(2,1)S(1)}, u32[]{:S(2)}, u32[]{:S(2)}) collective-permute-start(bf16[64,5632]{1,0:T(8,128)(2,1)S(1)} %collective-permute-done.8.refs_4_), channel_id=1, source_target_pairs={{0,2},{1,3},{2,0},{3,1},{4,6},{5,7},{6,4},{7,5},{8,10},{9,11},{10,... | collective-permute-start | bytes 2162696 | tf_op jit(solution)/shard_map/ppermute | solution.py:241
  61.3 18.0 %collective-permute-start.7 = (bf16[64,5632]{1,0:T(8,128)(2,1)S(1)}, bf16[64,5632]{1,0:T(8,128)(2,1)S(1)}, u32[]{:S(2)}, u32[]{:S(2)}) collective-permute-start(bf16[64,5632]{1,0:T(8,128)(2,1)S(1)} %collective-permute-done.5.piece0), channel_id=1, source_target_pairs={{0,2},{1,3},{2,0},{3,1},{4,6},{5,7},{6,4},{7,5},{8,10},{9,11},{10,... | collective-permute-start | bytes 2162696 | tf_op jit(solution)/shard_map/ppermute | solution.py:241
  63.1 1.4 %copy-start = (bf16[128,5760]{1,0:T(8,128)(2,1)S(1)}, bf16[128,5760]{1,0:T(8,128)(2,1)}, u32[]{:S(2)}) copy-start(bf16[128,5760]{1,0:T(8,128)(2,1)} %get-tuple-element.22.own) | copy-start | bytes 4423684
  66.9 12.4 %copy-start.1 = (bf16[128,5760]{1,0:T(8,128)(2,1)S(1)}, bf16[128,5760]{1,0:T(8,128)(2,1)}, u32[]{:S(2)}) copy-start(bf16[128,5760]{1,0:T(8,128)(2,1)} %get-tuple-element.22.own) | copy-start | bytes 4423684
  81.2 0.7 copy-start.4
  81.9 34.1 %copy-start.3 = (bf16[4096,256]{1,0:T(8,128)(2,1)S(1)}, bf16[4096,256]{1,0:T(8,128)(2,1)}, u32[]{:S(2)}) copy-start(bf16[4096,256]{1,0:T(8,128)(2,1)} %fisher.1) | copy-start | bytes 6291460
  81.9 1.9 %collective-permute-start.10 = (f32[128,256]{1,0:T(8,128)S(1)}, f32[128,256]{1,0:T(8,128)S(1)}, u32[]{:S(2)}, u32[]{:S(2)}) collective-permute-start(f32[128,256]{1,0:T(8,128)S(1)} %get-tuple-element.32), channel_id=1, source_target_pairs={{0,1},{1,0},{2,3},{3,2},{4,5},{5,4},{6,7},{7,6},{8,9},{9,8},{10,11... | collective-permute-start | bytes 393224 | tf_op jit(solution)/shard_map/ppermute | solution.py:241
  81.9 6.3 %collective-permute-start.11 = (f32[128,256]{1,0:T(8,128)S(1)}, f32[128,256]{1,0:T(8,128)S(1)}, u32[]{:S(2)}, u32[]{:S(2)}) collective-permute-start(f32[128,256]{1,0:T(8,128)S(1)} %get-tuple-element.33), channel_id=1, source_target_pairs={{0,16},{1,17},{2,18},{3,19},{4,20},{5,21},{6,22},{7,23},{8,24},{9,... | collective-permute-start | bytes 393224 | tf_op jit(solution)/shard_map/ppermute | solution.py:241
  82.2 8.0 %collective-permute-start.12 = (f32[128,256]{1,0:T(8,128)S(1)}, f32[128,256]{1,0:T(8,128)S(1)}, u32[]{:S(2)}, u32[]{:S(2)}) collective-permute-start(f32[128,256]{1,0:T(8,128)S(1)} %get-tuple-element.34), channel_id=1, source_target_pairs={{0,17},{1,16},{2,19},{3,18},{4,21},{5,20},{6,23},{7,22},{8,25},{9,... | collective-permute-start | bytes 393224 | tf_op jit(solution)/shard_map/ppermute | solution.py:241
  83.8 6.5 %copy-start.5 = (f32[128,256]{1,0:T(8,128)}, f32[128,256]{1,0:T(8,128)S(1)}, u32[]{:S(2)}) copy-start(f32[128,256]{1,0:T(8,128)S(1)} %collective-permute-done.10.p1) | copy-start | bytes 393220
  88.2 2.0 %copy-start.6 = (f32[128,256]{1,0:T(8,128)}, f32[128,256]{1,0:T(8,128)S(1)}, u32[]{:S(2)}) copy-start(f32[128,256]{1,0:T(8,128)S(1)} %collective-permute-done.11.p2) | copy-start | bytes 393220
  90.2 0.7 copy-start.7
  114.0 1.9 %collective-permute-start.13 = (bf16[8,16,16,128]{3,2,1,0:T(8,128)(2,1)S(1)}, bf16[8,16,16,128]{3,2,1,0:T(8,128)(2,1)S(1)}, u32[]{:S(2)}, u32[]{:S(2)}) collective-permute-start(bf16[8,16,16,128]{3,2,1,0:T(8,128)(2,1)S(1)} %all_to_all.10.own), channel_id=1, source_target_pairs={{0,1},{1,0},{2,3},{3,2},{4,5},{5,4},{6,7},{7,6},{8,9},{9,8},{10,11... | collective-permute-start | bytes 1572872 | tf_op jit(solution)/shard_map/ppermute | solution.py:241

commit v4 on v3

--- a/solution.py
+++ b/solution.py
@@ -92,10 +92,11 @@
         refs[-1][:, k * LANES : (k + 1) * LANES] = got
 
 
-def last_kernel(sub, width, ids, sizes, own, other, x, xc, piece0, piece1, early_ref, mid_ref, *outs):
+def last_kernel(sub, width, ids, sizes, own, other, x, xc, early_ref, mid_ref, *refs):
+    pieces, outs = refs[:-4], refs[-4:]
     experts = [piece_of(at, sizes) for at in ids]
     rows = [own[...], other[...], x[...], xc[...]]
-    for b, slots in enumerate(picks(rows, (piece0, piece1), experts, width, sub)):
+    for b, slots in enumerate(picks(rows, pieces, experts, width, sub)):
         for k, got in enumerate(slots):
             lanes = slice(k * LANES, (k + 1) * LANES)
             outs[b][:, lanes] = (early_ref[b, :, lanes] if b < 3 else mid_ref[:, lanes]) + got
@@ -167,27 +168,29 @@
     )(*operands)
 
 
-def gram_kernel(p0, p1, p2, p3, routes_ref, out_ref, flat):
+def gram_kernel(p0, p1, p2, p3, routes_ref, out_ref):
     total = (p0[...] + p1[...]) + (p2[...] + p3[...])
     first, second = total[:, :LANES], total[:, LANES:]
     left = jnp.concatenate([jnp.transpose(first)[:PROJ], jnp.transpose(second)[:PROJ]], axis=1)
     right = jnp.concatenate([first, second], axis=0)
-    named = routes_ref[...]
-    rows = jnp.concatenate([jnp.where(named == e, left, 0.0) for e in range(EXPERTS)], axis=0)
-    grams = lax.dot_general(
-        rows,
-        right,
-        (((1,), (0,)), ((), ())),
-        precision=lax.Precision.HIGHEST,
-        preferred_element_type=jnp.float32,
-    )
+    left_high, right_high = left.astype(jnp.bfloat16).astype(jnp.float32), right.astype(jnp.bfloat16)
+    left_low, right_low = left - left_high, (right - right_high.astype(jnp.float32)).astype(jnp.bfloat16)
+    expert = lax.broadcasted_iota(jnp.int32, (EXPERTS, 2 * TOK), 0)
+    chosen = jnp.where(jnp.broadcast_to(routes_ref[...], expert.shape) == expert, 1.0, 0.0)
+
+    def masked(x):
+        rows = [x[p : p + 1] * chosen for p in range(PROJ)]
+        return jnp.concatenate(rows, axis=0).astype(jnp.bfloat16)
+
+    high, low = masked(left_high), masked(left_low)
+    grams = jnp.dot(high, right_high, preferred_element_type=jnp.float32)
+    grams += jnp.dot(high, right_low, preferred_element_type=jnp.float32)
+    grams += jnp.dot(low, right_high, preferred_element_type=jnp.float32)
     grams = grams * (TOK**-0.5)
-    low = lax.broadcasted_iota(jnp.int32, (PROJ // 2, LANES), 1) < PROJ
-    for e in range(EXPERTS):
-        top = grams[e * PROJ : e * PROJ + PROJ // 2]
-        bottom = grams[e * PROJ + PROJ // 2 : (e + 1) * PROJ]
-        flat[:, e, :] = jnp.where(low, pltpu.roll(top, PROJ, 1), bottom)
-    mine = flat[...].reshape(PROJ // 4, 2 * EXPERTS, LANES).astype(jnp.bfloat16)
+    rows = PROJ // 2 * EXPERTS
+    first = lax.broadcasted_iota(jnp.int32, (rows, LANES), 1) < PROJ
+    mine = jnp.where(first, pltpu.roll(grams[:rows], PROJ, 1), grams[rows:])
+    mine = mine.reshape(PROJ // 4, 2 * EXPERTS, LANES).astype(jnp.bfloat16)
     for j in range(out_ref.shape[0]):
         out_ref[j] = mine
 
@@ -196,7 +199,6 @@
     return pl.pallas_call(
         gram_kernel,
         out_shape=jax.ShapeDtypeStruct((copies, PROJ // 4, 2 * EXPERTS, LANES), jnp.bfloat16),
-        scratch_shapes=[pltpu.VMEM((PROJ // 2, EXPERTS, LANES), jnp.float32)],
         compiler_params=pltpu.CompilerParams(vmem_limit_bytes=2 * VMEM),
         name="gram",
     )(*parts, routes)
@@ -220,9 +222,11 @@
             )
             lhs = rows[:, h].reshape(n * EXPERTS, LANES).astype(jnp.bfloat16)
             total += jnp.dot(lhs, table, preferred_element_type=jnp.float32)
+    width = fisher.shape[1]
     for j in range(n // 2):
-        out_ref[2 * j + core] = total[j * EXPERTS : (j + 1) * EXPERTS]
-        out_ref[2 * j + 1 - core] = total[(n // 2 + j) * EXPERTS : (n // 2 + j + 1) * EXPERTS]
+        for rows, place in ((j, 2 * j + core), (n // 2 + j, 2 * j + 1 - core)):
+            at = pl.multiple_of(place * width, LANES)
+            out_ref[:, pl.ds(at, width)] = total[rows * EXPERTS : (rows + 1) * EXPERTS]
 
 
 def shards(features, grads, routes, proj_in, proj_out, fisher_inverse):
@@ -307,9 +311,12 @@
             if across:
                 if i == 1:
                     block = after(block, facing)
+                block = facing if i == 0 else block
+                if 0 < i < len(blocks) - 1:
+                    block = move(block, to_y)
                 if i == len(blocks) - 1:
-                    block = after(block, x, pieces[3])
-                block = move(block, to_y) if i else facing
+                    near = move(after(block, x, pieces[3])[: PROJ // 2], to_y)
+                    block = (near, move(pieces[3][PROJ // 2 :], to_z))
             pieces.append(block)
             where.append((ids[i] % z_size, across))
 
@@ -331,7 +338,7 @@
         functools.partial(last_kernel, sub, quarter_out, where[-2:], sizes),
         "project_last",
         [jax.ShapeDtypeStruct((TOK, 2 * LANES), f32)] * 4,
-        [own, other, x, xc] + pieces[-2:] + [early, mid],
+        [own, other, x, xc, early, mid] + jax.tree.leaves(pieces[-2:]),
     )
     sums = [partial[0], move(partial[1], to_core), move(partial[2], to_x), move(partial[3], to_x_core)]
     mine = gram(sums, routes.reshape(1, -1), chips)
@@ -341,11 +348,11 @@
     columns = local(
         fisher_kernel,
         "precondition",
-        jax.ShapeDtypeStruct((n, EXPERTS, fisher_inverse.shape[1]), f32),
+        jax.ShapeDtypeStruct((EXPERTS, PROJ * PROJ), f32),
         [grams, move(grams, to_core), fisher_inverse],
     )
-    result = lax.all_to_all(columns, "dp", split_axis=0, concat_axis=0, tiled=True)
-    return jnp.transpose(result, (1, 0, 2)).reshape(1, EXPERTS, PROJ * PROJ)
+    result = lax.all_to_all(columns, "dp", split_axis=1, concat_axis=1, tiled=True)
+    return result.reshape(1, EXPERTS, PROJ * PROJ)
 
 
 def solution(mesh):

time: 129 us -> 123 us (0.953)
  waiting for transfers between devices: 59.6 us -> 53.2 us
    ppermute x14 -> x15, waiting for transfers between devices: 59.6 us -> 53.2 us  [move(): return lax.ppermute(x, AXES, pairs)]
    ppermute x14 -> x15, starting transfers between devices: 17.2 us -> 17.6 us  [move(): return lax.ppermute(x, AXES, pairs)]
  transfers between devices with their start and end apart: 14 -> 15, of which waited for: 10 -> 8; matrix products, arithmetic and copies ran while one was open for 0% -> 0% of each run, Pallas kernels for 6% -> 6%
where the time goes in v4:
time: 123 us; the launch traced here: 122 us
  waiting for transfers between devices  53.2 us (43%)
  blocking collectives  31.8 us (26%)
  starting transfers between devices  17.6 us (14%)
  Pallas kernels  16.3 us (13%)
  local copies, waits for them, and re-layouts  3.4 us (3%)
    ppermute x15, waiting for transfers between devices, move(): return lax.ppermute(x, AXES, pairs)  53.2 us
    all_to_all x1, blocking collectives, shards(): lax.all_to_all(mine, 'dp', split_axis=0, concat_axis=0, axis_index_groups...  20.3 us
    ppermute x15, starting transfers between devices, move(): return lax.ppermute(x, AXES, pairs)  17.6 us
    all_to_all x1, blocking collectives, shards(): lax.all_to_all(columns, 'dp', split_axis=1, concat_axis=1, tiled=True)  11.5 us
    pallas_call x2, Pallas kernels, pack(): pl.pallas_call(functools.partial(pack_kernel, [[b[1:] for b in out] for o...  7.52 us
    pallas_call x4, Pallas kernels, local(): pl.pallas_call(kernel, in_specs=[vmem] * len(operands), out_specs=jax.tre...  6.41 us
    unnamed x17, local copies, waits for them, and re-layouts  3.35 us
  transfers between devices with their start and end apart: 15, of which 8 were waited for; matrix products, arithmetic and copies ran while one was open for 0% of the time, Pallas kernels for 6%

profile of v4, /device:TPU:0, one launch (start us, length us, event | category | flops | bytes accessed | tf_op | source)
XLA Modules:
  0.0 122.2 jit_solution(11922839893377921340)
XLA Ops:
  0.0 3.9 %pack_first.1 = (bf16[64,5632]{1,0:T(8,128)(2,1)}, bf16[128,5760]{1,0:T(8,128)(2,1)}, bf16[128,5760]{1,0:T(8,128)(2,1)}) custom-call(s32[2,128]{1,0:T(2,128)} %bitcast.7, bf16[64,8192]{1,0:T(8,128)(2,1)} %refs_0_.2, bf16[64,3072]{1,0:T(8,128)(2,1)} %refs_1_.2, bf16[128,16384]{1,0:T(8,128)(2,1)} %refs_2_.3, bf16[128,6144]{1,0:T(8,128)(2,1)} %refs_3_.3, ...), custom_call_target="tpu_custom_call" | custom-call | tf_op jit(solution)/shard_map/pack_first/pallas_call | solution.py:147
  3.9 0.5 collective-permute-start
  4.4 2.6 %collective-permute-start.2 = (bf16[64,5632]{1,0:T(8,128)(2,1)}, bf16[64,5632]{1,0:T(8,128)(2,1)S(1)}, u32[]{:S(2)}, u32[]{:S(2)}) collective-permute-start(bf16[64,5632]{1,0:T(8,128)(2,1)} %get-tuple-element.25.refs_0_), channel_id=1, source_target_pairs={{0,2},{1,3},{2,0},{3,1},{4,6},{5,7},{6,4},{7,5},{8,10},{9,11},{10,... | collective-permute-start | bytes 2162696 | tf_op jit(solution)/shard_map/ppermute | solution.py:245
  7.0 0.0 copy-start.2
  7.0 1.5 %collective-permute-start.1 = (bf16[128,5760]{1,0:T(8,128)(2,1)}, bf16[128,5760]{1,0:T(8,128)(2,1)S(1)}, u32[]{:S(2)}, u32[]{:S(2)}) collective-permute-start(bf16[128,5760]{1,0:T(8,128)(2,1)} %get-tuple-element.20), channel_id=1, source_target_pairs={{0,16},{1,17},{2,18},{3,19},{4,20},{5,21},{6,22},{7,23},{8,24},{9,... | collective-permute-start | bytes 4423688 | tf_op jit(solution)/shard_map/ppermute | solution.py:245
  8.5 1.6 %collective-permute-start.4 = (bf16[64,5632]{1,0:T(8,128)(2,1)}, bf16[64,5632]{1,0:T(8,128)(2,1)S(1)}, u32[]{:S(2)}, u32[]{:S(2)}) collective-permute-start(bf16[64,5632]{1,0:T(8,128)(2,1)} %get-tuple-element.25.refs_0_), channel_id=1, source_target_pairs={{0,4},{1,5},{2,6},{3,7},{4,8},{5,9},{6,10},{7,11},{8,12},{9,13},{1... | collective-permute-start | bytes 2162696 | tf_op jit(solution)/shard_map/ppermute | solution.py:245
  10.1 3.6 %pack_second.1 = (bf16[128,5760]{1,0:T(8,128)(2,1)}, bf16[128,5760]{1,0:T(8,128)(2,1)}) custom-call(s32[2,128]{1,0:T(2,128)} %bitcast.8, bf16[128,16384]{1,0:T(8,128)(2,1)} %refs_2_.3, bf16[128,6144]{1,0:T(8,128)(2,1)} %refs_3_.3, bf16[128,16384]{1,0:T(8,128)(2,1)} %refs_2_.3, bf16[128,6144]{1,0:T(8,128)(2,1)} %refs_3_.3), custom_call_target="tpu_custom_call" | custom-call | tf_op jit(solution)/shard_map/pack_second/pallas_call | solution.py:147
  13.7 10.2 %collective-permute-done.2.refs_1_ = bf16[64,5632]{1,0:T(8,128)(2,1)S(1)} collective-permute-done((bf16[64,5632]{1,0:T(8,128)(2,1)}, bf16[64,5632]{1,0:T(8,128)(2,1)S(1)}, u32[]{:S(2)}, u32[]{:S(2)}) %collective-permute-start.2) | collective-permute-done | bytes 720928 | tf_op jit(solution)/shard_map/ppermute | solution.py:245
  24.0 1.0 collective-permute-start.3
  25.0 0.0 copy-done.2
  25.0 3.6 %collective-permute-start.6 = (bf16[64,5632]{1,0:T(8,128)(2,1)S(1)}, bf16[64,5632]{1,0:T(8,128)(2,1)S(1)}, u32[]{:S(2)}, u32[]{:S(2)}) collective-permute-start(bf16[64,5632]{1,0:T(8,128)(2,1)S(1)} %copy-done.2), channel_id=1, source_target_pairs={{0,12},{1,13},{2,14},{3,15},{4,0},{5,1},{6,2},{7,3},{8,4},{9,5},{1... | collective-permute-start | bytes 2162696 | tf_op jit(solution)/shard_map/ppermute | solution.py:245
  28.6 0.0 collective-permute-done.4.refs_2_
  28.6 1.5 %collective-permute-start.5 = (bf16[64,5632]{1,0:T(8,128)(2,1)S(1)}, bf16[64,5632]{1,0:T(8,128)(2,1)S(1)}, u32[]{:S(2)}, u32[]{:S(2)}) collective-permute-start(bf16[64,5632]{1,0:T(8,128)(2,1)S(1)} %collective-permute-done.4.refs_2_), channel_id=1, source_target_pairs={{0,2},{1,3},{2,0},{3,1},{4,6},{5,7},{6,4},{7,5},{8,10},{9,11},{10,... | collective-permute-start | bytes 2162696 | tf_op jit(solution)/shard_map/ppermute | solution.py:245
  30.1 0.0 collective-permute-done.other
  30.1 0.0 collective-permute-start.8
  30.1 15.0 %collective-permute-done.6.refs_4_ = bf16[64,5632]{1,0:T(8,128)(2,1)S(1)} collective-permute-done((bf16[64,5632]{1,0:T(8,128)(2,1)S(1)}, bf16[64,5632]{1,0:T(8,128)(2,1)S(1)}, u32[]{:S(2)}, u32[]{:S(2)}) %collective-permute-start.6) | collective-permute-done | bytes 720928 | tf_op jit(solution)/shard_map/ppermute | solution.py:245
  45.1 1.5 %collective-permute-start.7 = (bf16[64,5632]{1,0:T(8,128)(2,1)S(1)}, bf16[64,5632]{1,0:T(8,128)(2,1)S(1)}, u32[]{:S(2)}, u32[]{:S(2)}) collective-permute-start(bf16[64,5632]{1,0:T(8,128)(2,1)S(1)} %collective-permute-done.6.refs_4_), channel_id=1, source_target_pairs={{0,2},{1,3},{2,0},{3,1},{4,6},{5,7},{6,4},{7,5},{8,10},{9,11},{10,... | collective-permute-start | bytes 2162696 | tf_op jit(solution)/shard_map/ppermute | solution.py:245
  46.7 0.5 collective-permute-done.5.refs_3_
  47.2 0.1 collective-permute-start.10
  47.3 0.0 collective-permute-done.1.x
  47.3 14.2 %collective-permute-done.8.refs_0_ = bf16[64,5632]{1,0:T(8,128)(2,1)S(1)} collective-permute-done((bf16[64,5632]{1,0:T(8,128)(2,1)S(1)}, bf16[64,5632]{1,0:T(8,128)(2,1)S(1)}, u32[]{:S(2)}, u32[]{:S(2)}) %collective-permute-start.8) | collective-permute-done | bytes 720928 | tf_op jit(solution)/shard_map/ppermute | solution.py:245
  61.5 1.6 %collective-permute-start.9 = (bf16[32,5632]{1,0:T(8,128)(2,1)S(1)}, bf16[32,5632]{1,0:T(8,128)(2,1)S(1)}, u32[]{:S(2)}, u32[]{:S(2)}) collective-permute-start(bf16[32,5632]{1,0:T(8,128)(2,1)S(1)} %slice.6), channel_id=1, source_target_pairs={{0,2},{1,3},{2,0},{3,1},{4,6},{5,7},{6,4},{7,5},{8,10},{9,11},{10,... | collective-permute-start | bytes 1081352 | tf_op jit(solution)/shard_map/ppermute | solution.py:245
  63.1 0.0 collective-permute-done.7.refs_5_
  63.1 0.0 copy-start
  63.1 1.4 %copy-done = bf16[128,5760]{1,0:T(8,128)(2,1)S(1)} copy-done((bf16[128,5760]{1,0:T(8,128)(2,1)S(1)}, bf16[128,5760]{1,0:T(8,128)(2,1)}, u32[]{:S(2)}) %copy-start) | copy-done | bytes 1474584
  64.4 2.5 %project_early.1.early_ref = f32[3,128,256]{2,1,0:T(8,128)S(1)} custom-call(bf16[128,5760]{1,0:T(8,128)(2,1)S(1)} %copy-done, bf16[128,5760]{1,0:T(8,128)(2,1)S(1)} %collective-permute-done.other, bf16[128,5760]{1,0:T(8,128)(2,1)S(1)} %collective-permute-done.1.x, bf16[64,5632]{1,0:T(8,128)(2,1)S(1)} %copy-done.2, ...), custom_call_target="tpu_custom_call" | custom-call | tf_op jit(solution)/shard_map/project_early/pallas_call | solution.py:161
  66.9 0.0 copy-start.1
  66.9 5.5 %collective-permute-done.3.xc = bf16[128,5760]{1,0:T(8,128)(2,1)S(1)} collective-permute-done((bf16[128,5760]{1,0:T(8,128)(2,1)}, bf16[128,5760]{1,0:T(8,128)(2,1)S(1)}, u32[]{:S(2)}, u32[]{:S(2)}) %collective-permute-start.3) | collective-permute-done | bytes 1474592 | tf_op jit(solution)/shard_map/ppermute | solution.py:245
  72.4 1.4 %project_mid.1.mid_ref = f32[128,256]{1,0:T(8,128)S(1)} custom-call(bf16[128,5760]{1,0:T(8,128)(2,1)S(1)} %collective-permute-done.3.xc, bf16[64,5632]{1,0:T(8,128)(2,1)S(1)} %copy-done.2, bf16[64,5632]{1,0:T(8,128)(2,1)S(1)} %collective-permute-done.2.refs_1_, bf16[64,5632]{1,0:T(8,128)(2,1)S(1)} %collective-permute-done.4.refs_2_, ...), custom_call_target="tpu_custom_call" | custom-call | tf_op jit(solution)/shard_map/project_mid/pallas_call | solution.py:161
  73.8 0.0 collective-permute-done.10.refs_2_
  73.8 0.0 collective-permute-done.9.refs_1_
  73.8 0.0 copy-done.1
  73.8 1.9 %project_last.1 = (f32[128,256]{1,0:T(8,128)S(1)}, f32[128,256]{1,0:T(8,128)S(1)}, f32[128,256]{1,0:T(8,128)S(1)}, f32[128,256]{1,0:T(8,128)S(1)}) custom-call(bf16[128,5760]{1,0:T(8,128)(2,1)S(1)} %copy-done.1, bf16[128,5760]{1,0:T(8,128)(2,1)S(1)} %collective-permute-done.other, bf16[128,5760]{1,0:T(8,128)(2,1)S(1)} %collective-permute-done.1.x, ...), custom_call_target="tpu_custom_call" | custom-call | tf_op jit(solution)/shard_map/project_last/pallas_call | solution.py:161
  75.7 0.0 copy-start.4
  75.7 0.6 copy-done.4
  76.4 0.0 copy-start.3
  76.4 0.6 collective-permute-start.11
  77.0 1.5 %collective-permute-start.12 = (f32[128,256]{1,0:T(8,128)S(1)}, f32[128,256]{1,0:T(8,128)S(1)}, u32[]{:S(2)}, u32[]{:S(2)}) collective-permute-start(f32[128,256]{1,0:T(8,128)S(1)} %get-tuple-element.33), channel_id=1, source_target_pairs={{0,16},{1,17},{2,18},{3,19},{4,20},{5,21},{6,22},{7,23},{8,24},{9,... | collective-permute-start | bytes 393224 | tf_op jit(solution)/shard_map/ppermute | solution.py:245
  78.5 0.0 collective-permute-start.13
  78.5 0.0 collective-permute-done.11.p1
  78.5 0.0 copy-start.5
  78.5 4.8 %collective-permute-done.12.p2 = f32[128,256]{1,0:T(8,128)S(1)} collective-permute-done((f32[128,256]{1,0:T(8,128)S(1)}, f32[128,256]{1,0:T(8,128)S(1)}, u32[]{:S(2)}, u32[]{:S(2)}) %collective-permute-start.12) | collective-permute-done | bytes 131104 | tf_op jit(solution)/shard_map/ppermute | solution.py:245
  83.3 0.0 copy-start.6
  83.3 0.9 collective-permute-done.13.p3
  84.2 0.0 copy-start.7
  84.2 0.0 copy-done.5
  84.2 0.0 copy-done.6
  84.3 0.7 copy-done.7
  84.9 2.3 %gram.1 = bf16[8,16,16,128]{3,2,1,0:T(8,128)(2,1)} custom-call(f32[128,256]{1,0:T(8,128)} %copy-done.4, f32[128,256]{1,0:T(8,128)} %copy-done.5, f32[128,256]{1,0:T(8,128)} %copy-done.6, f32[128,256]{1,0:T(8,128)} %copy-done.7, s32[1,256]{1,0:T(1,128)} %bitcast.9), custom_call_target="tpu_custom_call" | custom-call | tf_op jit(solution)/shard_map/gram/pallas_call | solution.py:199
  87.2 20.3 %all_to_all.14.own = bf16[8,16,16,128]{3,2,1,0:T(8,128)(2,1)S(1)} all-to-all(bf16[8,16,16,128]{3,2,1,0:T(8,128)(2,1)} %gram.1), channel_id=1, replica_groups={{0,2,4,6,8,10,12,14},{1,3,5,7,9,11,13,15},{16,18,20,22,24,26,28,30},{17..., dimensions={0} | all-to-all | bytes 1048576 | tf_op jit(solution)/shard_map/all_to_all | solution.py:347
  107.5 0.0 collective-permute-start.14
  107.5 1.9 %collective-permute-done.14.other = bf16[8,16,16,128]{3,2,1,0:T(8,128)(2,1)S(1)} collective-permute-done((bf16[8,16,16,128]{3,2,1,0:T(8,128)(2,1)S(1)}, bf16[8,16,16,128]{3,2,1,0:T(8,128)(2,1)S(1)}, u32[]{:S(2)}, u32[]{:S(2)}) %collective-permute-start.14) | collective-permute-done | bytes 524320 | tf_op jit(solution)/shard_map/ppermute | solution.py:245
  109.4 0.0 copy-done.3
  109.4 0.7 precondition.1
  110.1 11.5 %all_to_all.15 = f32[8,16,256]{2,0,1:T(8,128)S(1)} all-to-all(f32[8,16,256]{2,0,1:T(8,128)S(1)} %bitcast.5), channel_id=1, replica_groups=mesh['groups'=2,'dp'=16] {'dp'}, dimensions={1} | all-to-all | bytes 262144 | tf_op jit(solution)/shard_map/all_to_all | solution.py:354
  121.6 0.7 copy.8
  (2 shorter events, 0.0 us)
Async XLA Ops:
  3.9 26.2 %collective-permute-start = (bf16[128,5760]{1,0:T(8,128)(2,1)}, bf16[128,5760]{1,0:T(8,128)(2,1)S(1)}, u32[]{:S(2)}, u32[]{:S(2)}) collective-permute-start(bf16[128,5760]{1,0:T(8,128)(2,1)} %get-tuple-element.23), channel_id=1, source_target_pairs={{0,1},{1,0},{2,3},{3,2},{4,5},{5,4},{6,7},{7,6},{8,9},{9,8},{10,11... | collective-permute-start | bytes 4423688 | tf_op jit(solution)/shard_map/ppermute | solution.py:245
  4.4 19.5 %collective-permute-start.2 = (bf16[64,5632]{1,0:T(8,128)(2,1)}, bf16[64,5632]{1,0:T(8,128)(2,1)S(1)}, u32[]{:S(2)}, u32[]{:S(2)}) collective-permute-start(bf16[64,5632]{1,0:T(8,128)(2,1)} %get-tuple-element.25.refs_0_), channel_id=1, source_target_pairs={{0,2},{1,3},{2,0},{3,1},{4,6},{5,7},{6,4},{7,5},{8,10},{9,11},{10,... | collective-permute-start | bytes 2162696 | tf_op jit(solution)/shard_map/ppermute | solution.py:245
  7.0 17.9 %copy-start.2 = (bf16[64,5632]{1,0:T(8,128)(2,1)S(1)}, bf16[64,5632]{1,0:T(8,128)(2,1)}, u32[]{:S(2)}) copy-start(bf16[64,5632]{1,0:T(8,128)(2,1)} %get-tuple-element.25.refs_0_) | copy-start | bytes 2162692
  7.0 40.3 %collective-permute-start.1 = (bf16[128,5760]{1,0:T(8,128)(2,1)}, bf16[128,5760]{1,0:T(8,128)(2,1)S(1)}, u32[]{:S(2)}, u32[]{:S(2)}) collective-permute-start(bf16[128,5760]{1,0:T(8,128)(2,1)} %get-tuple-element.20), channel_id=1, source_target_pairs={{0,16},{1,17},{2,18},{3,19},{4,20},{5,21},{6,22},{7,23},{8,24},{9,... | collective-permute-start | bytes 4423688 | tf_op jit(solution)/shard_map/ppermute | solution.py:245
  8.5 20.0 %collective-permute-start.4 = (bf16[64,5632]{1,0:T(8,128)(2,1)}, bf16[64,5632]{1,0:T(8,128)(2,1)S(1)}, u32[]{:S(2)}, u32[]{:S(2)}) collective-permute-start(bf16[64,5632]{1,0:T(8,128)(2,1)} %get-tuple-element.25.refs_0_), channel_id=1, source_target_pairs={{0,4},{1,5},{2,6},{3,7},{4,8},{5,9},{6,10},{7,11},{8,12},{9,13},{1... | collective-permute-start | bytes 2162696 | tf_op jit(solution)/shard_map/ppermute | solution.py:245
  24.0 48.5 %collective-permute-start.3 = (bf16[128,5760]{1,0:T(8,128)(2,1)}, bf16[128,5760]{1,0:T(8,128)(2,1)S(1)}, u32[]{:S(2)}, u32[]{:S(2)}) collective-permute-start(bf16[128,5760]{1,0:T(8,128)(2,1)} %get-tuple-element.26), channel_id=1, source_target_pairs={{0,17},{1,16},{2,19},{3,18},{4,21},{5,20},{6,23},{7,22},{8,25},{9,... | collective-permute-start | bytes 4423688 | tf_op jit(solution)/shard_map/ppermute | solution.py:245
  25.0 20.2 %collective-permute-start.6 = (bf16[64,5632]{1,0:T(8,128)(2,1)S(1)}, bf16[64,5632]{1,0:T(8,128)(2,1)S(1)}, u32[]{:S(2)}, u32[]{:S(2)}) collective-permute-start(bf16[64,5632]{1,0:T(8,128)(2,1)S(1)} %copy-done.2), channel_id=1, source_target_pairs={{0,12},{1,13},{2,14},{3,15},{4,0},{5,1},{6,2},{7,3},{8,4},{9,5},{1... | collective-permute-start | bytes 2162696 | tf_op jit(solution)/shard_map/ppermute | solution.py:245
  28.6 18.6 %collective-permute-start.5 = (bf16[64,5632]{1,0:T(8,128)(2,1)S(1)}, bf16[64,5632]{1,0:T(8,128)(2,1)S(1)}, u32[]{:S(2)}, u32[]{:S(2)}) collective-permute-start(bf16[64,5632]{1,0:T(8,128)(2,1)S(1)} %collective-permute-done.4.refs_2_), channel_id=1, source_target_pairs={{0,2},{1,3},{2,0},{3,1},{4,6},{5,7},{6,4},{7,5},{8,10},{9,11},{10,... | collective-permute-start | bytes 2162696 | tf_op jit(solution)/shard_map/ppermute | solution.py:245
  30.1 31.4 %collective-permute-start.8 = (bf16[64,5632]{1,0:T(8,128)(2,1)S(1)}, bf16[64,5632]{1,0:T(8,128)(2,1)S(1)}, u32[]{:S(2)}, u32[]{:S(2)}) collective-permute-start(bf16[64,5632]{1,0:T(8,128)(2,1)S(1)} %collective-permute-done.4.refs_2_), channel_id=1, source_target_pairs={{0,4},{1,5},{2,6},{3,7},{4,8},{5,9},{6,10},{7,11},{8,12},{9,13},{1... | collective-permute-start | bytes 2162696 | tf_op jit(solution)/shard_map/ppermute | solution.py:245
  45.1 17.9 %collective-permute-start.7 = (bf16[64,5632]{1,0:T(8,128)(2,1)S(1)}, bf16[64,5632]{1,0:T(8,128)(2,1)S(1)}, u32[]{:S(2)}, u32[]{:S(2)}) collective-permute-start(bf16[64,5632]{1,0:T(8,128)(2,1)S(1)} %collective-permute-done.6.refs_4_), channel_id=1, source_target_pairs={{0,2},{1,3},{2,0},{3,1},{4,6},{5,7},{6,4},{7,5},{8,10},{9,11},{10,... | collective-permute-start | bytes 2162696 | tf_op jit(solution)/shard_map/ppermute | solution.py:245
  47.2 26.6 %collective-permute-start.10 = (bf16[32,5632]{1,0:T(8,128)(2,1)S(1)}, bf16[32,5632]{1,0:T(8,128)(2,1)S(1)}, u32[]{:S(2)}, u32[]{:S(2)}) collective-permute-start(bf16[32,5632]{1,0:T(8,128)(2,1)S(1)} %slice.8), channel_id=1, source_target_pairs={{0,4},{1,5},{2,6},{3,7},{4,8},{5,9},{6,10},{7,11},{8,12},{9,13},{1... | collective-permute-start | bytes 1081352 | tf_op jit(solution)/shard_map/ppermute | solution.py:245
  61.5 12.4 %collective-permute-start.9 = (bf16[32,5632]{1,0:T(8,128)(2,1)S(1)}, bf16[32,5632]{1,0:T(8,128)(2,1)S(1)}, u32[]{:S(2)}, u32[]{:S(2)}) collective-permute-start(bf16[32,5632]{1,0:T(8,128)(2,1)S(1)} %slice.6), channel_id=1, source_target_pairs={{0,2},{1,3},{2,0},{3,1},{4,6},{5,7},{6,4},{7,5},{8,10},{9,11},{10,... | collective-permute-start | bytes 1081352 | tf_op jit(solution)/shard_map/ppermute | solution.py:245
  63.1 1.4 %copy-start = (bf16[128,5760]{1,0:T(8,128)(2,1)S(1)}, bf16[128,5760]{1,0:T(8,128)(2,1)}, u32[]{:S(2)}) copy-start(bf16[128,5760]{1,0:T(8,128)(2,1)} %get-tuple-element.22.own) | copy-start | bytes 4423684
  66.9 6.9 %copy-start.1 = (bf16[128,5760]{1,0:T(8,128)(2,1)S(1)}, bf16[128,5760]{1,0:T(8,128)(2,1)}, u32[]{:S(2)}) copy-start(bf16[128,5760]{1,0:T(8,128)(2,1)} %get-tuple-element.22.own) | copy-start | bytes 4423684
  75.7 0.7 copy-start.4
  76.4 33.0 %copy-start.3 = (bf16[4096,256]{1,0:T(8,128)(2,1)S(1)}, bf16[4096,256]{1,0:T(8,128)(2,1)}, u32[]{:S(2)}) copy-start(bf16[4096,256]{1,0:T(8,128)(2,1)} %fisher.1) | copy-start | bytes 6291460
  76.4 2.1 %collective-permute-start.11 = (f32[128,256]{1,0:T(8,128)S(1)}, f32[128,256]{1,0:T(8,128)S(1)}, u32[]{:S(2)}, u32[]{:S(2)}) collective-permute-start(f32[128,256]{1,0:T(8,128)S(1)} %get-tuple-element.32), channel_id=1, source_target_pairs={{0,1},{1,0},{2,3},{3,2},{4,5},{5,4},{6,7},{7,6},{8,9},{9,8},{10,11... | collective-permute-start | bytes 393224 | tf_op jit(solution)/shard_map/ppermute | solution.py:245
  77.0 6.3 %collective-permute-start.12 = (f32[128,256]{1,0:T(8,128)S(1)}, f32[128,256]{1,0:T(8,128)S(1)}, u32[]{:S(2)}, u32[]{:S(2)}) collective-permute-start(f32[128,256]{1,0:T(8,128)S(1)} %get-tuple-element.33), channel_id=1, source_target_pairs={{0,16},{1,17},{2,18},{3,19},{4,20},{5,21},{6,22},{7,23},{8,24},{9,... | collective-permute-start | bytes 393224 | tf_op jit(solution)/shard_map/ppermute | solution.py:245
  78.5 5.8 %collective-permute-start.13 = (f32[128,256]{1,0:T(8,128)S(1)}, f32[128,256]{1,0:T(8,128)S(1)}, u32[]{:S(2)}, u32[]{:S(2)}) collective-permute-start(f32[128,256]{1,0:T(8,128)S(1)} %get-tuple-element.34), channel_id=1, source_target_pairs={{0,17},{1,16},{2,19},{3,18},{4,21},{5,20},{6,23},{7,22},{8,25},{9,... | collective-permute-start | bytes 393224 | tf_op jit(solution)/shard_map/ppermute | solution.py:245
  78.5 5.8 %copy-start.5 = (f32[128,256]{1,0:T(8,128)}, f32[128,256]{1,0:T(8,128)S(1)}, u32[]{:S(2)}) copy-start(f32[128,256]{1,0:T(8,128)S(1)} %collective-permute-done.11.p1) | copy-start | bytes 393220
  83.3 1.0 copy-start.6
  84.2 0.7 copy-start.7
  107.5 1.9 %collective-permute-start.14 = (bf16[8,16,16,128]{3,2,1,0:T(8,128)(2,1)S(1)}, bf16[8,16,16,128]{3,2,1,0:T(8,128)(2,1)S(1)}, u32[]{:S(2)}, u32[]{:S(2)}) collective-permute-start(bf16[8,16,16,128]{3,2,1,0:T(8,128)(2,1)S(1)} %all_to_all.14.own), channel_id=1, source_target_pairs={{0,1},{1,0},{2,3},{3,2},{4,5},{5,4},{6,7},{7,6},{8,9},{9,8},{10,11... | collective-permute-start | bytes 1572872 | tf_op jit(solution)/shard_map/ppermute | solution.py:245

commit v5 on v4

--- a/solution.py
+++ b/solution.py
@@ -86,54 +86,47 @@
             refs[-1][b, :, k * LANES : (k + 1) * LANES] = got
 
 
-def mid_kernel(sub, width, ids, sizes, xc, *refs):
+def late_kernel(sub, width, ids, sizes, own, other, x, early_ref, *refs):
+    pieces, outs = refs[:-3], refs[-3:]
+    experts = [piece_of(at, sizes) for at in ids]
+    rows = [own[...], other[...], x[...]]
+    for b, slots in enumerate(picks(rows, pieces, experts, width, sub)):
+        for k, got in enumerate(slots):
+            lanes = slice(k * LANES, (k + 1) * LANES)
+            outs[b][:, lanes] = early_ref[b, :, lanes] + got
+
+
+def last_kernel(sub, width, ids, sizes, xc, *refs):
     experts = [piece_of(at, sizes) for at in ids]
     for k, got in enumerate(picks([xc[...]], refs[:-1], experts, width, sub)[0]):
         refs[-1][:, k * LANES : (k + 1) * LANES] = got
 
 
-def last_kernel(sub, width, ids, sizes, own, other, x, xc, early_ref, mid_ref, *refs):
-    pieces, outs = refs[:-4], refs[-4:]
-    experts = [piece_of(at, sizes) for at in ids]
-    rows = [own[...], other[...], x[...], xc[...]]
-    for b, slots in enumerate(picks(rows, pieces, experts, width, sub)):
-        for k, got in enumerate(slots):
-            lanes = slice(k * LANES, (k + 1) * LANES)
-            outs[b][:, lanes] = (early_ref[b, :, lanes] if b < 3 else mid_ref[:, lanes]) + got
-
-
 def pack_kernel(outputs, routes_ref, *refs):
     core, _, half = position()
     n_blocks = sum(len(blocks) for blocks in outputs)
-    ins, outs = refs[:n_blocks], refs[n_blocks : n_blocks + len(outputs)]
-    buffers, in_sems, out_sems = refs[n_blocks + len(outputs) : -2], refs[-2], refs[-1]
+    ins, outs, routes, sems = refs[:n_blocks], refs[n_blocks:-2], refs[-2], refs[-1]
     copies, i = [], 0
-    for blocks, buffer in zip(outputs, buffers):
-        at, group = 0, []
+    named = pltpu.make_async_copy(routes_ref, routes, sems.at[n_blocks])
+    named.start()
+    for blocks, out in zip(outputs, outs):
+        at = 0
         for width, place, offset in blocks:
             start = pl.multiple_of((place(core, half) + offset) * width, LANES)
-            copy = pltpu.make_async_copy(
-                ins[i].at[:, pl.ds(start, width)], buffer.at[:, at : at + width], in_sems.at[i]
-            )
+            copy = pltpu.make_async_copy(ins[i].at[:, pl.ds(start, width)], out.at[:, at : at + width], sems.at[i])
             copy.start()
-            group.append(copy)
+            copies.append(copy)
             at, i = at + width, i + 1
-        copies.append(group)
     row = lax.broadcasted_iota(jnp.int32, (TOK, LANES), 0)
-    routes = routes_ref[...].astype(jnp.float32)
+    named.wait()
+    routes = routes[...].astype(jnp.float32)
     named = jnp.where(row == 0, routes[0:1], jnp.where(row == 1, routes[1:2], 0.0))
     named = jnp.transpose(named).astype(jnp.bfloat16)
-    back = []
-    for i, (blocks, buffer, group) in enumerate(zip(outputs, buffers, copies)):
+    for blocks, out in zip(outputs, outs):
         size = sum(block[0] for block in blocks)
-        if buffer.shape[1] > size:
-            buffer[:, size:] = named
-        for copy in group:
-            copy.wait()
-        copy = pltpu.make_async_copy(buffer, outs[i], out_sems.at[i])
-        copy.start()
-        back.append(copy)
-    for copy in back:
+        if out.shape[1] > size:
+            out[:, size:] = named
+    for copy in copies:
         copy.wait()
 
 
@@ -143,17 +136,15 @@
     for out in outputs:
         rows = out[0][0].shape[0]
         shapes.append((rows, sum(b[1] for b in out) + (LANES if rows == TOK else 0)))
-    hbm = pl.BlockSpec(memory_space=pl.ANY)
     return pl.pallas_call(
         functools.partial(pack_kernel, [[b[1:] for b in out] for out in outputs]),
-        in_specs=[pl.BlockSpec(memory_space=pltpu.VMEM)] + [hbm] * len(blocks),
-        out_specs=[hbm] * len(shapes),
+        in_specs=[pl.BlockSpec(memory_space=pltpu.HBM)] * (1 + len(blocks)),
+        out_specs=[pl.BlockSpec(memory_space=pltpu.VMEM)] * len(shapes),
         out_shape=[jax.ShapeDtypeStruct(x, jnp.bfloat16) for x in shapes],
-        scratch_shapes=[pltpu.VMEM(x, jnp.bfloat16) for x in shapes]
-        + [pltpu.SemaphoreType.DMA((len(blocks),)), pltpu.SemaphoreType.DMA((len(shapes),))],
-        compiler_params=pltpu.CompilerParams(vmem_limit_bytes=2 * VMEM),
+        scratch_shapes=[pltpu.VMEM((2, TOK), jnp.int32), pltpu.SemaphoreType.DMA((len(blocks) + 1,))],
+        compiler_params=pltpu.CompilerParams(vmem_limit_bytes=VMEM),
         name=name,
-    )(routes, *[b[0] for b in blocks])
+    )(*[pltpu.with_memory_space_constraint(x, pltpu.HBM) for x in [routes] + [b[0] for b in blocks]])
 
 
 def local(kernel, name, out_shape, operands):
@@ -193,15 +184,6 @@
     mine = mine.reshape(PROJ // 4, 2 * EXPERTS, LANES).astype(jnp.bfloat16)
     for j in range(out_ref.shape[0]):
         out_ref[j] = mine
-
-
-def gram(parts, routes, copies):
-    return pl.pallas_call(
-        gram_kernel,
-        out_shape=jax.ShapeDtypeStruct((copies, PROJ // 4, 2 * EXPERTS, LANES), jnp.bfloat16),
-        compiler_params=pltpu.CompilerParams(vmem_limit_bytes=2 * VMEM),
-        name="gram",
-    )(*parts, routes)
 
 
 def fisher_kernel(own, other, fisher, out_ref):
@@ -328,20 +310,26 @@
         jax.ShapeDtypeStruct((3, TOK, 2 * LANES), f32),
         [own, other, x] + pieces[:-2],
     )
-    mid = local(
-        functools.partial(mid_kernel, sub, quarter_out, where[:-2], sizes),
-        "project_mid",
-        jax.ShapeDtypeStruct((TOK, 2 * LANES), f32),
-        [after(xc, early)] + pieces[:-2],
-    )
+    block = jax.ShapeDtypeStruct((TOK, 2 * LANES), f32)
     partial = local(
-        functools.partial(last_kernel, sub, quarter_out, where[-2:], sizes),
+        functools.partial(late_kernel, sub, quarter_out, where[-2:], sizes),
+        "project_late",
+        [block] * 3,
+        [own, other, x, early] + jax.tree.leaves(pieces[-2:]),
+    )
+    ending = local(
+        functools.partial(last_kernel, sub, quarter_out, where, sizes),
         "project_last",
-        [jax.ShapeDtypeStruct((TOK, 2 * LANES), f32)] * 4,
-        [own, other, x, xc, early, mid] + jax.tree.leaves(pieces[-2:]),
-    )
-    sums = [partial[0], move(partial[1], to_core), move(partial[2], to_x), move(partial[3], to_x_core)]
-    mine = gram(sums, routes.reshape(1, -1), chips)
+        block,
+        [after(xc, partial[0])] + jax.tree.leaves(pieces),
+    )
+    sums = [partial[0], move(partial[1], to_core), move(partial[2], to_x), move(ending, to_x_core)]
+    mine = local(
+        gram_kernel,
+        "gram",
+        jax.ShapeDtypeStruct((chips, PROJ // 4, 2 * EXPERTS, LANES), jnp.bfloat16),
+        sums + [routes.reshape(1, -1)],
+    )
 
     same_core = [list(range(c, n, 2)) for c in range(2)]
     grams = lax.all_to_all(mine, "dp", split_axis=0, concat_axis=0, axis_index_groups=same_core, tiled=True)

time: 123 us -> 115 us (0.935)
  Pallas kernels: 16.3 us -> 10.9 us
  local copies, waits for them, and re-layouts: 3.4 us -> 0.71 us
    pallas_call x2, Pallas kernels: 7.52 us -> 3.85 us  [pack(): pl.pallas_call(functools.partial(pack_kernel, [[b[1:] for b in out] for o...]
    unnamed x17 -> x5, local copies, waits for them, and re-layouts: 3.35 us -> 0.67 us
    pallas_call x1 -> x0, Pallas kernels: 2.32 us -> none  [gram(): pl.pallas_call(gram_kernel, out_shape=jax.ShapeDtypeStruct((copies, PROJ...]
    pallas_call x4 -> x5, Pallas kernels: 6.41 us -> 7.07 us  [local(): pl.pallas_call(kernel, in_specs=[vmem] * len(operands), out_specs=jax.tre...]
  transfers between devices with their start and end apart: 15 -> 15, of which waited for: 8 -> 9; matrix products, arithmetic and copies ran while one was open for 0% -> 0% of each run, Pallas kernels for 6% -> 7%
where the time goes in v5:
time: 115 us
  waiting for transfers between devices  54.1 us (47%)
  blocking collectives  31.6 us (27%)
  starting transfers between devices  17.4 us (15%)
  Pallas kernels  10.9 us (9%)
    ppermute x15, waiting for transfers between devices, move(): return lax.ppermute(x, AXES, pairs)  54.1 us
    all_to_all x1, blocking collectives, shards(): lax.all_to_all(mine, 'dp', split_axis=0, concat_axis=0, axis_index_groups...  20.1 us
    ppermute x15, starting transfers between devices, move(): return lax.ppermute(x, AXES, pairs)  17.4 us
    all_to_all x1, blocking collectives, shards(): lax.all_to_all(columns, 'dp', split_axis=1, concat_axis=1, tiled=True)  11.5 us
    pallas_call x5, Pallas kernels, local(): pl.pallas_call(kernel, in_specs=[vmem] * len(operands), out_specs=jax.tre...  7.07 us
    pallas_call x2, Pallas kernels, pack(): pl.pallas_call(functools.partial(pack_kernel, [[b[1:] for b in out] for o...  3.85 us
  transfers between devices with their start and end apart: 15, of which 9 were waited for; matrix products, arithmetic and copies ran while one was open for 0% of the time, Pallas kernels for 7%

profile of v5, /device:TPU:0, one launch (start us, length us, event | category | flops | bytes accessed | tf_op | source)
XLA Modules:
  0.0 114.9 jit_solution(15707607511888713216)
XLA Ops:
  0.0 2.0 %pack_first.1 = (bf16[64,5632]{1,0:T(8,128)(2,1)S(1)}, bf16[128,5760]{1,0:T(8,128)(2,1)S(1)}, bf16[128,5760]{1,0:T(8,128)(2,1)S(1)}) custom-call(s32[2,128]{1,0:T(2,128)} %bitcast.6, bf16[64,8192]{1,0:T(8,128)(2,1)} %refs_0_.2, bf16[64,3072]{1,0:T(8,128)(2,1)} %refs_1_.2, bf16[128,16384]{1,0:T(8,128)(2,1)} %refs_2_.3, bf16[128,6144]{1,0:T(8,128)(2,1)} %refs_3_.3, ...), custom_call_target="tpu_custom_call" | custom-call | tf_op jit(solution)/shard_map/pack_first/pallas_call | solution.py:139
  2.0 0.5 collective-permute-start
  2.6 2.6 %collective-permute-start.2 = (bf16[64,5632]{1,0:T(8,128)(2,1)S(1)}, bf16[64,5632]{1,0:T(8,128)(2,1)S(1)}, u32[]{:S(2)}, u32[]{:S(2)}) collective-permute-start(bf16[64,5632]{1,0:T(8,128)(2,1)S(1)} %get-tuple-element.23.refs_0_), channel_id=1, source_target_pairs={{0,2},{1,3},{2,0},{3,1},{4,6},{5,7},{6,4},{7,5},{8,10},{9,11},{10,... | collective-permute-start | bytes 2162696 | tf_op jit(solution)/shard_map/ppermute | solution.py:227
  5.2 1.5 %collective-permute-start.1 = (bf16[128,5760]{1,0:T(8,128)(2,1)S(1)}, bf16[128,5760]{1,0:T(8,128)(2,1)S(1)}, u32[]{:S(2)}, u32[]{:S(2)}) collective-permute-start(bf16[128,5760]{1,0:T(8,128)(2,1)S(1)} %get-tuple-element.19), channel_id=1, source_target_pairs={{0,16},{1,17},{2,18},{3,19},{4,20},{5,21},{6,22},{7,23},{8,24},{9,... | collective-permute-start | bytes 4423688 | tf_op jit(solution)/shard_map/ppermute | solution.py:227
  6.7 1.6 %collective-permute-start.3 = (bf16[64,5632]{1,0:T(8,128)(2,1)S(1)}, bf16[64,5632]{1,0:T(8,128)(2,1)S(1)}, u32[]{:S(2)}, u32[]{:S(2)}) collective-permute-start(bf16[64,5632]{1,0:T(8,128)(2,1)S(1)} %get-tuple-element.23.refs_0_), channel_id=1, source_target_pairs={{0,4},{1,5},{2,6},{3,7},{4,8},{5,9},{6,10},{7,11},{8,12},{9,13},{1... | collective-permute-start | bytes 2162696 | tf_op jit(solution)/shard_map/ppermute | solution.py:227
  8.2 1.8 %pack_second.1 = (bf16[128,5760]{1,0:T(8,128)(2,1)S(1)}, bf16[128,5760]{1,0:T(8,128)(2,1)S(1)}) custom-call(s32[2,128]{1,0:T(2,128)} %bitcast.7, bf16[128,16384]{1,0:T(8,128)(2,1)} %refs_2_.3, bf16[128,6144]{1,0:T(8,128)(2,1)} %refs_3_.3, bf16[128,16384]{1,0:T(8,128)(2,1)} %refs_2_.3, bf16[128,6144]{1,0:T(8,128)(2,1)} %refs_3_.3), custom_call_target="tpu_custom_call" | custom-call | tf_op jit(solution)/shard_map/pack_second/pallas_call | solution.py:139
  10.0 11.8 %collective-permute-done.2.refs_1_ = bf16[64,5632]{1,0:T(8,128)(2,1)S(1)} collective-permute-done((bf16[64,5632]{1,0:T(8,128)(2,1)S(1)}, bf16[64,5632]{1,0:T(8,128)(2,1)S(1)}, u32[]{:S(2)}, u32[]{:S(2)}) %collective-permute-start.2) | collective-permute-done | bytes 720928 | tf_op jit(solution)/shard_map/ppermute | solution.py:227
  21.9 1.0 collective-permute-start.12
  22.9 3.6 %collective-permute-start.5 = (bf16[64,5632]{1,0:T(8,128)(2,1)S(1)}, bf16[64,5632]{1,0:T(8,128)(2,1)S(1)}, u32[]{:S(2)}, u32[]{:S(2)}) collective-permute-start(bf16[64,5632]{1,0:T(8,128)(2,1)S(1)} %get-tuple-element.23.refs_0_), channel_id=1, source_target_pairs={{0,12},{1,13},{2,14},{3,15},{4,0},{5,1},{6,2},{7,3},{8,4},{9,5},{1... | collective-permute-start | bytes 2162696 | tf_op jit(solution)/shard_map/ppermute | solution.py:227
  26.5 0.0 collective-permute-done.3.refs_2_
  26.5 1.5 %collective-permute-start.4 = (bf16[64,5632]{1,0:T(8,128)(2,1)S(1)}, bf16[64,5632]{1,0:T(8,128)(2,1)S(1)}, u32[]{:S(2)}, u32[]{:S(2)}) collective-permute-start(bf16[64,5632]{1,0:T(8,128)(2,1)S(1)} %collective-permute-done.3.refs_2_), channel_id=1, source_target_pairs={{0,2},{1,3},{2,0},{3,1},{4,6},{5,7},{6,4},{7,5},{8,10},{9,11},{10,... | collective-permute-start | bytes 2162696 | tf_op jit(solution)/shard_map/ppermute | solution.py:227
  28.0 0.0 collective-permute-done.other
  28.0 0.0 collective-permute-start.7
  28.0 15.0 %collective-permute-done.5.refs_4_ = bf16[64,5632]{1,0:T(8,128)(2,1)S(1)} collective-permute-done((bf16[64,5632]{1,0:T(8,128)(2,1)S(1)}, bf16[64,5632]{1,0:T(8,128)(2,1)S(1)}, u32[]{:S(2)}, u32[]{:S(2)}) %collective-permute-start.5) | collective-permute-done | bytes 720928 | tf_op jit(solution)/shard_map/ppermute | solution.py:227
  43.1 1.5 %collective-permute-start.6 = (bf16[64,5632]{1,0:T(8,128)(2,1)S(1)}, bf16[64,5632]{1,0:T(8,128)(2,1)S(1)}, u32[]{:S(2)}, u32[]{:S(2)}) collective-permute-start(bf16[64,5632]{1,0:T(8,128)(2,1)S(1)} %collective-permute-done.5.refs_4_), channel_id=1, source_target_pairs={{0,2},{1,3},{2,0},{3,1},{4,6},{5,7},{6,4},{7,5},{8,10},{9,11},{10,... | collective-permute-start | bytes 2162696 | tf_op jit(solution)/shard_map/ppermute | solution.py:227
  44.6 0.5 collective-permute-done.4.refs_3_
  45.1 0.1 collective-permute-start.9
  45.2 0.0 collective-permute-done.1.x
  45.2 14.2 %collective-permute-done.7.refs_0_.refs_6_ = bf16[64,5632]{1,0:T(8,128)(2,1)S(1)} collective-permute-done((bf16[64,5632]{1,0:T(8,128)(2,1)S(1)}, bf16[64,5632]{1,0:T(8,128)(2,1)S(1)}, u32[]{:S(2)}, u32[]{:S(2)}) %collective-permute-start.7) | collective-permute-done | bytes 720928 | tf_op jit(solution)/shard_map/ppermute | solution.py:227
  59.4 1.6 %collective-permute-start.8 = (bf16[32,5632]{1,0:T(8,128)(2,1)S(1)}, bf16[32,5632]{1,0:T(8,128)(2,1)S(1)}, u32[]{:S(2)}, u32[]{:S(2)}) collective-permute-start(bf16[32,5632]{1,0:T(8,128)(2,1)S(1)} %slice.6), channel_id=1, source_target_pairs={{0,2},{1,3},{2,0},{3,1},{4,6},{5,7},{6,4},{7,5},{8,10},{9,11},{10,... | collective-permute-start | bytes 1081352 | tf_op jit(solution)/shard_map/ppermute | solution.py:227
  61.0 0.0 collective-permute-done.6.refs_5_
  61.0 2.5 %project_early.1.early_ref = f32[3,128,256]{2,1,0:T(8,128)S(1)} custom-call(bf16[128,5760]{1,0:T(8,128)(2,1)S(1)} %get-tuple-element.21.own, bf16[128,5760]{1,0:T(8,128)(2,1)S(1)} %collective-permute-done.other, bf16[128,5760]{1,0:T(8,128)(2,1)S(1)} %collective-permute-done.1.x, bf16[64,5632]{1,0:T(8,128)(2,1)S(1)} %get-tuple-element.23.refs_0_, ...), custom_call_target="tpu_custom_call" | custom-call | tf_op jit(solution)/shard_map/project_early/pallas_call | solution.py:152
  63.5 3.5 %collective-permute-done.9.refs_2_.refs_8_ = bf16[32,5632]{1,0:T(8,128)(2,1)S(1)} collective-permute-done((bf16[32,5632]{1,0:T(8,128)(2,1)S(1)}, bf16[32,5632]{1,0:T(8,128)(2,1)S(1)}, u32[]{:S(2)}, u32[]{:S(2)}) %collective-permute-start.9) | collective-permute-done | bytes 360480 | tf_op jit(solution)/shard_map/ppermute | solution.py:227
  67.0 2.7 %collective-permute-done.8.refs_1_.refs_7_ = bf16[32,5632]{1,0:T(8,128)(2,1)S(1)} collective-permute-done((bf16[32,5632]{1,0:T(8,128)(2,1)S(1)}, bf16[32,5632]{1,0:T(8,128)(2,1)S(1)}, u32[]{:S(2)}, u32[]{:S(2)}) %collective-permute-start.8) | collective-permute-done | bytes 360480 | tf_op jit(solution)/shard_map/ppermute | solution.py:227
  69.7 1.4 %project_late.1 = (f32[128,256]{1,0:T(8,128)S(1)}, f32[128,256]{1,0:T(8,128)S(1)}, f32[128,256]{1,0:T(8,128)S(1)}) custom-call(bf16[128,5760]{1,0:T(8,128)(2,1)S(1)} %get-tuple-element.21.own, bf16[128,5760]{1,0:T(8,128)(2,1)S(1)} %collective-permute-done.other, bf16[128,5760]{1,0:T(8,128)(2,1)S(1)} %collective-permute-done.1.x, ...), custom_call_target="tpu_custom_call" | custom-call | tf_op jit(solution)/shard_map/project_late/pallas_call | solution.py:152
  71.1 0.1 collective-permute-start.10
  71.2 0.4 collective-permute-start.11
  71.6 0.0 collective-permute-done.12.xc
  71.6 0.0 copy-start.1
  71.6 2.0 %project_last.1 = f32[128,256]{1,0:T(8,128)S(1)} custom-call(bf16[128,5760]{1,0:T(8,128)(2,1)S(1)} %collective-permute-done.12.xc, bf16[64,5632]{1,0:T(8,128)(2,1)S(1)} %get-tuple-element.23.refs_0_, bf16[64,5632]{1,0:T(8,128)(2,1)S(1)} %collective-permute-done.2.refs_1_, bf16[64,5632]{1,0:T(8,128)(2,1)S(1)} %collective-permute-done.3.refs_2_, ...), custom_call_target="tpu_custom_call" | custom-call | tf_op jit(solution)/shard_map/project_last/pallas_call | solution.py:152
  73.6 0.0 copy-start
  73.7 1.5 %collective-permute-start.13 = (f32[128,256]{1,0:T(8,128)S(1)}, f32[128,256]{1,0:T(8,128)S(1)}, u32[]{:S(2)}, u32[]{:S(2)}) collective-permute-start(f32[128,256]{1,0:T(8,128)S(1)} %project_last.1), channel_id=1, source_target_pairs={{0,17},{1,16},{2,19},{3,18},{4,21},{5,20},{6,23},{7,22},{8,25},{9,... | collective-permute-start | bytes 393224 | tf_op jit(solution)/shard_map/ppermute | solution.py:227
  75.2 0.0 collective-permute-done.10.p1
  75.2 2.2 %collective-permute-done.11.p2 = f32[128,256]{1,0:T(8,128)S(1)} collective-permute-done((f32[128,256]{1,0:T(8,128)S(1)}, f32[128,256]{1,0:T(8,128)S(1)}, u32[]{:S(2)}, u32[]{:S(2)}) %collective-permute-start.11) | collective-permute-done | bytes 131104 | tf_op jit(solution)/shard_map/ppermute | solution.py:227
  77.4 2.2 %collective-permute-done.13.p3 = f32[128,256]{1,0:T(8,128)S(1)} collective-permute-done((f32[128,256]{1,0:T(8,128)S(1)}, f32[128,256]{1,0:T(8,128)S(1)}, u32[]{:S(2)}, u32[]{:S(2)}) %collective-permute-start.13) | collective-permute-done | bytes 131104 | tf_op jit(solution)/shard_map/ppermute | solution.py:227
  79.6 0.0 copy-done.1
  79.6 0.4 gram.1
  80.0 20.1 %all_to_all.14.own = bf16[8,16,16,128]{3,2,1,0:T(8,128)(2,1)S(1)} all-to-all(bf16[8,16,16,128]{3,2,1,0:T(8,128)(2,1)S(1)} %gram.1), channel_id=1, replica_groups={{0,2,4,6,8,10,12,14},{1,3,5,7,9,11,13,15},{16,18,20,22,24,26,28,30},{17..., dimensions={0} | all-to-all | bytes 1048576 | tf_op jit(solution)/shard_map/all_to_all | solution.py:335
  100.2 0.0 collective-permute-start.14
  100.2 1.9 %collective-permute-done.14.other = bf16[8,16,16,128]{3,2,1,0:T(8,128)(2,1)S(1)} collective-permute-done((bf16[8,16,16,128]{3,2,1,0:T(8,128)(2,1)S(1)}, bf16[8,16,16,128]{3,2,1,0:T(8,128)(2,1)S(1)}, u32[]{:S(2)}, u32[]{:S(2)}) %collective-permute-start.14) | collective-permute-done | bytes 524320 | tf_op jit(solution)/shard_map/ppermute | solution.py:227
  102.1 0.0 copy-done
  102.1 0.7 precondition.1
  102.8 11.5 %all_to_all.15 = f32[8,16,256]{2,0,1:T(8,128)S(1)} all-to-all(f32[8,16,256]{2,0,1:T(8,128)S(1)} %bitcast.5), channel_id=1, replica_groups=mesh['groups'=2,'dp'=16] {'dp'}, dimensions={1} | all-to-all | bytes 262144 | tf_op jit(solution)/shard_map/all_to_all | solution.py:342
  114.3 0.7 copy.8
  (2 shorter events, 0.0 us)
Async XLA Ops:
  2.0 26.0 %collective-permute-start = (bf16[128,5760]{1,0:T(8,128)(2,1)S(1)}, bf16[128,5760]{1,0:T(8,128)(2,1)S(1)}, u32[]{:S(2)}, u32[]{:S(2)}) collective-permute-start(bf16[128,5760]{1,0:T(8,128)(2,1)S(1)} %get-tuple-element.22), channel_id=1, source_target_pairs={{0,1},{1,0},{2,3},{3,2},{4,5},{5,4},{6,7},{7,6},{8,9},{9,8},{10,11... | collective-permute-start | bytes 4423688 | tf_op jit(solution)/shard_map/ppermute | solution.py:227
  2.6 19.3 %collective-permute-start.2 = (bf16[64,5632]{1,0:T(8,128)(2,1)S(1)}, bf16[64,5632]{1,0:T(8,128)(2,1)S(1)}, u32[]{:S(2)}, u32[]{:S(2)}) collective-permute-start(bf16[64,5632]{1,0:T(8,128)(2,1)S(1)} %get-tuple-element.23.refs_0_), channel_id=1, source_target_pairs={{0,2},{1,3},{2,0},{3,1},{4,6},{5,7},{6,4},{7,5},{8,10},{9,11},{10,... | collective-permute-start | bytes 2162696 | tf_op jit(solution)/shard_map/ppermute | solution.py:227
  5.2 40.0 %collective-permute-start.1 = (bf16[128,5760]{1,0:T(8,128)(2,1)S(1)}, bf16[128,5760]{1,0:T(8,128)(2,1)S(1)}, u32[]{:S(2)}, u32[]{:S(2)}) collective-permute-start(bf16[128,5760]{1,0:T(8,128)(2,1)S(1)} %get-tuple-element.19), channel_id=1, source_target_pairs={{0,16},{1,17},{2,18},{3,19},{4,20},{5,21},{6,22},{7,23},{8,24},{9,... | collective-permute-start | bytes 4423688 | tf_op jit(solution)/shard_map/ppermute | solution.py:227
  6.7 19.8 %collective-permute-start.3 = (bf16[64,5632]{1,0:T(8,128)(2,1)S(1)}, bf16[64,5632]{1,0:T(8,128)(2,1)S(1)}, u32[]{:S(2)}, u32[]{:S(2)}) collective-permute-start(bf16[64,5632]{1,0:T(8,128)(2,1)S(1)} %get-tuple-element.23.refs_0_), channel_id=1, source_target_pairs={{0,4},{1,5},{2,6},{3,7},{4,8},{5,9},{6,10},{7,11},{8,12},{9,13},{1... | collective-permute-start | bytes 2162696 | tf_op jit(solution)/shard_map/ppermute | solution.py:227
  21.9 49.7 %collective-permute-start.12 = (bf16[128,5760]{1,0:T(8,128)(2,1)S(1)}, bf16[128,5760]{1,0:T(8,128)(2,1)S(1)}, u32[]{:S(2)}, u32[]{:S(2)}) collective-permute-start(bf16[128,5760]{1,0:T(8,128)(2,1)S(1)} %get-tuple-element.31), channel_id=1, source_target_pairs={{0,17},{1,16},{2,19},{3,18},{4,21},{5,20},{6,23},{7,22},{8,25},{9,... | collective-permute-start | bytes 4423688 | tf_op jit(solution)/shard_map/ppermute | solution.py:227
  22.9 20.2 %collective-permute-start.5 = (bf16[64,5632]{1,0:T(8,128)(2,1)S(1)}, bf16[64,5632]{1,0:T(8,128)(2,1)S(1)}, u32[]{:S(2)}, u32[]{:S(2)}) collective-permute-start(bf16[64,5632]{1,0:T(8,128)(2,1)S(1)} %get-tuple-element.23.refs_0_), channel_id=1, source_target_pairs={{0,12},{1,13},{2,14},{3,15},{4,0},{5,1},{6,2},{7,3},{8,4},{9,5},{1... | collective-permute-start | bytes 2162696 | tf_op jit(solution)/shard_map/ppermute | solution.py:227
  26.5 18.6 %collective-permute-start.4 = (bf16[64,5632]{1,0:T(8,128)(2,1)S(1)}, bf16[64,5632]{1,0:T(8,128)(2,1)S(1)}, u32[]{:S(2)}, u32[]{:S(2)}) collective-permute-start(bf16[64,5632]{1,0:T(8,128)(2,1)S(1)} %collective-permute-done.3.refs_2_), channel_id=1, source_target_pairs={{0,2},{1,3},{2,0},{3,1},{4,6},{5,7},{6,4},{7,5},{8,10},{9,11},{10,... | collective-permute-start | bytes 2162696 | tf_op jit(solution)/shard_map/ppermute | solution.py:227
  28.0 31.4 %collective-permute-start.7 = (bf16[64,5632]{1,0:T(8,128)(2,1)S(1)}, bf16[64,5632]{1,0:T(8,128)(2,1)S(1)}, u32[]{:S(2)}, u32[]{:S(2)}) collective-permute-start(bf16[64,5632]{1,0:T(8,128)(2,1)S(1)} %collective-permute-done.3.refs_2_), channel_id=1, source_target_pairs={{0,4},{1,5},{2,6},{3,7},{4,8},{5,9},{6,10},{7,11},{8,12},{9,13},{1... | collective-permute-start | bytes 2162696 | tf_op jit(solution)/shard_map/ppermute | solution.py:227
  43.1 17.9 %collective-permute-start.6 = (bf16[64,5632]{1,0:T(8,128)(2,1)S(1)}, bf16[64,5632]{1,0:T(8,128)(2,1)S(1)}, u32[]{:S(2)}, u32[]{:S(2)}) collective-permute-start(bf16[64,5632]{1,0:T(8,128)(2,1)S(1)} %collective-permute-done.5.refs_4_), channel_id=1, source_target_pairs={{0,2},{1,3},{2,0},{3,1},{4,6},{5,7},{6,4},{7,5},{8,10},{9,11},{10,... | collective-permute-start | bytes 2162696 | tf_op jit(solution)/shard_map/ppermute | solution.py:227
  45.1 21.8 %collective-permute-start.9 = (bf16[32,5632]{1,0:T(8,128)(2,1)S(1)}, bf16[32,5632]{1,0:T(8,128)(2,1)S(1)}, u32[]{:S(2)}, u32[]{:S(2)}) collective-permute-start(bf16[32,5632]{1,0:T(8,128)(2,1)S(1)} %slice.8), channel_id=1, source_target_pairs={{0,4},{1,5},{2,6},{3,7},{4,8},{5,9},{6,10},{7,11},{8,12},{9,13},{1... | collective-permute-start | bytes 1081352 | tf_op jit(solution)/shard_map/ppermute | solution.py:227
  59.4 10.3 %collective-permute-start.8 = (bf16[32,5632]{1,0:T(8,128)(2,1)S(1)}, bf16[32,5632]{1,0:T(8,128)(2,1)S(1)}, u32[]{:S(2)}, u32[]{:S(2)}) collective-permute-start(bf16[32,5632]{1,0:T(8,128)(2,1)S(1)} %slice.6), channel_id=1, source_target_pairs={{0,2},{1,3},{2,0},{3,1},{4,6},{5,7},{6,4},{7,5},{8,10},{9,11},{10,... | collective-permute-start | bytes 1081352 | tf_op jit(solution)/shard_map/ppermute | solution.py:227
  71.1 4.1 %collective-permute-start.10 = (f32[128,256]{1,0:T(8,128)S(1)}, f32[128,256]{1,0:T(8,128)S(1)}, u32[]{:S(2)}, u32[]{:S(2)}) collective-permute-start(f32[128,256]{1,0:T(8,128)S(1)} %get-tuple-element.28), channel_id=1, source_target_pairs={{0,1},{1,0},{2,3},{3,2},{4,5},{5,4},{6,7},{7,6},{8,9},{9,8},{10,11... | collective-permute-start | bytes 393224 | tf_op jit(solution)/shard_map/ppermute | solution.py:227
  71.2 6.2 %collective-permute-start.11 = (f32[128,256]{1,0:T(8,128)S(1)}, f32[128,256]{1,0:T(8,128)S(1)}, u32[]{:S(2)}, u32[]{:S(2)}) collective-permute-start(f32[128,256]{1,0:T(8,128)S(1)} %get-tuple-element.29), channel_id=1, source_target_pairs={{0,16},{1,17},{2,18},{3,19},{4,20},{5,21},{6,22},{7,23},{8,24},{9,... | collective-permute-start | bytes 393224 | tf_op jit(solution)/shard_map/ppermute | solution.py:227
  71.6 8.0 %copy-start.1 = (s32[128,2]{0,1:T(2,128)S(1)}, s32[128,2]{0,1:T(2,128)}, u32[]{:S(2)}) copy-start(s32[128,2]{0,1:T(2,128)} %param.8) | copy-start | bytes 3076
  73.6 28.4 %copy-start = (bf16[4096,256]{1,0:T(8,128)(2,1)S(1)}, bf16[4096,256]{1,0:T(8,128)(2,1)}, u32[]{:S(2)}) copy-start(bf16[4096,256]{1,0:T(8,128)(2,1)} %fisher.1) | copy-start | bytes 6291460
  73.7 5.9 %collective-permute-start.13 = (f32[128,256]{1,0:T(8,128)S(1)}, f32[128,256]{1,0:T(8,128)S(1)}, u32[]{:S(2)}, u32[]{:S(2)}) collective-permute-start(f32[128,256]{1,0:T(8,128)S(1)} %project_last.1), channel_id=1, source_target_pairs={{0,17},{1,16},{2,19},{3,18},{4,21},{5,20},{6,23},{7,22},{8,25},{9,... | collective-permute-start | bytes 393224 | tf_op jit(solution)/shard_map/ppermute | solution.py:227
  100.2 1.9 %collective-permute-start.14 = (bf16[8,16,16,128]{3,2,1,0:T(8,128)(2,1)S(1)}, bf16[8,16,16,128]{3,2,1,0:T(8,128)(2,1)S(1)}, u32[]{:S(2)}, u32[]{:S(2)}) collective-permute-start(bf16[8,16,16,128]{3,2,1,0:T(8,128)(2,1)S(1)} %all_to_all.14.own), channel_id=1, source_target_pairs={{0,1},{1,0},{2,3},{3,2},{4,5},{5,4},{6,7},{7,6},{8,9},{9,8},{10,11... | collective-permute-start | bytes 1572872 | tf_op jit(solution)/shard_map/ppermute | solution.py:227

commit v6 on v5

--- a/solution.py
+++ b/solution.py
@@ -181,18 +181,16 @@
     rows = PROJ // 2 * EXPERTS
     first = lax.broadcasted_iota(jnp.int32, (rows, LANES), 1) < PROJ
     mine = jnp.where(first, pltpu.roll(grams[:rows], PROJ, 1), grams[rows:])
-    mine = mine.reshape(PROJ // 4, 2 * EXPERTS, LANES).astype(jnp.bfloat16)
-    for j in range(out_ref.shape[0]):
-        out_ref[j] = mine
-
-
-def fisher_kernel(own, other, fisher, out_ref):
-    n = 2 * own.shape[0]
-    core, _, _ = position()
+    out_ref[...] = mine.reshape(PROJ // 4, 2 * EXPERTS, LANES).astype(jnp.bfloat16)
+
+
+def fisher_kernel(steps, *refs):
+    fisher, out_ref = refs[-2:]
+    n = 2 * len(steps)
+    core, chip, _ = position()
     total = jnp.zeros((n * EXPERTS, fisher.shape[1]), jnp.float32)
     for i in range(PROJ // 4):
-        rows = jnp.concatenate([x[:, i].astype(jnp.float32) for x in (own, other)], axis=0)
-        rows = rows.reshape(n, 2, EXPERTS, LANES)
+        rows = jnp.concatenate([x[i].astype(jnp.float32).reshape(1, 2, EXPERTS, LANES) for x in refs[:n]], axis=0)
         for h in range(2):
             p = 2 * i + h
             table = jnp.concatenate(
@@ -205,10 +203,10 @@
             lhs = rows[:, h].reshape(n * EXPERTS, LANES).astype(jnp.bfloat16)
             total += jnp.dot(lhs, table, preferred_element_type=jnp.float32)
     width = fisher.shape[1]
-    for j in range(n // 2):
-        for rows, place in ((j, 2 * j + core), (n // 2 + j, 2 * j + 1 - core)):
-            at = pl.multiple_of(place * width, LANES)
-            out_ref[:, pl.ds(at, width)] = total[rows * EXPERTS : (rows + 1) * EXPERTS]
+    for j in range(n):
+        owner = 2 * jnp.bitwise_xor(chip, steps[j % len(steps)]) + (core if j < len(steps) else 1 - core)
+        at = pl.multiple_of(owner * width, LANES)
+        out_ref[:, pl.ds(at, width)] = total[j * EXPERTS : (j + 1) * EXPERTS]
 
 
 def shards(features, grads, routes, proj_in, proj_out, fisher_inverse):
@@ -327,17 +325,25 @@
     mine = local(
         gram_kernel,
         "gram",
-        jax.ShapeDtypeStruct((chips, PROJ // 4, 2 * EXPERTS, LANES), jnp.bfloat16),
+        jax.ShapeDtypeStruct((PROJ // 4, 2 * EXPERTS, LANES), jnp.bfloat16),
         sums + [routes.reshape(1, -1)],
     )
 
-    same_core = [list(range(c, n, 2)) for c in range(2)]
-    grams = lax.all_to_all(mine, "dp", split_axis=0, concat_axis=0, axis_index_groups=same_core, tiled=True)
+    def far(step):
+        return lambda g, d: (g, d ^ (2 * step))
+
+    grams, steps = [mine], [0]
+    for step in sorted(range(1, z_size), key=lambda k: (-(k >= z_size // 2), k)):
+        grams.append(move(mine, far(step * y_size)))
+        steps.append(step * y_size)
+    if y_size == 2:
+        grams = grams + [move(x, to_y) for x in grams]
+        steps = steps + [step ^ 1 for step in steps]
     columns = local(
-        fisher_kernel,
+        functools.partial(fisher_kernel, steps),
         "precondition",
         jax.ShapeDtypeStruct((EXPERTS, PROJ * PROJ), f32),
-        [grams, move(grams, to_core), fisher_inverse],
+        grams + [move(x, to_core) for x in grams] + [fisher_inverse],
     )
     result = lax.all_to_all(columns, "dp", split_axis=1, concat_axis=1, tiled=True)
     return result.reshape(1, EXPERTS, PROJ * PROJ)

time: 115 us -> 111 us (0.965)
  blocking collectives: 31.6 us -> 11.8 us
  starting transfers between devices: 17.4 us -> 25.4 us
  waiting for transfers between devices: 54.1 us -> 62.1 us
    all_to_all x1 -> x0, blocking collectives: 20.1 us -> none  [shards(): lax.all_to_all(mine, 'dp', split_axis=0, concat_axis=0, axis_index_groups...]
    ppermute x15 -> x29, waiting for transfers between devices: 54.1 us -> 62.1 us  [move(): return lax.ppermute(x, AXES, pairs)]
    ppermute x15 -> x29, starting transfers between devices: 17.4 us -> 25.4 us  [move(): return lax.ppermute(x, AXES, pairs)]
  transfers between devices with their start and end apart: 15 -> 29, of which waited for: 9 -> 14; matrix products, arithmetic and copies ran while one was open for 0% -> 0% of each run, Pallas kernels for 7% -> 7%
where the time goes in v6:
time: 111 us
  waiting for transfers between devices  62.1 us (56%)
  starting transfers between devices  25.4 us (23%)
  blocking collectives  11.8 us (11%)
  Pallas kernels  10.9 us (10%)
    ppermute x29, waiting for transfers between devices, move(): return lax.ppermute(x, AXES, pairs)  62.1 us
    ppermute x29, starting transfers between devices, move(): return lax.ppermute(x, AXES, pairs)  25.4 us
    all_to_all x1, blocking collectives, shards(): lax.all_to_all(columns, 'dp', split_axis=1, concat_axis=1, tiled=True)  11.8 us
    pallas_call x5, Pallas kernels, local(): pl.pallas_call(kernel, in_specs=[vmem] * len(operands), out_specs=jax.tre...  7.08 us
    pallas_call x2, Pallas kernels, pack(): pl.pallas_call(functools.partial(pack_kernel, [[b[1:] for b in out] for o...  3.85 us
  transfers between devices with their start and end apart: 29, of which 14 were waited for; matrix products, arithmetic and copies ran while one was open for 0% of the time, Pallas kernels for 7%

profile of v6, /device:TPU:0, one launch (start us, length us, event | category | flops | bytes accessed | tf_op | source)
XLA Modules:
  0.0 111.1 jit_solution(7952987003042914179)
XLA Ops:
  0.0 2.0 %pack_first.1 = (bf16[64,5632]{1,0:T(8,128)(2,1)S(1)}, bf16[128,5760]{1,0:T(8,128)(2,1)S(1)}, bf16[128,5760]{1,0:T(8,128)(2,1)S(1)}) custom-call(s32[2,128]{1,0:T(2,128)} %bitcast.6, bf16[64,8192]{1,0:T(8,128)(2,1)} %refs_0_.2, bf16[64,3072]{1,0:T(8,128)(2,1)} %refs_1_.2, bf16[128,16384]{1,0:T(8,128)(2,1)} %refs_2_.3, bf16[128,6144]{1,0:T(8,128)(2,1)} %refs_3_.3, ...), custom_call_target="tpu_custom_call" | custom-call | tf_op jit(solution)/shard_map/pack_first/pallas_call | solution.py:139
  2.0 0.5 collective-permute-start
  2.6 2.6 %collective-permute-start.2 = (bf16[64,5632]{1,0:T(8,128)(2,1)S(1)}, bf16[64,5632]{1,0:T(8,128)(2,1)S(1)}, u32[]{:S(2)}, u32[]{:S(2)}) collective-permute-start(bf16[64,5632]{1,0:T(8,128)(2,1)S(1)} %get-tuple-element.23.refs_0_), channel_id=1, source_target_pairs={{0,2},{1,3},{2,0},{3,1},{4,6},{5,7},{6,4},{7,5},{8,10},{9,11},{10,... | collective-permute-start | bytes 2162696 | tf_op jit(solution)/shard_map/ppermute | solution.py:225
  5.2 1.5 %collective-permute-start.1 = (bf16[128,5760]{1,0:T(8,128)(2,1)S(1)}, bf16[128,5760]{1,0:T(8,128)(2,1)S(1)}, u32[]{:S(2)}, u32[]{:S(2)}) collective-permute-start(bf16[128,5760]{1,0:T(8,128)(2,1)S(1)} %get-tuple-element.19), channel_id=1, source_target_pairs={{0,16},{1,17},{2,18},{3,19},{4,20},{5,21},{6,22},{7,23},{8,24},{9,... | collective-permute-start | bytes 4423688 | tf_op jit(solution)/shard_map/ppermute | solution.py:225
  6.7 1.6 %collective-permute-start.3 = (bf16[64,5632]{1,0:T(8,128)(2,1)S(1)}, bf16[64,5632]{1,0:T(8,128)(2,1)S(1)}, u32[]{:S(2)}, u32[]{:S(2)}) collective-permute-start(bf16[64,5632]{1,0:T(8,128)(2,1)S(1)} %get-tuple-element.23.refs_0_), channel_id=1, source_target_pairs={{0,4},{1,5},{2,6},{3,7},{4,8},{5,9},{6,10},{7,11},{8,12},{9,13},{1... | collective-permute-start | bytes 2162696 | tf_op jit(solution)/shard_map/ppermute | solution.py:225
  8.2 1.8 %pack_second.1 = (bf16[128,5760]{1,0:T(8,128)(2,1)S(1)}, bf16[128,5760]{1,0:T(8,128)(2,1)S(1)}) custom-call(s32[2,128]{1,0:T(2,128)} %bitcast.7, bf16[128,16384]{1,0:T(8,128)(2,1)} %refs_2_.3, bf16[128,6144]{1,0:T(8,128)(2,1)} %refs_3_.3, bf16[128,16384]{1,0:T(8,128)(2,1)} %refs_2_.3, bf16[128,6144]{1,0:T(8,128)(2,1)} %refs_3_.3), custom_call_target="tpu_custom_call" | custom-call | tf_op jit(solution)/shard_map/pack_second/pallas_call | solution.py:139
  10.0 11.8 %collective-permute-done.2.refs_1_ = bf16[64,5632]{1,0:T(8,128)(2,1)S(1)} collective-permute-done((bf16[64,5632]{1,0:T(8,128)(2,1)S(1)}, bf16[64,5632]{1,0:T(8,128)(2,1)S(1)}, u32[]{:S(2)}, u32[]{:S(2)}) %collective-permute-start.2) | collective-permute-done | bytes 720928 | tf_op jit(solution)/shard_map/ppermute | solution.py:225
  21.9 1.0 collective-permute-start.12
  22.9 3.6 %collective-permute-start.5 = (bf16[64,5632]{1,0:T(8,128)(2,1)S(1)}, bf16[64,5632]{1,0:T(8,128)(2,1)S(1)}, u32[]{:S(2)}, u32[]{:S(2)}) collective-permute-start(bf16[64,5632]{1,0:T(8,128)(2,1)S(1)} %get-tuple-element.23.refs_0_), channel_id=1, source_target_pairs={{0,12},{1,13},{2,14},{3,15},{4,0},{5,1},{6,2},{7,3},{8,4},{9,5},{1... | collective-permute-start | bytes 2162696 | tf_op jit(solution)/shard_map/ppermute | solution.py:225
  26.5 0.0 collective-permute-done.3.refs_2_
  26.5 1.5 %collective-permute-start.4 = (bf16[64,5632]{1,0:T(8,128)(2,1)S(1)}, bf16[64,5632]{1,0:T(8,128)(2,1)S(1)}, u32[]{:S(2)}, u32[]{:S(2)}) collective-permute-start(bf16[64,5632]{1,0:T(8,128)(2,1)S(1)} %collective-permute-done.3.refs_2_), channel_id=1, source_target_pairs={{0,2},{1,3},{2,0},{3,1},{4,6},{5,7},{6,4},{7,5},{8,10},{9,11},{10,... | collective-permute-start | bytes 2162696 | tf_op jit(solution)/shard_map/ppermute | solution.py:225
  28.0 0.0 collective-permute-done.other
  28.0 0.0 collective-permute-start.7
  28.0 15.0 %collective-permute-done.5.refs_4_ = bf16[64,5632]{1,0:T(8,128)(2,1)S(1)} collective-permute-done((bf16[64,5632]{1,0:T(8,128)(2,1)S(1)}, bf16[64,5632]{1,0:T(8,128)(2,1)S(1)}, u32[]{:S(2)}, u32[]{:S(2)}) %collective-permute-start.5) | collective-permute-done | bytes 720928 | tf_op jit(solution)/shard_map/ppermute | solution.py:225
  43.1 1.5 %collective-permute-start.6 = (bf16[64,5632]{1,0:T(8,128)(2,1)S(1)}, bf16[64,5632]{1,0:T(8,128)(2,1)S(1)}, u32[]{:S(2)}, u32[]{:S(2)}) collective-permute-start(bf16[64,5632]{1,0:T(8,128)(2,1)S(1)} %collective-permute-done.5.refs_4_), channel_id=1, source_target_pairs={{0,2},{1,3},{2,0},{3,1},{4,6},{5,7},{6,4},{7,5},{8,10},{9,11},{10,... | collective-permute-start | bytes 2162696 | tf_op jit(solution)/shard_map/ppermute | solution.py:225
  44.6 0.5 collective-permute-done.4.refs_3_
  45.1 0.1 collective-permute-start.9
  45.2 0.0 collective-permute-done.1.x
  45.2 14.2 %collective-permute-done.7.refs_0_.refs_6_ = bf16[64,5632]{1,0:T(8,128)(2,1)S(1)} collective-permute-done((bf16[64,5632]{1,0:T(8,128)(2,1)S(1)}, bf16[64,5632]{1,0:T(8,128)(2,1)S(1)}, u32[]{:S(2)}, u32[]{:S(2)}) %collective-permute-start.7) | collective-permute-done | bytes 720928 | tf_op jit(solution)/shard_map/ppermute | solution.py:225
  59.4 1.6 %collective-permute-start.8 = (bf16[32,5632]{1,0:T(8,128)(2,1)S(1)}, bf16[32,5632]{1,0:T(8,128)(2,1)S(1)}, u32[]{:S(2)}, u32[]{:S(2)}) collective-permute-start(bf16[32,5632]{1,0:T(8,128)(2,1)S(1)} %slice.6), channel_id=1, source_target_pairs={{0,2},{1,3},{2,0},{3,1},{4,6},{5,7},{6,4},{7,5},{8,10},{9,11},{10,... | collective-permute-start | bytes 1081352 | tf_op jit(solution)/shard_map/ppermute | solution.py:225
  61.0 0.0 collective-permute-done.6.refs_5_
  61.0 2.5 %project_early.1.early_ref = f32[3,128,256]{2,1,0:T(8,128)S(1)} custom-call(bf16[128,5760]{1,0:T(8,128)(2,1)S(1)} %get-tuple-element.21.own, bf16[128,5760]{1,0:T(8,128)(2,1)S(1)} %collective-permute-done.other, bf16[128,5760]{1,0:T(8,128)(2,1)S(1)} %collective-permute-done.1.x, bf16[64,5632]{1,0:T(8,128)(2,1)S(1)} %get-tuple-element.23.refs_0_, ...), custom_call_target="tpu_custom_call" | custom-call | tf_op jit(solution)/shard_map/project_early/pallas_call | solution.py:152
  63.5 3.5 %collective-permute-done.9.refs_2_.refs_8_ = bf16[32,5632]{1,0:T(8,128)(2,1)S(1)} collective-permute-done((bf16[32,5632]{1,0:T(8,128)(2,1)S(1)}, bf16[32,5632]{1,0:T(8,128)(2,1)S(1)}, u32[]{:S(2)}, u32[]{:S(2)}) %collective-permute-start.9) | collective-permute-done | bytes 360480 | tf_op jit(solution)/shard_map/ppermute | solution.py:225
  67.0 2.7 %collective-permute-done.8.refs_1_.refs_7_ = bf16[32,5632]{1,0:T(8,128)(2,1)S(1)} collective-permute-done((bf16[32,5632]{1,0:T(8,128)(2,1)S(1)}, bf16[32,5632]{1,0:T(8,128)(2,1)S(1)}, u32[]{:S(2)}, u32[]{:S(2)}) %collective-permute-start.8) | collective-permute-done | bytes 360480 | tf_op jit(solution)/shard_map/ppermute | solution.py:225
  69.7 1.4 %project_late.1 = (f32[128,256]{1,0:T(8,128)S(1)}, f32[128,256]{1,0:T(8,128)S(1)}, f32[128,256]{1,0:T(8,128)S(1)}) custom-call(bf16[128,5760]{1,0:T(8,128)(2,1)S(1)} %get-tuple-element.21.own, bf16[128,5760]{1,0:T(8,128)(2,1)S(1)} %collective-permute-done.other, bf16[128,5760]{1,0:T(8,128)(2,1)S(1)} %collective-permute-done.1.x, ...), custom_call_target="tpu_custom_call" | custom-call | tf_op jit(solution)/shard_map/project_late/pallas_call | solution.py:152
  71.1 0.1 collective-permute-start.10
  71.2 0.4 collective-permute-start.11
  71.6 0.0 collective-permute-done.12.xc
  71.6 2.0 %project_last.1 = f32[128,256]{1,0:T(8,128)S(1)} custom-call(bf16[128,5760]{1,0:T(8,128)(2,1)S(1)} %collective-permute-done.12.xc, bf16[64,5632]{1,0:T(8,128)(2,1)S(1)} %get-tuple-element.23.refs_0_, bf16[64,5632]{1,0:T(8,128)(2,1)S(1)} %collective-permute-done.2.refs_1_, bf16[64,5632]{1,0:T(8,128)(2,1)S(1)} %collective-permute-done.3.refs_2_, ...), custom_call_target="tpu_custom_call" | custom-call | tf_op jit(solution)/shard_map/project_last/pallas_call | solution.py:152
  73.7 1.5 %collective-permute-start.13 = (f32[128,256]{1,0:T(8,128)S(1)}, f32[128,256]{1,0:T(8,128)S(1)}, u32[]{:S(2)}, u32[]{:S(2)}) collective-permute-start(f32[128,256]{1,0:T(8,128)S(1)} %project_last.1), channel_id=1, source_target_pairs={{0,17},{1,16},{2,19},{3,18},{4,21},{5,20},{6,23},{7,22},{8,25},{9,... | collective-permute-start | bytes 393224 | tf_op jit(solution)/shard_map/ppermute | solution.py:225
  75.2 0.0 collective-permute-done.10.p1
  75.2 2.2 %collective-permute-done.11.p2 = f32[128,256]{1,0:T(8,128)S(1)} collective-permute-done((f32[128,256]{1,0:T(8,128)S(1)}, f32[128,256]{1,0:T(8,128)S(1)}, u32[]{:S(2)}, u32[]{:S(2)}) %collective-permute-start.11) | collective-permute-done | bytes 131104 | tf_op jit(solution)/shard_map/ppermute | solution.py:225
  77.4 2.2 %collective-permute-done.13.p3 = f32[128,256]{1,0:T(8,128)S(1)} collective-permute-done((f32[128,256]{1,0:T(8,128)S(1)}, f32[128,256]{1,0:T(8,128)S(1)}, u32[]{:S(2)}, u32[]{:S(2)}) %collective-permute-start.13) | collective-permute-done | bytes 131104 | tf_op jit(solution)/shard_map/ppermute | solution.py:225
  79.6 0.4 gram.1.refs_0_
  80.0 1.6 %collective-permute-start.17 = (bf16[16,16,128]{2,1,0:T(8,128)(2,1)S(1)}, bf16[16,16,128]{2,1,0:T(8,128)(2,1)S(1)}, u32[]{:S(2)}, u32[]{:S(2)}) collective-permute-start(bf16[16,16,128]{2,1,0:T(8,128)(2,1)S(1)} %gram.1.refs_0_), channel_id=1, source_target_pairs={{0,2},{1,3},{2,0},{3,1},{4,6},{5,7},{6,4},{7,5},{8,10},{9,11},{10,... | collective-permute-start | bytes 196616 | tf_op jit(solution)/shard_map/ppermute | solution.py:225
  81.6 1.6 %collective-permute-start.16 = (bf16[16,16,128]{2,1,0:T(8,128)(2,1)S(1)}, bf16[16,16,128]{2,1,0:T(8,128)(2,1)S(1)}, u32[]{:S(2)}, u32[]{:S(2)}) collective-permute-start(bf16[16,16,128]{2,1,0:T(8,128)(2,1)S(1)} %gram.1.refs_0_), channel_id=1, source_target_pairs={{0,4},{1,5},{2,6},{3,7},{4,0},{5,1},{6,2},{7,3},{8,12},{9,13},{10,... | collective-permute-start | bytes 196616 | tf_op jit(solution)/shard_map/ppermute | solution.py:225
  83.2 0.0 collective-permute-start.21
  83.2 1.7 %collective-permute-start.15 = (bf16[16,16,128]{2,1,0:T(8,128)(2,1)S(1)}, bf16[16,16,128]{2,1,0:T(8,128)(2,1)S(1)}, u32[]{:S(2)}, u32[]{:S(2)}) collective-permute-start(bf16[16,16,128]{2,1,0:T(8,128)(2,1)S(1)} %gram.1.refs_0_), channel_id=1, source_target_pairs={{0,12},{1,13},{2,14},{3,15},{4,8},{5,9},{6,10},{7,11},{8,4},{9,5},... | collective-permute-start | bytes 196616 | tf_op jit(solution)/shard_map/ppermute | solution.py:225
  84.9 0.6 collective-permute-start.14
  85.5 0.0 collective-permute-done.17.refs_4_
  85.5 0.2 collective-permute-start.25
  85.7 0.1 collective-permute-done.16.refs_3_
  85.9 0.1 collective-permute-start.24
  86.0 0.0 collective-permute-done.21.refs_8_
  86.0 0.5 collective-permute-start.20
  86.5 3.4 %collective-permute-done.15.refs_2_ = bf16[16,16,128]{2,1,0:T(8,128)(2,1)S(1)} collective-permute-done((bf16[16,16,128]{2,1,0:T(8,128)(2,1)S(1)}, bf16[16,16,128]{2,1,0:T(8,128)(2,1)S(1)}, u32[]{:S(2)}, u32[]{:S(2)}) %collective-permute-start.15) | collective-permute-done | bytes 65568 | tf_op jit(solution)/shard_map/ppermute | solution.py:225
  90.0 0.5 collective-permute-start.19
  90.5 1.9 %collective-permute-done.14.refs_1_ = bf16[16,16,128]{2,1,0:T(8,128)(2,1)S(1)} collective-permute-done((bf16[16,16,128]{2,1,0:T(8,128)(2,1)S(1)}, bf16[16,16,128]{2,1,0:T(8,128)(2,1)S(1)}, u32[]{:S(2)}, u32[]{:S(2)}) %collective-permute-start.14) | collective-permute-done | bytes 65568 | tf_op jit(solution)/shard_map/ppermute | solution.py:225
  92.4 0.5 collective-permute-start.18
  92.9 0.0 collective-permute-done.25.refs_12_
  92.9 0.0 collective-permute-start.23
  92.9 0.0 collective-permute-done.24.refs_11_
  92.9 0.5 collective-permute-start.22
  93.5 0.0 collective-permute-done.20.refs_7_
  93.5 0.1 collective-permute-start.28
  93.5 0.7 collective-permute-done.19.refs_6_
  94.2 2.4 %collective-permute-done.18.refs_5_ = bf16[16,16,128]{2,1,0:T(8,128)(2,1)S(1)} collective-permute-done((bf16[16,16,128]{2,1,0:T(8,128)(2,1)S(1)}, bf16[16,16,128]{2,1,0:T(8,128)(2,1)S(1)}, u32[]{:S(2)}, u32[]{:S(2)}) %collective-permute-start.18) | collective-permute-done | bytes 65568 | tf_op jit(solution)/shard_map/ppermute | solution.py:225
  96.7 0.0 collective-permute-start.26
  96.7 0.0 collective-permute-done.23.refs_10_
  96.7 0.0 collective-permute-done.27.refs_14_
  96.7 1.2 %collective-permute-done.26.refs_13_ = bf16[16,16,128]{2,1,0:T(8,128)(2,1)S(1)} collective-permute-done((bf16[16,16,128]{2,1,0:T(8,128)(2,1)S(1)}, bf16[16,16,128]{2,1,0:T(8,128)(2,1)S(1)}, u32[]{:S(2)}, u32[]{:S(2)}) %collective-permute-start.26) | collective-permute-done | bytes 65568 | tf_op jit(solution)/shard_map/ppermute | solution.py:225
  97.9 0.7 precondition.1
  98.6 11.8 %all_to_all.9 = f32[8,16,256]{2,0,1:T(8,128)S(1)} all-to-all(f32[8,16,256]{2,0,1:T(8,128)S(1)} %bitcast.5), channel_id=1, replica_groups=mesh['groups'=2,'dp'=16] {'dp'}, dimensions={1} | all-to-all | bytes 262144 | tf_op jit(solution)/shard_map/all_to_all | solution.py:348
  110.4 0.7 copy.8
  (9 shorter events, 0.1 us)
Async XLA Ops:
  2.0 26.0 %collective-permute-start = (bf16[128,5760]{1,0:T(8,128)(2,1)S(1)}, bf16[128,5760]{1,0:T(8,128)(2,1)S(1)}, u32[]{:S(2)}, u32[]{:S(2)}) collective-permute-start(bf16[128,5760]{1,0:T(8,128)(2,1)S(1)} %get-tuple-element.22), channel_id=1, source_target_pairs={{0,1},{1,0},{2,3},{3,2},{4,5},{5,4},{6,7},{7,6},{8,9},{9,8},{10,11... | collective-permute-start | bytes 4423688 | tf_op jit(solution)/shard_map/ppermute | solution.py:225
  2.6 19.3 %collective-permute-start.2 = (bf16[64,5632]{1,0:T(8,128)(2,1)S(1)}, bf16[64,5632]{1,0:T(8,128)(2,1)S(1)}, u32[]{:S(2)}, u32[]{:S(2)}) collective-permute-start(bf16[64,5632]{1,0:T(8,128)(2,1)S(1)} %get-tuple-element.23.refs_0_), channel_id=1, source_target_pairs={{0,2},{1,3},{2,0},{3,1},{4,6},{5,7},{6,4},{7,5},{8,10},{9,11},{10,... | collective-permute-start | bytes 2162696 | tf_op jit(solution)/shard_map/ppermute | solution.py:225
  5.2 40.0 %collective-permute-start.1 = (bf16[128,5760]{1,0:T(8,128)(2,1)S(1)}, bf16[128,5760]{1,0:T(8,128)(2,1)S(1)}, u32[]{:S(2)}, u32[]{:S(2)}) collective-permute-start(bf16[128,5760]{1,0:T(8,128)(2,1)S(1)} %get-tuple-element.19), channel_id=1, source_target_pairs={{0,16},{1,17},{2,18},{3,19},{4,20},{5,21},{6,22},{7,23},{8,24},{9,... | collective-permute-start | bytes 4423688 | tf_op jit(solution)/shard_map/ppermute | solution.py:225
  6.7 19.8 %collective-permute-start.3 = (bf16[64,5632]{1,0:T(8,128)(2,1)S(1)}, bf16[64,5632]{1,0:T(8,128)(2,1)S(1)}, u32[]{:S(2)}, u32[]{:S(2)}) collective-permute-start(bf16[64,5632]{1,0:T(8,128)(2,1)S(1)} %get-tuple-element.23.refs_0_), channel_id=1, source_target_pairs={{0,4},{1,5},{2,6},{3,7},{4,8},{5,9},{6,10},{7,11},{8,12},{9,13},{1... | collective-permute-start | bytes 2162696 | tf_op jit(solution)/shard_map/ppermute | solution.py:225
  21.9 49.7 %collective-permute-start.12 = (bf16[128,5760]{1,0:T(8,128)(2,1)S(1)}, bf16[128,5760]{1,0:T(8,128)(2,1)S(1)}, u32[]{:S(2)}, u32[]{:S(2)}) collective-permute-start(bf16[128,5760]{1,0:T(8,128)(2,1)S(1)} %get-tuple-element.31), channel_id=1, source_target_pairs={{0,17},{1,16},{2,19},{3,18},{4,21},{5,20},{6,23},{7,22},{8,25},{9,... | collective-permute-start | bytes 4423688 | tf_op jit(solution)/shard_map/ppermute | solution.py:225
  22.9 20.2 %collective-permute-start.5 = (bf16[64,5632]{1,0:T(8,128)(2,1)S(1)}, bf16[64,5632]{1,0:T(8,128)(2,1)S(1)}, u32[]{:S(2)}, u32[]{:S(2)}) collective-permute-start(bf16[64,5632]{1,0:T(8,128)(2,1)S(1)} %get-tuple-element.23.refs_0_), channel_id=1, source_target_pairs={{0,12},{1,13},{2,14},{3,15},{4,0},{5,1},{6,2},{7,3},{8,4},{9,5},{1... | collective-permute-start | bytes 2162696 | tf_op jit(solution)/shard_map/ppermute | solution.py:225
  26.5 18.6 %collective-permute-start.4 = (bf16[64,5632]{1,0:T(8,128)(2,1)S(1)}, bf16[64,5632]{1,0:T(8,128)(2,1)S(1)}, u32[]{:S(2)}, u32[]{:S(2)}) collective-permute-start(bf16[64,5632]{1,0:T(8,128)(2,1)S(1)} %collective-permute-done.3.refs_2_), channel_id=1, source_target_pairs={{0,2},{1,3},{2,0},{3,1},{4,6},{5,7},{6,4},{7,5},{8,10},{9,11},{10,... | collective-permute-start | bytes 2162696 | tf_op jit(solution)/shard_map/ppermute | solution.py:225
  28.0 31.4 %collective-permute-start.7 = (bf16[64,5632]{1,0:T(8,128)(2,1)S(1)}, bf16[64,5632]{1,0:T(8,128)(2,1)S(1)}, u32[]{:S(2)}, u32[]{:S(2)}) collective-permute-start(bf16[64,5632]{1,0:T(8,128)(2,1)S(1)} %collective-permute-done.3.refs_2_), channel_id=1, source_target_pairs={{0,4},{1,5},{2,6},{3,7},{4,8},{5,9},{6,10},{7,11},{8,12},{9,13},{1... | collective-permute-start | bytes 2162696 | tf_op jit(solution)/shard_map/ppermute | solution.py:225
  43.1 17.9 %collective-permute-start.6 = (bf16[64,5632]{1,0:T(8,128)(2,1)S(1)}, bf16[64,5632]{1,0:T(8,128)(2,1)S(1)}, u32[]{:S(2)}, u32[]{:S(2)}) collective-permute-start(bf16[64,5632]{1,0:T(8,128)(2,1)S(1)} %collective-permute-done.5.refs_4_), channel_id=1, source_target_pairs={{0,2},{1,3},{2,0},{3,1},{4,6},{5,7},{6,4},{7,5},{8,10},{9,11},{10,... | collective-permute-start | bytes 2162696 | tf_op jit(solution)/shard_map/ppermute | solution.py:225
  45.1 21.8 %collective-permute-start.9 = (bf16[32,5632]{1,0:T(8,128)(2,1)S(1)}, bf16[32,5632]{1,0:T(8,128)(2,1)S(1)}, u32[]{:S(2)}, u32[]{:S(2)}) collective-permute-start(bf16[32,5632]{1,0:T(8,128)(2,1)S(1)} %slice.8), channel_id=1, source_target_pairs={{0,4},{1,5},{2,6},{3,7},{4,8},{5,9},{6,10},{7,11},{8,12},{9,13},{1... | collective-permute-start | bytes 1081352 | tf_op jit(solution)/shard_map/ppermute | solution.py:225
  59.4 10.3 %collective-permute-start.8 = (bf16[32,5632]{1,0:T(8,128)(2,1)S(1)}, bf16[32,5632]{1,0:T(8,128)(2,1)S(1)}, u32[]{:S(2)}, u32[]{:S(2)}) collective-permute-start(bf16[32,5632]{1,0:T(8,128)(2,1)S(1)} %slice.6), channel_id=1, source_target_pairs={{0,2},{1,3},{2,0},{3,1},{4,6},{5,7},{6,4},{7,5},{8,10},{9,11},{10,... | collective-permute-start | bytes 1081352 | tf_op jit(solution)/shard_map/ppermute | solution.py:225
  71.1 4.1 %collective-permute-start.10 = (f32[128,256]{1,0:T(8,128)S(1)}, f32[128,256]{1,0:T(8,128)S(1)}, u32[]{:S(2)}, u32[]{:S(2)}) collective-permute-start(f32[128,256]{1,0:T(8,128)S(1)} %get-tuple-element.28), channel_id=1, source_target_pairs={{0,1},{1,0},{2,3},{3,2},{4,5},{5,4},{6,7},{7,6},{8,9},{9,8},{10,11... | collective-permute-start | bytes 393224 | tf_op jit(solution)/shard_map/ppermute | solution.py:225
  71.2 6.2 %collective-permute-start.11 = (f32[128,256]{1,0:T(8,128)S(1)}, f32[128,256]{1,0:T(8,128)S(1)}, u32[]{:S(2)}, u32[]{:S(2)}) collective-permute-start(f32[128,256]{1,0:T(8,128)S(1)} %get-tuple-element.29), channel_id=1, source_target_pairs={{0,16},{1,17},{2,18},{3,19},{4,20},{5,21},{6,22},{7,23},{8,24},{9,... | collective-permute-start | bytes 393224 | tf_op jit(solution)/shard_map/ppermute | solution.py:225
  71.6 8.0 %copy-start.1 = (s32[128,2]{0,1:T(2,128)S(1)}, s32[128,2]{0,1:T(2,128)}, u32[]{:S(2)}) copy-start(s32[128,2]{0,1:T(2,128)} %param.8) | copy-start | bytes 3076
  71.6 26.3 %copy-start = (bf16[4096,256]{1,0:T(8,128)(2,1)S(1)}, bf16[4096,256]{1,0:T(8,128)(2,1)}, u32[]{:S(2)}) copy-start(bf16[4096,256]{1,0:T(8,128)(2,1)} %refs_16_.1) | copy-start | bytes 6291460
  73.7 5.9 %collective-permute-start.13 = (f32[128,256]{1,0:T(8,128)S(1)}, f32[128,256]{1,0:T(8,128)S(1)}, u32[]{:S(2)}, u32[]{:S(2)}) collective-permute-start(f32[128,256]{1,0:T(8,128)S(1)} %project_last.1), channel_id=1, source_target_pairs={{0,17},{1,16},{2,19},{3,18},{4,21},{5,20},{6,23},{7,22},{8,25},{9,... | collective-permute-start | bytes 393224 | tf_op jit(solution)/shard_map/ppermute | solution.py:225
  80.0 5.5 %collective-permute-start.17 = (bf16[16,16,128]{2,1,0:T(8,128)(2,1)S(1)}, bf16[16,16,128]{2,1,0:T(8,128)(2,1)S(1)}, u32[]{:S(2)}, u32[]{:S(2)}) collective-permute-start(bf16[16,16,128]{2,1,0:T(8,128)(2,1)S(1)} %gram.1.refs_0_), channel_id=1, source_target_pairs={{0,2},{1,3},{2,0},{3,1},{4,6},{5,7},{6,4},{7,5},{8,10},{9,11},{10,... | collective-permute-start | bytes 196616 | tf_op jit(solution)/shard_map/ppermute | solution.py:225
  81.6 4.3 %collective-permute-start.16 = (bf16[16,16,128]{2,1,0:T(8,128)(2,1)S(1)}, bf16[16,16,128]{2,1,0:T(8,128)(2,1)S(1)}, u32[]{:S(2)}, u32[]{:S(2)}) collective-permute-start(bf16[16,16,128]{2,1,0:T(8,128)(2,1)S(1)} %gram.1.refs_0_), channel_id=1, source_target_pairs={{0,4},{1,5},{2,6},{3,7},{4,0},{5,1},{6,2},{7,3},{8,12},{9,13},{10,... | collective-permute-start | bytes 196616 | tf_op jit(solution)/shard_map/ppermute | solution.py:225
  83.2 2.8 %collective-permute-start.21 = (bf16[16,16,128]{2,1,0:T(8,128)(2,1)S(1)}, bf16[16,16,128]{2,1,0:T(8,128)(2,1)S(1)}, u32[]{:S(2)}, u32[]{:S(2)}) collective-permute-start(bf16[16,16,128]{2,1,0:T(8,128)(2,1)S(1)} %gram.1.refs_0_), channel_id=1, source_target_pairs={{0,1},{1,0},{2,3},{3,2},{4,5},{5,4},{6,7},{7,6},{8,9},{9,8},{10,11... | collective-permute-start | bytes 196616 | tf_op jit(solution)/shard_map/ppermute | solution.py:225
  83.2 6.8 %collective-permute-start.15 = (bf16[16,16,128]{2,1,0:T(8,128)(2,1)S(1)}, bf16[16,16,128]{2,1,0:T(8,128)(2,1)S(1)}, u32[]{:S(2)}, u32[]{:S(2)}) collective-permute-start(bf16[16,16,128]{2,1,0:T(8,128)(2,1)S(1)} %gram.1.refs_0_), channel_id=1, source_target_pairs={{0,12},{1,13},{2,14},{3,15},{4,8},{5,9},{6,10},{7,11},{8,4},{9,5},... | collective-permute-start | bytes 196616 | tf_op jit(solution)/shard_map/ppermute | solution.py:225
  84.9 7.5 %collective-permute-start.14 = (bf16[16,16,128]{2,1,0:T(8,128)(2,1)S(1)}, bf16[16,16,128]{2,1,0:T(8,128)(2,1)S(1)}, u32[]{:S(2)}, u32[]{:S(2)}) collective-permute-start(bf16[16,16,128]{2,1,0:T(8,128)(2,1)S(1)} %gram.1.refs_0_), channel_id=1, source_target_pairs={{0,8},{1,9},{2,10},{3,11},{4,12},{5,13},{6,14},{7,15},{8,0},{9,1},... | collective-permute-start | bytes 196616 | tf_op jit(solution)/shard_map/ppermute | solution.py:225
  85.5 7.5 %collective-permute-start.25 = (bf16[16,16,128]{2,1,0:T(8,128)(2,1)S(1)}, bf16[16,16,128]{2,1,0:T(8,128)(2,1)S(1)}, u32[]{:S(2)}, u32[]{:S(2)}) collective-permute-start(bf16[16,16,128]{2,1,0:T(8,128)(2,1)S(1)} %collective-permute-done.17.refs_4_), channel_id=1, source_target_pairs={{0,1},{1,0},{2,3},{3,2},{4,5},{5,4},{6,7},{7,6},{8,9},{9,8},{10,11... | collective-permute-start | bytes 196616 | tf_op jit(solution)/shard_map/ppermute | solution.py:225
  85.9 7.1 %collective-permute-start.24 = (bf16[16,16,128]{2,1,0:T(8,128)(2,1)S(1)}, bf16[16,16,128]{2,1,0:T(8,128)(2,1)S(1)}, u32[]{:S(2)}, u32[]{:S(2)}) collective-permute-start(bf16[16,16,128]{2,1,0:T(8,128)(2,1)S(1)} %collective-permute-done.16.refs_3_), channel_id=1, source_target_pairs={{0,1},{1,0},{2,3},{3,2},{4,5},{5,4},{6,7},{7,6},{8,9},{9,8},{10,11... | collective-permute-start | bytes 196616 | tf_op jit(solution)/shard_map/ppermute | solution.py:225
  86.0 7.5 %collective-permute-start.20 = (bf16[16,16,128]{2,1,0:T(8,128)(2,1)S(1)}, bf16[16,16,128]{2,1,0:T(8,128)(2,1)S(1)}, u32[]{:S(2)}, u32[]{:S(2)}) collective-permute-start(bf16[16,16,128]{2,1,0:T(8,128)(2,1)S(1)} %collective-permute-done.16.refs_3_), channel_id=1, source_target_pairs={{0,2},{1,3},{2,0},{3,1},{4,6},{5,7},{6,4},{7,5},{8,10},{9,11},{10,... | collective-permute-start | bytes 196616 | tf_op jit(solution)/shard_map/ppermute | solution.py:225
  90.0 4.3 %collective-permute-start.19 = (bf16[16,16,128]{2,1,0:T(8,128)(2,1)S(1)}, bf16[16,16,128]{2,1,0:T(8,128)(2,1)S(1)}, u32[]{:S(2)}, u32[]{:S(2)}) collective-permute-start(bf16[16,16,128]{2,1,0:T(8,128)(2,1)S(1)} %collective-permute-done.15.refs_2_), channel_id=1, source_target_pairs={{0,2},{1,3},{2,0},{3,1},{4,6},{5,7},{6,4},{7,5},{8,10},{9,11},{10,... | collective-permute-start | bytes 196616 | tf_op jit(solution)/shard_map/ppermute | solution.py:225
  92.4 4.3 %collective-permute-start.18 = (bf16[16,16,128]{2,1,0:T(8,128)(2,1)S(1)}, bf16[16,16,128]{2,1,0:T(8,128)(2,1)S(1)}, u32[]{:S(2)}, u32[]{:S(2)}) collective-permute-start(bf16[16,16,128]{2,1,0:T(8,128)(2,1)S(1)} %collective-permute-done.14.refs_1_), channel_id=1, source_target_pairs={{0,2},{1,3},{2,0},{3,1},{4,6},{5,7},{6,4},{7,5},{8,10},{9,11},{10,... | collective-permute-start | bytes 196616 | tf_op jit(solution)/shard_map/ppermute | solution.py:225
  92.9 3.8 %collective-permute-start.23 = (bf16[16,16,128]{2,1,0:T(8,128)(2,1)S(1)}, bf16[16,16,128]{2,1,0:T(8,128)(2,1)S(1)}, u32[]{:S(2)}, u32[]{:S(2)}) collective-permute-start(bf16[16,16,128]{2,1,0:T(8,128)(2,1)S(1)} %collective-permute-done.15.refs_2_), channel_id=1, source_target_pairs={{0,1},{1,0},{2,3},{3,2},{4,5},{5,4},{6,7},{7,6},{8,9},{9,8},{10,11... | collective-permute-start | bytes 196616 | tf_op jit(solution)/shard_map/ppermute | solution.py:225
  92.9 3.7 %collective-permute-start.22 = (bf16[16,16,128]{2,1,0:T(8,128)(2,1)S(1)}, bf16[16,16,128]{2,1,0:T(8,128)(2,1)S(1)}, u32[]{:S(2)}, u32[]{:S(2)}) collective-permute-start(bf16[16,16,128]{2,1,0:T(8,128)(2,1)S(1)} %collective-permute-done.14.refs_1_), channel_id=1, source_target_pairs={{0,1},{1,0},{2,3},{3,2},{4,5},{5,4},{6,7},{7,6},{8,9},{9,8},{10,11... | collective-permute-start | bytes 196616 | tf_op jit(solution)/shard_map/ppermute | solution.py:225
  93.5 3.2 %collective-permute-start.28 = (bf16[16,16,128]{2,1,0:T(8,128)(2,1)S(1)}, bf16[16,16,128]{2,1,0:T(8,128)(2,1)S(1)}, u32[]{:S(2)}, u32[]{:S(2)}) collective-permute-start(bf16[16,16,128]{2,1,0:T(8,128)(2,1)S(1)} %collective-permute-done.20.refs_7_), channel_id=1, source_target_pairs={{0,1},{1,0},{2,3},{3,2},{4,5},{5,4},{6,7},{7,6},{8,9},{9,8},{10,11... | collective-permute-start | bytes 196616 | tf_op jit(solution)/shard_map/ppermute | solution.py:225
  94.2 2.5 %collective-permute-start.27 = (bf16[16,16,128]{2,1,0:T(8,128)(2,1)S(1)}, bf16[16,16,128]{2,1,0:T(8,128)(2,1)S(1)}, u32[]{:S(2)}, u32[]{:S(2)}) collective-permute-start(bf16[16,16,128]{2,1,0:T(8,128)(2,1)S(1)} %collective-permute-done.19.refs_6_), channel_id=1, source_target_pairs={{0,1},{1,0},{2,3},{3,2},{4,5},{5,4},{6,7},{7,6},{8,9},{9,8},{10,11... | collective-permute-start | bytes 196616 | tf_op jit(solution)/shard_map/ppermute | solution.py:225
  96.7 1.3 %collective-permute-start.26 = (bf16[16,16,128]{2,1,0:T(8,128)(2,1)S(1)}, bf16[16,16,128]{2,1,0:T(8,128)(2,1)S(1)}, u32[]{:S(2)}, u32[]{:S(2)}) collective-permute-start(bf16[16,16,128]{2,1,0:T(8,128)(2,1)S(1)} %collective-permute-done.18.refs_5_), channel_id=1, source_target_pairs={{0,1},{1,0},{2,3},{3,2},{4,5},{5,4},{6,7},{7,6},{8,9},{9,8},{10,11... | collective-permute-start | bytes 196616 | tf_op jit(solution)/shard_map/ppermute | solution.py:225

commit v7 on v6

--- a/solution.py
+++ b/solution.py
@@ -185,28 +185,30 @@
 
 
 def fisher_kernel(steps, *refs):
-    fisher, out_ref = refs[-2:]
-    n = 2 * len(steps)
+    n = len(steps)
+    tables, out_ref = refs[n : n + 2], refs[n + 2]
     core, chip, _ = position()
-    total = jnp.zeros((n * EXPERTS, fisher.shape[1]), jnp.float32)
+    width = tables[0].shape[1]
+    totals = [jnp.zeros((n * EXPERTS, width), jnp.float32) for _ in tables]
     for i in range(PROJ // 4):
         rows = jnp.concatenate([x[i].astype(jnp.float32).reshape(1, 2, EXPERTS, LANES) for x in refs[:n]], axis=0)
         for h in range(2):
             p = 2 * i + h
-            table = jnp.concatenate(
-                [
-                    fisher[p * PROJ : (p + 1) * PROJ, :],
-                    fisher[(PROJ // 2 + p) * PROJ : (PROJ // 2 + p + 1) * PROJ, :],
-                ],
-                axis=0,
-            )
             lhs = rows[:, h].reshape(n * EXPERTS, LANES).astype(jnp.bfloat16)
-            total += jnp.dot(lhs, table, preferred_element_type=jnp.float32)
-    width = fisher.shape[1]
-    for j in range(n):
-        owner = 2 * jnp.bitwise_xor(chip, steps[j % len(steps)]) + (core if j < len(steps) else 1 - core)
-        at = pl.multiple_of(owner * width, LANES)
-        out_ref[:, pl.ds(at, width)] = total[j * EXPERTS : (j + 1) * EXPERTS]
+            for k, fisher in enumerate(tables):
+                table = jnp.concatenate(
+                    [
+                        fisher[p * PROJ : (p + 1) * PROJ, :],
+                        fisher[(PROJ // 2 + p) * PROJ : (PROJ // 2 + p + 1) * PROJ, :],
+                    ],
+                    axis=0,
+                )
+                totals[k] += jnp.dot(lhs, table, preferred_element_type=jnp.float32)
+    for j, step in enumerate(steps):
+        for k, total in enumerate(totals):
+            place = 2 * jnp.bitwise_xor(chip, step) + (1 - core if k else core)
+            at = pl.multiple_of(place * width, LANES)
+            out_ref[:, pl.ds(at, width)] = total[j * EXPERTS : (j + 1) * EXPERTS]
 
 
 def shards(features, grads, routes, proj_in, proj_out, fisher_inverse):
@@ -329,6 +331,7 @@
         sums + [routes.reshape(1, -1)],
     )
 
+    fisher_other = move(after(fisher_inverse, mine), to_core)
     def far(step):
         return lambda g, d: (g, d ^ (2 * step))
 
@@ -343,9 +346,12 @@
         functools.partial(fisher_kernel, steps),
         "precondition",
         jax.ShapeDtypeStruct((EXPERTS, PROJ * PROJ), f32),
-        grams + [move(x, to_core) for x in grams] + [fisher_inverse],
-    )
-    result = lax.all_to_all(columns, "dp", split_axis=1, concat_axis=1, tiled=True)
+        grams + [fisher_inverse, fisher_other],
+    )
+    same_core = [list(range(c, n, 2)) for c in range(2)]
+    result = lax.all_to_all(
+        columns, "dp", split_axis=1, concat_axis=1, axis_index_groups=same_core, tiled=True
+    )
     return result.reshape(1, EXPERTS, PROJ * PROJ)
 
 

time: 111 us -> 109 us (0.982)
  waiting for transfers between devices: 62.1 us -> 57.9 us
  starting transfers between devices: 25.4 us -> 26.6 us
    ppermute x29 -> x22, waiting for transfers between devices: 62.1 us -> 57.9 us  [move(): return lax.ppermute(x, AXES, pairs)]
    ppermute x29 -> x22, starting transfers between devices: 25.4 us -> 26.6 us  [move(): return lax.ppermute(x, AXES, pairs)]
  transfers between devices with their start and end apart: 29 -> 22, of which waited for: 14 -> 12; matrix products, arithmetic and copies ran while one was open for 0% -> 0% of each run, Pallas kernels for 7% -> 7%
where the time goes in v7:
time: 109 us; the launch traced here: 108 us
  waiting for transfers between devices  57.9 us (53%)
  starting transfers between devices  26.6 us (24%)
  blocking collectives  12 us (11%)
  Pallas kernels  10.9 us (10%)
    ppermute x22, waiting for transfers between devices, move(): return lax.ppermute(x, AXES, pairs)  57.9 us
    ppermute x22, starting transfers between devices, move(): return lax.ppermute(x, AXES, pairs)  26.6 us
    all_to_all x1, blocking collectives, shards(): lax.all_to_all(columns, 'dp', split_axis=1, concat_axis=1, axis_index_gro...  12 us
    pallas_call x5, Pallas kernels, local(): pl.pallas_call(kernel, in_specs=[vmem] * len(operands), out_specs=jax.tre...  7.08 us
    pallas_call x2, Pallas kernels, pack(): pl.pallas_call(functools.partial(pack_kernel, [[b[1:] for b in out] for o...  3.85 us
  transfers between devices with their start and end apart: 22, of which 12 were waited for; matrix products, arithmetic and copies ran while one was open for 0% of the time, Pallas kernels for 7%

profile of v7, /device:TPU:0, one launch (start us, length us, event | category | flops | bytes accessed | tf_op | source)
XLA Modules:
  0.0 108.3 jit_solution(1959614293021375570)
XLA Ops:
  0.0 2.0 %pack_first.1 = (bf16[64,5632]{1,0:T(8,128)(2,1)S(1)}, bf16[128,5760]{1,0:T(8,128)(2,1)S(1)}, bf16[128,5760]{1,0:T(8,128)(2,1)S(1)}) custom-call(s32[2,128]{1,0:T(2,128)} %bitcast.6, bf16[64,8192]{1,0:T(8,128)(2,1)} %refs_0_.2, bf16[64,3072]{1,0:T(8,128)(2,1)} %refs_1_.2, bf16[128,16384]{1,0:T(8,128)(2,1)} %refs_2_.3, bf16[128,6144]{1,0:T(8,128)(2,1)} %refs_3_.3, ...), custom_call_target="tpu_custom_call" | custom-call | tf_op jit(solution)/shard_map/pack_first/pallas_call | solution.py:139
  2.0 0.5 collective-permute-start
  2.6 2.6 %collective-permute-start.2 = (bf16[64,5632]{1,0:T(8,128)(2,1)S(1)}, bf16[64,5632]{1,0:T(8,128)(2,1)S(1)}, u32[]{:S(2)}, u32[]{:S(2)}) collective-permute-start(bf16[64,5632]{1,0:T(8,128)(2,1)S(1)} %get-tuple-element.24.refs_0_), channel_id=1, source_target_pairs={{0,2},{1,3},{2,0},{3,1},{4,6},{5,7},{6,4},{7,5},{8,10},{9,11},{10,... | collective-permute-start | bytes 2162696 | tf_op jit(solution)/shard_map/ppermute | solution.py:227
  5.2 1.5 %collective-permute-start.1 = (bf16[128,5760]{1,0:T(8,128)(2,1)S(1)}, bf16[128,5760]{1,0:T(8,128)(2,1)S(1)}, u32[]{:S(2)}, u32[]{:S(2)}) collective-permute-start(bf16[128,5760]{1,0:T(8,128)(2,1)S(1)} %get-tuple-element.20), channel_id=1, source_target_pairs={{0,16},{1,17},{2,18},{3,19},{4,20},{5,21},{6,22},{7,23},{8,24},{9,... | collective-permute-start | bytes 4423688 | tf_op jit(solution)/shard_map/ppermute | solution.py:227
  6.7 1.6 %collective-permute-start.3 = (bf16[64,5632]{1,0:T(8,128)(2,1)S(1)}, bf16[64,5632]{1,0:T(8,128)(2,1)S(1)}, u32[]{:S(2)}, u32[]{:S(2)}) collective-permute-start(bf16[64,5632]{1,0:T(8,128)(2,1)S(1)} %get-tuple-element.24.refs_0_), channel_id=1, source_target_pairs={{0,4},{1,5},{2,6},{3,7},{4,8},{5,9},{6,10},{7,11},{8,12},{9,13},{1... | collective-permute-start | bytes 2162696 | tf_op jit(solution)/shard_map/ppermute | solution.py:227
  8.2 1.8 %pack_second.1 = (bf16[128,5760]{1,0:T(8,128)(2,1)S(1)}, bf16[128,5760]{1,0:T(8,128)(2,1)S(1)}) custom-call(s32[2,128]{1,0:T(2,128)} %bitcast.7, bf16[128,16384]{1,0:T(8,128)(2,1)} %refs_2_.3, bf16[128,6144]{1,0:T(8,128)(2,1)} %refs_3_.3, bf16[128,16384]{1,0:T(8,128)(2,1)} %refs_2_.3, bf16[128,6144]{1,0:T(8,128)(2,1)} %refs_3_.3), custom_call_target="tpu_custom_call" | custom-call | tf_op jit(solution)/shard_map/pack_second/pallas_call | solution.py:139
  10.0 11.8 %collective-permute-done.2.refs_1_ = bf16[64,5632]{1,0:T(8,128)(2,1)S(1)} collective-permute-done((bf16[64,5632]{1,0:T(8,128)(2,1)S(1)}, bf16[64,5632]{1,0:T(8,128)(2,1)S(1)}, u32[]{:S(2)}, u32[]{:S(2)}) %collective-permute-start.2) | collective-permute-done | bytes 720928 | tf_op jit(solution)/shard_map/ppermute | solution.py:227
  21.9 1.0 collective-permute-start.12
  22.9 3.6 %collective-permute-start.5 = (bf16[64,5632]{1,0:T(8,128)(2,1)S(1)}, bf16[64,5632]{1,0:T(8,128)(2,1)S(1)}, u32[]{:S(2)}, u32[]{:S(2)}) collective-permute-start(bf16[64,5632]{1,0:T(8,128)(2,1)S(1)} %get-tuple-element.24.refs_0_), channel_id=1, source_target_pairs={{0,12},{1,13},{2,14},{3,15},{4,0},{5,1},{6,2},{7,3},{8,4},{9,5},{1... | collective-permute-start | bytes 2162696 | tf_op jit(solution)/shard_map/ppermute | solution.py:227
  26.5 0.0 collective-permute-done.3.refs_2_
  26.5 1.5 %collective-permute-start.4 = (bf16[64,5632]{1,0:T(8,128)(2,1)S(1)}, bf16[64,5632]{1,0:T(8,128)(2,1)S(1)}, u32[]{:S(2)}, u32[]{:S(2)}) collective-permute-start(bf16[64,5632]{1,0:T(8,128)(2,1)S(1)} %collective-permute-done.3.refs_2_), channel_id=1, source_target_pairs={{0,2},{1,3},{2,0},{3,1},{4,6},{5,7},{6,4},{7,5},{8,10},{9,11},{10,... | collective-permute-start | bytes 2162696 | tf_op jit(solution)/shard_map/ppermute | solution.py:227
  28.0 0.0 collective-permute-done.other
  28.0 0.0 collective-permute-start.7
  28.0 15.0 %collective-permute-done.5.refs_4_ = bf16[64,5632]{1,0:T(8,128)(2,1)S(1)} collective-permute-done((bf16[64,5632]{1,0:T(8,128)(2,1)S(1)}, bf16[64,5632]{1,0:T(8,128)(2,1)S(1)}, u32[]{:S(2)}, u32[]{:S(2)}) %collective-permute-start.5) | collective-permute-done | bytes 720928 | tf_op jit(solution)/shard_map/ppermute | solution.py:227
  43.1 1.5 %collective-permute-start.6 = (bf16[64,5632]{1,0:T(8,128)(2,1)S(1)}, bf16[64,5632]{1,0:T(8,128)(2,1)S(1)}, u32[]{:S(2)}, u32[]{:S(2)}) collective-permute-start(bf16[64,5632]{1,0:T(8,128)(2,1)S(1)} %collective-permute-done.5.refs_4_), channel_id=1, source_target_pairs={{0,2},{1,3},{2,0},{3,1},{4,6},{5,7},{6,4},{7,5},{8,10},{9,11},{10,... | collective-permute-start | bytes 2162696 | tf_op jit(solution)/shard_map/ppermute | solution.py:227
  44.6 0.5 collective-permute-done.4.refs_3_
  45.1 0.1 collective-permute-start.9
  45.2 0.0 collective-permute-done.1.x
  45.2 14.2 %collective-permute-done.7.refs_0_.refs_6_ = bf16[64,5632]{1,0:T(8,128)(2,1)S(1)} collective-permute-done((bf16[64,5632]{1,0:T(8,128)(2,1)S(1)}, bf16[64,5632]{1,0:T(8,128)(2,1)S(1)}, u32[]{:S(2)}, u32[]{:S(2)}) %collective-permute-start.7) | collective-permute-done | bytes 720928 | tf_op jit(solution)/shard_map/ppermute | solution.py:227
  59.4 1.6 %collective-permute-start.8 = (bf16[32,5632]{1,0:T(8,128)(2,1)S(1)}, bf16[32,5632]{1,0:T(8,128)(2,1)S(1)}, u32[]{:S(2)}, u32[]{:S(2)}) collective-permute-start(bf16[32,5632]{1,0:T(8,128)(2,1)S(1)} %slice.6), channel_id=1, source_target_pairs={{0,2},{1,3},{2,0},{3,1},{4,6},{5,7},{6,4},{7,5},{8,10},{9,11},{10,... | collective-permute-start | bytes 1081352 | tf_op jit(solution)/shard_map/ppermute | solution.py:227
  61.0 0.0 collective-permute-done.6.refs_5_
  61.0 2.5 %project_early.1.early_ref = f32[3,128,256]{2,1,0:T(8,128)S(1)} custom-call(bf16[128,5760]{1,0:T(8,128)(2,1)S(1)} %get-tuple-element.22.own, bf16[128,5760]{1,0:T(8,128)(2,1)S(1)} %collective-permute-done.other, bf16[128,5760]{1,0:T(8,128)(2,1)S(1)} %collective-permute-done.1.x, bf16[64,5632]{1,0:T(8,128)(2,1)S(1)} %get-tuple-element.24.refs_0_, ...), custom_call_target="tpu_custom_call" | custom-call | tf_op jit(solution)/shard_map/project_early/pallas_call | solution.py:152
  63.5 3.5 %collective-permute-done.9.refs_2_.refs_8_ = bf16[32,5632]{1,0:T(8,128)(2,1)S(1)} collective-permute-done((bf16[32,5632]{1,0:T(8,128)(2,1)S(1)}, bf16[32,5632]{1,0:T(8,128)(2,1)S(1)}, u32[]{:S(2)}, u32[]{:S(2)}) %collective-permute-start.9) | collective-permute-done | bytes 360480 | tf_op jit(solution)/shard_map/ppermute | solution.py:227
  67.0 2.7 %collective-permute-done.8.refs_1_.refs_7_ = bf16[32,5632]{1,0:T(8,128)(2,1)S(1)} collective-permute-done((bf16[32,5632]{1,0:T(8,128)(2,1)S(1)}, bf16[32,5632]{1,0:T(8,128)(2,1)S(1)}, u32[]{:S(2)}, u32[]{:S(2)}) %collective-permute-start.8) | collective-permute-done | bytes 360480 | tf_op jit(solution)/shard_map/ppermute | solution.py:227
  69.7 1.4 %project_late.1 = (f32[128,256]{1,0:T(8,128)S(1)}, f32[128,256]{1,0:T(8,128)S(1)}, f32[128,256]{1,0:T(8,128)S(1)}) custom-call(bf16[128,5760]{1,0:T(8,128)(2,1)S(1)} %get-tuple-element.22.own, bf16[128,5760]{1,0:T(8,128)(2,1)S(1)} %collective-permute-done.other, bf16[128,5760]{1,0:T(8,128)(2,1)S(1)} %collective-permute-done.1.x, ...), custom_call_target="tpu_custom_call" | custom-call | tf_op jit(solution)/shard_map/project_late/pallas_call | solution.py:152
  71.1 0.1 collective-permute-start.10
  71.2 0.4 collective-permute-start.11
  71.6 0.0 collective-permute-done.12.xc
  71.6 0.0 copy-start.1
  71.6 0.0 copy-start
  71.6 2.0 %project_last.1 = f32[128,256]{1,0:T(8,128)S(1)} custom-call(bf16[128,5760]{1,0:T(8,128)(2,1)S(1)} %collective-permute-done.12.xc, bf16[64,5632]{1,0:T(8,128)(2,1)S(1)} %get-tuple-element.24.refs_0_, bf16[64,5632]{1,0:T(8,128)(2,1)S(1)} %collective-permute-done.2.refs_1_, bf16[64,5632]{1,0:T(8,128)(2,1)S(1)} %collective-permute-done.3.refs_2_, ...), custom_call_target="tpu_custom_call" | custom-call | tf_op jit(solution)/shard_map/project_last/pallas_call | solution.py:152
  73.7 1.5 %collective-permute-start.13 = (f32[128,256]{1,0:T(8,128)S(1)}, f32[128,256]{1,0:T(8,128)S(1)}, u32[]{:S(2)}, u32[]{:S(2)}) collective-permute-start(f32[128,256]{1,0:T(8,128)S(1)} %project_last.1), channel_id=1, source_target_pairs={{0,17},{1,16},{2,19},{3,18},{4,21},{5,20},{6,23},{7,22},{8,25},{9,... | collective-permute-start | bytes 393224 | tf_op jit(solution)/shard_map/ppermute | solution.py:227
  75.2 0.0 collective-permute-done.10.p1
  75.2 2.2 %collective-permute-done.11.p2 = f32[128,256]{1,0:T(8,128)S(1)} collective-permute-done((f32[128,256]{1,0:T(8,128)S(1)}, f32[128,256]{1,0:T(8,128)S(1)}, u32[]{:S(2)}, u32[]{:S(2)}) %collective-permute-start.11) | collective-permute-done | bytes 131104 | tf_op jit(solution)/shard_map/ppermute | solution.py:227
  77.4 2.2 %collective-permute-done.13.p3 = f32[128,256]{1,0:T(8,128)S(1)} collective-permute-done((f32[128,256]{1,0:T(8,128)S(1)}, f32[128,256]{1,0:T(8,128)S(1)}, u32[]{:S(2)}, u32[]{:S(2)}) %collective-permute-start.13) | collective-permute-done | bytes 131104 | tf_op jit(solution)/shard_map/ppermute | solution.py:227
  79.6 0.0 copy-done.1
  79.6 0.4 gram.1.refs_0_
  80.0 0.0 copy-done
  80.0 0.2 collective-permute-start.21
  80.2 1.6 %collective-permute-start.16 = (bf16[16,16,128]{2,1,0:T(8,128)(2,1)S(1)}, bf16[16,16,128]{2,1,0:T(8,128)(2,1)S(1)}, u32[]{:S(2)}, u32[]{:S(2)}) collective-permute-start(bf16[16,16,128]{2,1,0:T(8,128)(2,1)S(1)} %gram.1.refs_0_), channel_id=1, source_target_pairs={{0,4},{1,5},{2,6},{3,7},{4,0},{5,1},{6,2},{7,3},{8,12},{9,13},{10,... | collective-permute-start | bytes 196616 | tf_op jit(solution)/shard_map/ppermute | solution.py:227
  81.9 1.7 %collective-permute-start.15 = (bf16[16,16,128]{2,1,0:T(8,128)(2,1)S(1)}, bf16[16,16,128]{2,1,0:T(8,128)(2,1)S(1)}, u32[]{:S(2)}, u32[]{:S(2)}) collective-permute-start(bf16[16,16,128]{2,1,0:T(8,128)(2,1)S(1)} %gram.1.refs_0_), channel_id=1, source_target_pairs={{0,12},{1,13},{2,14},{3,15},{4,8},{5,9},{6,10},{7,11},{8,4},{9,5},... | collective-permute-start | bytes 196616 | tf_op jit(solution)/shard_map/ppermute | solution.py:227
  83.6 0.6 collective-permute-start.14
  84.1 1.5 %collective-permute-start.17 = (bf16[16,16,128]{2,1,0:T(8,128)(2,1)S(1)}, bf16[16,16,128]{2,1,0:T(8,128)(2,1)S(1)}, u32[]{:S(2)}, u32[]{:S(2)}) collective-permute-start(bf16[16,16,128]{2,1,0:T(8,128)(2,1)S(1)} %gram.1.refs_0_), channel_id=1, source_target_pairs={{0,2},{1,3},{2,0},{3,1},{4,6},{5,7},{6,4},{7,5},{8,10},{9,11},{10,... | collective-permute-start | bytes 196616 | tf_op jit(solution)/shard_map/ppermute | solution.py:227
  85.6 0.0 collective-permute-done.16.refs_3_
  85.6 0.5 collective-permute-start.20
  86.2 2.3 %collective-permute-done.15.refs_2_ = bf16[16,16,128]{2,1,0:T(8,128)(2,1)S(1)} collective-permute-done((bf16[16,16,128]{2,1,0:T(8,128)(2,1)S(1)}, bf16[16,16,128]{2,1,0:T(8,128)(2,1)S(1)}, u32[]{:S(2)}, u32[]{:S(2)}) %collective-permute-start.15) | collective-permute-done | bytes 65568 | tf_op jit(solution)/shard_map/ppermute | solution.py:227
  88.4 1.5 %collective-permute-start.19 = (bf16[16,16,128]{2,1,0:T(8,128)(2,1)S(1)}, bf16[16,16,128]{2,1,0:T(8,128)(2,1)S(1)}, u32[]{:S(2)}, u32[]{:S(2)}) collective-permute-start(bf16[16,16,128]{2,1,0:T(8,128)(2,1)S(1)} %collective-permute-done.15.refs_2_), channel_id=1, source_target_pairs={{0,2},{1,3},{2,0},{3,1},{4,6},{5,7},{6,4},{7,5},{8,10},{9,11},{10,... | collective-permute-start | bytes 196616 | tf_op jit(solution)/shard_map/ppermute | solution.py:227
  90.0 0.7 collective-permute-done.14.refs_1_
  90.7 1.5 %collective-permute-start.18 = (bf16[16,16,128]{2,1,0:T(8,128)(2,1)S(1)}, bf16[16,16,128]{2,1,0:T(8,128)(2,1)S(1)}, u32[]{:S(2)}, u32[]{:S(2)}) collective-permute-start(bf16[16,16,128]{2,1,0:T(8,128)(2,1)S(1)} %collective-permute-done.14.refs_1_), channel_id=1, source_target_pairs={{0,2},{1,3},{2,0},{3,1},{4,6},{5,7},{6,4},{7,5},{8,10},{9,11},{10,... | collective-permute-start | bytes 196616 | tf_op jit(solution)/shard_map/ppermute | solution.py:227
  92.2 0.0 collective-permute-done.17.refs_4_
  92.2 0.0 collective-permute-done.20.refs_7_
  92.2 0.5 collective-permute-done.19.refs_6_
  92.7 2.2 %collective-permute-done.18.refs_5_ = bf16[16,16,128]{2,1,0:T(8,128)(2,1)S(1)} collective-permute-done((bf16[16,16,128]{2,1,0:T(8,128)(2,1)S(1)}, bf16[16,16,128]{2,1,0:T(8,128)(2,1)S(1)}, u32[]{:S(2)}, u32[]{:S(2)}) %collective-permute-start.18) | collective-permute-done | bytes 65568 | tf_op jit(solution)/shard_map/ppermute | solution.py:227
  94.9 0.0 collective-permute-done.21.refs_9_
  94.9 0.7 precondition.1
  95.6 12.0 %all_to_all.9 = f32[8,8,512]{2,0,1:T(8,128)S(1)} all-to-all(f32[8,8,512]{2,0,1:T(8,128)S(1)} %bitcast.5), channel_id=1, replica_groups={{0,2,4,6,8,10,12,14},{1,3,5,7,9,11,13,15},{16,18,20,22,24,26,28,30},{17..., dimensions={1} | all-to-all | bytes 262144 | tf_op jit(solution)/shard_map/all_to_all | solution.py:352
  107.6 0.7 copy.8
  (2 shorter events, 0.0 us)
Async XLA Ops:
  2.0 26.0 %collective-permute-start = (bf16[128,5760]{1,0:T(8,128)(2,1)S(1)}, bf16[128,5760]{1,0:T(8,128)(2,1)S(1)}, u32[]{:S(2)}, u32[]{:S(2)}) collective-permute-start(bf16[128,5760]{1,0:T(8,128)(2,1)S(1)} %get-tuple-element.23), channel_id=1, source_target_pairs={{0,1},{1,0},{2,3},{3,2},{4,5},{5,4},{6,7},{7,6},{8,9},{9,8},{10,11... | collective-permute-start | bytes 4423688 | tf_op jit(solution)/shard_map/ppermute | solution.py:227
  2.6 19.3 %collective-permute-start.2 = (bf16[64,5632]{1,0:T(8,128)(2,1)S(1)}, bf16[64,5632]{1,0:T(8,128)(2,1)S(1)}, u32[]{:S(2)}, u32[]{:S(2)}) collective-permute-start(bf16[64,5632]{1,0:T(8,128)(2,1)S(1)} %get-tuple-element.24.refs_0_), channel_id=1, source_target_pairs={{0,2},{1,3},{2,0},{3,1},{4,6},{5,7},{6,4},{7,5},{8,10},{9,11},{10,... | collective-permute-start | bytes 2162696 | tf_op jit(solution)/shard_map/ppermute | solution.py:227
  5.2 40.0 %collective-permute-start.1 = (bf16[128,5760]{1,0:T(8,128)(2,1)S(1)}, bf16[128,5760]{1,0:T(8,128)(2,1)S(1)}, u32[]{:S(2)}, u32[]{:S(2)}) collective-permute-start(bf16[128,5760]{1,0:T(8,128)(2,1)S(1)} %get-tuple-element.20), channel_id=1, source_target_pairs={{0,16},{1,17},{2,18},{3,19},{4,20},{5,21},{6,22},{7,23},{8,24},{9,... | collective-permute-start | bytes 4423688 | tf_op jit(solution)/shard_map/ppermute | solution.py:227
  6.7 19.8 %collective-permute-start.3 = (bf16[64,5632]{1,0:T(8,128)(2,1)S(1)}, bf16[64,5632]{1,0:T(8,128)(2,1)S(1)}, u32[]{:S(2)}, u32[]{:S(2)}) collective-permute-start(bf16[64,5632]{1,0:T(8,128)(2,1)S(1)} %get-tuple-element.24.refs_0_), channel_id=1, source_target_pairs={{0,4},{1,5},{2,6},{3,7},{4,8},{5,9},{6,10},{7,11},{8,12},{9,13},{1... | collective-permute-start | bytes 2162696 | tf_op jit(solution)/shard_map/ppermute | solution.py:227
  21.9 49.7 %collective-permute-start.12 = (bf16[128,5760]{1,0:T(8,128)(2,1)S(1)}, bf16[128,5760]{1,0:T(8,128)(2,1)S(1)}, u32[]{:S(2)}, u32[]{:S(2)}) collective-permute-start(bf16[128,5760]{1,0:T(8,128)(2,1)S(1)} %get-tuple-element.32), channel_id=1, source_target_pairs={{0,17},{1,16},{2,19},{3,18},{4,21},{5,20},{6,23},{7,22},{8,25},{9,... | collective-permute-start | bytes 4423688 | tf_op jit(solution)/shard_map/ppermute | solution.py:227
  22.9 20.2 %collective-permute-start.5 = (bf16[64,5632]{1,0:T(8,128)(2,1)S(1)}, bf16[64,5632]{1,0:T(8,128)(2,1)S(1)}, u32[]{:S(2)}, u32[]{:S(2)}) collective-permute-start(bf16[64,5632]{1,0:T(8,128)(2,1)S(1)} %get-tuple-element.24.refs_0_), channel_id=1, source_target_pairs={{0,12},{1,13},{2,14},{3,15},{4,0},{5,1},{6,2},{7,3},{8,4},{9,5},{1... | collective-permute-start | bytes 2162696 | tf_op jit(solution)/shard_map/ppermute | solution.py:227
  26.5 18.6 %collective-permute-start.4 = (bf16[64,5632]{1,0:T(8,128)(2,1)S(1)}, bf16[64,5632]{1,0:T(8,128)(2,1)S(1)}, u32[]{:S(2)}, u32[]{:S(2)}) collective-permute-start(bf16[64,5632]{1,0:T(8,128)(2,1)S(1)} %collective-permute-done.3.refs_2_), channel_id=1, source_target_pairs={{0,2},{1,3},{2,0},{3,1},{4,6},{5,7},{6,4},{7,5},{8,10},{9,11},{10,... | collective-permute-start | bytes 2162696 | tf_op jit(solution)/shard_map/ppermute | solution.py:227
  28.0 31.4 %collective-permute-start.7 = (bf16[64,5632]{1,0:T(8,128)(2,1)S(1)}, bf16[64,5632]{1,0:T(8,128)(2,1)S(1)}, u32[]{:S(2)}, u32[]{:S(2)}) collective-permute-start(bf16[64,5632]{1,0:T(8,128)(2,1)S(1)} %collective-permute-done.3.refs_2_), channel_id=1, source_target_pairs={{0,4},{1,5},{2,6},{3,7},{4,8},{5,9},{6,10},{7,11},{8,12},{9,13},{1... | collective-permute-start | bytes 2162696 | tf_op jit(solution)/shard_map/ppermute | solution.py:227
  43.1 17.9 %collective-permute-start.6 = (bf16[64,5632]{1,0:T(8,128)(2,1)S(1)}, bf16[64,5632]{1,0:T(8,128)(2,1)S(1)}, u32[]{:S(2)}, u32[]{:S(2)}) collective-permute-start(bf16[64,5632]{1,0:T(8,128)(2,1)S(1)} %collective-permute-done.5.refs_4_), channel_id=1, source_target_pairs={{0,2},{1,3},{2,0},{3,1},{4,6},{5,7},{6,4},{7,5},{8,10},{9,11},{10,... | collective-permute-start | bytes 2162696 | tf_op jit(solution)/shard_map/ppermute | solution.py:227
  45.1 21.8 %collective-permute-start.9 = (bf16[32,5632]{1,0:T(8,128)(2,1)S(1)}, bf16[32,5632]{1,0:T(8,128)(2,1)S(1)}, u32[]{:S(2)}, u32[]{:S(2)}) collective-permute-start(bf16[32,5632]{1,0:T(8,128)(2,1)S(1)} %slice.8), channel_id=1, source_target_pairs={{0,4},{1,5},{2,6},{3,7},{4,8},{5,9},{6,10},{7,11},{8,12},{9,13},{1... | collective-permute-start | bytes 1081352 | tf_op jit(solution)/shard_map/ppermute | solution.py:227
  59.4 10.3 %collective-permute-start.8 = (bf16[32,5632]{1,0:T(8,128)(2,1)S(1)}, bf16[32,5632]{1,0:T(8,128)(2,1)S(1)}, u32[]{:S(2)}, u32[]{:S(2)}) collective-permute-start(bf16[32,5632]{1,0:T(8,128)(2,1)S(1)} %slice.6), channel_id=1, source_target_pairs={{0,2},{1,3},{2,0},{3,1},{4,6},{5,7},{6,4},{7,5},{8,10},{9,11},{10,... | collective-permute-start | bytes 1081352 | tf_op jit(solution)/shard_map/ppermute | solution.py:227
  71.1 4.1 %collective-permute-start.10 = (f32[128,256]{1,0:T(8,128)S(1)}, f32[128,256]{1,0:T(8,128)S(1)}, u32[]{:S(2)}, u32[]{:S(2)}) collective-permute-start(f32[128,256]{1,0:T(8,128)S(1)} %get-tuple-element.29), channel_id=1, source_target_pairs={{0,1},{1,0},{2,3},{3,2},{4,5},{5,4},{6,7},{7,6},{8,9},{9,8},{10,11... | collective-permute-start | bytes 393224 | tf_op jit(solution)/shard_map/ppermute | solution.py:227
  71.2 6.2 %collective-permute-start.11 = (f32[128,256]{1,0:T(8,128)S(1)}, f32[128,256]{1,0:T(8,128)S(1)}, u32[]{:S(2)}, u32[]{:S(2)}) collective-permute-start(f32[128,256]{1,0:T(8,128)S(1)} %get-tuple-element.30), channel_id=1, source_target_pairs={{0,16},{1,17},{2,18},{3,19},{4,20},{5,21},{6,22},{7,23},{8,24},{9,... | collective-permute-start | bytes 393224 | tf_op jit(solution)/shard_map/ppermute | solution.py:227
  71.6 8.0 %copy-start.1 = (s32[128,2]{0,1:T(2,128)S(1)}, s32[128,2]{0,1:T(2,128)}, u32[]{:S(2)}) copy-start(s32[128,2]{0,1:T(2,128)} %param.8) | copy-start | bytes 3076
  71.6 8.4 %copy-start = (bf16[4096,256]{1,0:T(8,128)(2,1)S(1)}, bf16[4096,256]{1,0:T(8,128)(2,1)}, u32[]{:S(2)}) copy-start(bf16[4096,256]{1,0:T(8,128)(2,1)} %refs_8_.1) | copy-start | bytes 6291460
  73.7 5.9 %collective-permute-start.13 = (f32[128,256]{1,0:T(8,128)S(1)}, f32[128,256]{1,0:T(8,128)S(1)}, u32[]{:S(2)}, u32[]{:S(2)}) collective-permute-start(f32[128,256]{1,0:T(8,128)S(1)} %project_last.1), channel_id=1, source_target_pairs={{0,17},{1,16},{2,19},{3,18},{4,21},{5,20},{6,23},{7,22},{8,25},{9,... | collective-permute-start | bytes 393224 | tf_op jit(solution)/shard_map/ppermute | solution.py:227
  80.0 14.9 %collective-permute-start.21 = (bf16[4096,256]{1,0:T(8,128)(2,1)S(1)}, bf16[4096,256]{1,0:T(8,128)(2,1)S(1)}, u32[]{:S(2)}, u32[]{:S(2)}) collective-permute-start(bf16[4096,256]{1,0:T(8,128)(2,1)S(1)} %copy-done), channel_id=1, source_target_pairs={{0,1},{1,0},{2,3},{3,2},{4,5},{5,4},{6,7},{7,6},{8,9},{9,8},{10,11... | collective-permute-start | bytes 6291464 | tf_op jit(solution)/shard_map/ppermute | solution.py:227
  80.2 5.4 %collective-permute-start.16 = (bf16[16,16,128]{2,1,0:T(8,128)(2,1)S(1)}, bf16[16,16,128]{2,1,0:T(8,128)(2,1)S(1)}, u32[]{:S(2)}, u32[]{:S(2)}) collective-permute-start(bf16[16,16,128]{2,1,0:T(8,128)(2,1)S(1)} %gram.1.refs_0_), channel_id=1, source_target_pairs={{0,4},{1,5},{2,6},{3,7},{4,0},{5,1},{6,2},{7,3},{8,12},{9,13},{10,... | collective-permute-start | bytes 196616 | tf_op jit(solution)/shard_map/ppermute | solution.py:227
  81.9 6.6 %collective-permute-start.15 = (bf16[16,16,128]{2,1,0:T(8,128)(2,1)S(1)}, bf16[16,16,128]{2,1,0:T(8,128)(2,1)S(1)}, u32[]{:S(2)}, u32[]{:S(2)}) collective-permute-start(bf16[16,16,128]{2,1,0:T(8,128)(2,1)S(1)} %gram.1.refs_0_), channel_id=1, source_target_pairs={{0,12},{1,13},{2,14},{3,15},{4,8},{5,9},{6,10},{7,11},{8,4},{9,5},... | collective-permute-start | bytes 196616 | tf_op jit(solution)/shard_map/ppermute | solution.py:227
  83.6 7.1 %collective-permute-start.14 = (bf16[16,16,128]{2,1,0:T(8,128)(2,1)S(1)}, bf16[16,16,128]{2,1,0:T(8,128)(2,1)S(1)}, u32[]{:S(2)}, u32[]{:S(2)}) collective-permute-start(bf16[16,16,128]{2,1,0:T(8,128)(2,1)S(1)} %gram.1.refs_0_), channel_id=1, source_target_pairs={{0,8},{1,9},{2,10},{3,11},{4,12},{5,13},{6,14},{7,15},{8,0},{9,1},... | collective-permute-start | bytes 196616 | tf_op jit(solution)/shard_map/ppermute | solution.py:227
  84.1 8.1 %collective-permute-start.17 = (bf16[16,16,128]{2,1,0:T(8,128)(2,1)S(1)}, bf16[16,16,128]{2,1,0:T(8,128)(2,1)S(1)}, u32[]{:S(2)}, u32[]{:S(2)}) collective-permute-start(bf16[16,16,128]{2,1,0:T(8,128)(2,1)S(1)} %gram.1.refs_0_), channel_id=1, source_target_pairs={{0,2},{1,3},{2,0},{3,1},{4,6},{5,7},{6,4},{7,5},{8,10},{9,11},{10,... | collective-permute-start | bytes 196616 | tf_op jit(solution)/shard_map/ppermute | solution.py:227
  85.6 6.5 %collective-permute-start.20 = (bf16[16,16,128]{2,1,0:T(8,128)(2,1)S(1)}, bf16[16,16,128]{2,1,0:T(8,128)(2,1)S(1)}, u32[]{:S(2)}, u32[]{:S(2)}) collective-permute-start(bf16[16,16,128]{2,1,0:T(8,128)(2,1)S(1)} %collective-permute-done.16.refs_3_), channel_id=1, source_target_pairs={{0,2},{1,3},{2,0},{3,1},{4,6},{5,7},{6,4},{7,5},{8,10},{9,11},{10,... | collective-permute-start | bytes 196616 | tf_op jit(solution)/shard_map/ppermute | solution.py:227
  88.4 4.3 %collective-permute-start.19 = (bf16[16,16,128]{2,1,0:T(8,128)(2,1)S(1)}, bf16[16,16,128]{2,1,0:T(8,128)(2,1)S(1)}, u32[]{:S(2)}, u32[]{:S(2)}) collective-permute-start(bf16[16,16,128]{2,1,0:T(8,128)(2,1)S(1)} %collective-permute-done.15.refs_2_), channel_id=1, source_target_pairs={{0,2},{1,3},{2,0},{3,1},{4,6},{5,7},{6,4},{7,5},{8,10},{9,11},{10,... | collective-permute-start | bytes 196616 | tf_op jit(solution)/shard_map/ppermute | solution.py:227
  90.7 4.3 %collective-permute-start.18 = (bf16[16,16,128]{2,1,0:T(8,128)(2,1)S(1)}, bf16[16,16,128]{2,1,0:T(8,128)(2,1)S(1)}, u32[]{:S(2)}, u32[]{:S(2)}) collective-permute-start(bf16[16,16,128]{2,1,0:T(8,128)(2,1)S(1)} %collective-permute-done.14.refs_1_), channel_id=1, source_target_pairs={{0,2},{1,3},{2,0},{3,1},{4,6},{5,7},{6,4},{7,5},{8,10},{9,11},{10,... | collective-permute-start | bytes 196616 | tf_op jit(solution)/shard_map/ppermute | solution.py:227

commit v8 on v7

--- a/solution.py
+++ b/solution.py
@@ -97,9 +97,26 @@
 
 
 def last_kernel(sub, width, ids, sizes, xc, *refs):
-    experts = [piece_of(at, sizes) for at in ids]
-    for k, got in enumerate(picks([xc[...]], refs[:-1], experts, width, sub)[0]):
-        refs[-1][:, k * LANES : (k + 1) * LANES] = got
+    pieces, out = refs[:-1], refs[-1]
+    toks = xc[...]
+    named = jnp.transpose(toks[:, -LANES:].astype(jnp.float32))
+    sides = []
+    for at, size, table in (
+        (sub * width, pieces[0].shape[1] - width, jnp.concatenate([p[:, width:] for p in pieces], axis=0)),
+        (0, width, jnp.concatenate([p[:, :width] for p in pieces], axis=0)),
+    ):
+        sides.append([nt(table, toks[:, at + a * size : at + (a + 1) * size]) for a in range(sub)])
+    for k in range(2):
+        parts = []
+        for sums in sides:
+            picked = jnp.zeros((PROJ, TOK), jnp.float32)
+            for i, place in enumerate(ids):
+                expert, part = piece_of(place, sizes)
+                for a in range(sub):
+                    wanted = jnp.where(part == a, expert, -1).astype(jnp.float32)
+                    picked += jnp.where(named[k : k + 1] == wanted, sums[a][i * PROJ : (i + 1) * PROJ], 0.0)
+            parts.append(picked)
+        out[:, k * LANES : (k + 1) * LANES] = jnp.transpose(jnp.concatenate(parts, axis=0))
 
 
 def pack_kernel(outputs, routes_ref, *refs):
@@ -336,7 +353,7 @@
         return lambda g, d: (g, d ^ (2 * step))
 
     grams, steps = [mine], [0]
-    for step in sorted(range(1, z_size), key=lambda k: (-(k >= z_size // 2), k)):
+    for step in range(1, z_size):
         grams.append(move(mine, far(step * y_size)))
         steps.append(step * y_size)
     if y_size == 2:

time: 109 us -> 108 us (level)
  blocking collectives: 12 us -> 10.6 us
    all_to_all x1, blocking collectives: 12 us -> 10.6 us  [shards(): lax.all_to_all(columns, 'dp', split_axis=1, concat_axis=1, axis_index_gro...]
where the time goes in v8:
time: 108 us; the launch traced here: 107 us
  waiting for transfers between devices  58.3 us (54%)
  starting transfers between devices  27.3 us (25%)
  Pallas kernels  10.6 us (10%)
  blocking collectives  10.6 us (10%)
    ppermute x22, waiting for transfers between devices, move(): return lax.ppermute(x, AXES, pairs)  58.3 us
    ppermute x22, starting transfers between devices, move(): return lax.ppermute(x, AXES, pairs)  27.3 us
    all_to_all x1, blocking collectives, shards(): lax.all_to_all(columns, 'dp', split_axis=1, concat_axis=1, axis_index_gro...  10.6 us
    pallas_call x5, Pallas kernels, local(): pl.pallas_call(kernel, in_specs=[vmem] * len(operands), out_specs=jax.tre...  6.74 us
    pallas_call x2, Pallas kernels, pack(): pl.pallas_call(functools.partial(pack_kernel, [[b[1:] for b in out] for o...  3.85 us
  transfers between devices with their start and end apart: 22, of which 12 were waited for; matrix products, arithmetic and copies ran while one was open for 0% of the time, Pallas kernels for 7%

profile of v8, /device:TPU:0, one launch (start us, length us, event | category | flops | bytes accessed | tf_op | source)
XLA Modules:
  0.0 107.5 jit_solution(16496299025050354003)
XLA Ops:
  0.0 2.0 %pack_first.1 = (bf16[64,5632]{1,0:T(8,128)(2,1)S(1)}, bf16[128,5760]{1,0:T(8,128)(2,1)S(1)}, bf16[128,5760]{1,0:T(8,128)(2,1)S(1)}) custom-call(s32[2,128]{1,0:T(2,128)} %bitcast.6, bf16[64,8192]{1,0:T(8,128)(2,1)} %refs_0_.2, bf16[64,3072]{1,0:T(8,128)(2,1)} %refs_1_.2, bf16[128,16384]{1,0:T(8,128)(2,1)} %refs_2_.3, bf16[128,6144]{1,0:T(8,128)(2,1)} %refs_3_.3, ...), custom_call_target="tpu_custom_call" | custom-call | tf_op jit(solution)/shard_map/pack_first/pallas_call | solution.py:156
  2.0 0.5 collective-permute-start
  2.6 2.6 %collective-permute-start.2 = (bf16[64,5632]{1,0:T(8,128)(2,1)S(1)}, bf16[64,5632]{1,0:T(8,128)(2,1)S(1)}, u32[]{:S(2)}, u32[]{:S(2)}) collective-permute-start(bf16[64,5632]{1,0:T(8,128)(2,1)S(1)} %get-tuple-element.24.refs_0_), channel_id=1, source_target_pairs={{0,2},{1,3},{2,0},{3,1},{4,6},{5,7},{6,4},{7,5},{8,10},{9,11},{10,... | collective-permute-start | bytes 2162696 | tf_op jit(solution)/shard_map/ppermute | solution.py:244
  5.2 1.5 %collective-permute-start.1 = (bf16[128,5760]{1,0:T(8,128)(2,1)S(1)}, bf16[128,5760]{1,0:T(8,128)(2,1)S(1)}, u32[]{:S(2)}, u32[]{:S(2)}) collective-permute-start(bf16[128,5760]{1,0:T(8,128)(2,1)S(1)} %get-tuple-element.20), channel_id=1, source_target_pairs={{0,16},{1,17},{2,18},{3,19},{4,20},{5,21},{6,22},{7,23},{8,24},{9,... | collective-permute-start | bytes 4423688 | tf_op jit(solution)/shard_map/ppermute | solution.py:244
  6.7 1.6 %collective-permute-start.3 = (bf16[64,5632]{1,0:T(8,128)(2,1)S(1)}, bf16[64,5632]{1,0:T(8,128)(2,1)S(1)}, u32[]{:S(2)}, u32[]{:S(2)}) collective-permute-start(bf16[64,5632]{1,0:T(8,128)(2,1)S(1)} %get-tuple-element.24.refs_0_), channel_id=1, source_target_pairs={{0,4},{1,5},{2,6},{3,7},{4,8},{5,9},{6,10},{7,11},{8,12},{9,13},{1... | collective-permute-start | bytes 2162696 | tf_op jit(solution)/shard_map/ppermute | solution.py:244
  8.2 1.8 %pack_second.1 = (bf16[128,5760]{1,0:T(8,128)(2,1)S(1)}, bf16[128,5760]{1,0:T(8,128)(2,1)S(1)}) custom-call(s32[2,128]{1,0:T(2,128)} %bitcast.7, bf16[128,16384]{1,0:T(8,128)(2,1)} %refs_2_.3, bf16[128,6144]{1,0:T(8,128)(2,1)} %refs_3_.3, bf16[128,16384]{1,0:T(8,128)(2,1)} %refs_2_.3, bf16[128,6144]{1,0:T(8,128)(2,1)} %refs_3_.3), custom_call_target="tpu_custom_call" | custom-call | tf_op jit(solution)/shard_map/pack_second/pallas_call | solution.py:156
  10.0 11.8 %collective-permute-done.2.refs_1_ = bf16[64,5632]{1,0:T(8,128)(2,1)S(1)} collective-permute-done((bf16[64,5632]{1,0:T(8,128)(2,1)S(1)}, bf16[64,5632]{1,0:T(8,128)(2,1)S(1)}, u32[]{:S(2)}, u32[]{:S(2)}) %collective-permute-start.2) | collective-permute-done | bytes 720928 | tf_op jit(solution)/shard_map/ppermute | solution.py:244
  21.9 1.0 collective-permute-start.12
  22.9 3.6 %collective-permute-start.5 = (bf16[64,5632]{1,0:T(8,128)(2,1)S(1)}, bf16[64,5632]{1,0:T(8,128)(2,1)S(1)}, u32[]{:S(2)}, u32[]{:S(2)}) collective-permute-start(bf16[64,5632]{1,0:T(8,128)(2,1)S(1)} %get-tuple-element.24.refs_0_), channel_id=1, source_target_pairs={{0,12},{1,13},{2,14},{3,15},{4,0},{5,1},{6,2},{7,3},{8,4},{9,5},{1... | collective-permute-start | bytes 2162696 | tf_op jit(solution)/shard_map/ppermute | solution.py:244
  26.5 0.0 collective-permute-done.3.refs_2_
  26.5 1.5 %collective-permute-start.4 = (bf16[64,5632]{1,0:T(8,128)(2,1)S(1)}, bf16[64,5632]{1,0:T(8,128)(2,1)S(1)}, u32[]{:S(2)}, u32[]{:S(2)}) collective-permute-start(bf16[64,5632]{1,0:T(8,128)(2,1)S(1)} %collective-permute-done.3.refs_2_), channel_id=1, source_target_pairs={{0,2},{1,3},{2,0},{3,1},{4,6},{5,7},{6,4},{7,5},{8,10},{9,11},{10,... | collective-permute-start | bytes 2162696 | tf_op jit(solution)/shard_map/ppermute | solution.py:244
  28.0 0.0 collective-permute-done.other
  28.0 0.0 collective-permute-start.7
  28.0 15.0 %collective-permute-done.5.refs_4_ = bf16[64,5632]{1,0:T(8,128)(2,1)S(1)} collective-permute-done((bf16[64,5632]{1,0:T(8,128)(2,1)S(1)}, bf16[64,5632]{1,0:T(8,128)(2,1)S(1)}, u32[]{:S(2)}, u32[]{:S(2)}) %collective-permute-start.5) | collective-permute-done | bytes 720928 | tf_op jit(solution)/shard_map/ppermute | solution.py:244
  43.1 1.5 %collective-permute-start.6 = (bf16[64,5632]{1,0:T(8,128)(2,1)S(1)}, bf16[64,5632]{1,0:T(8,128)(2,1)S(1)}, u32[]{:S(2)}, u32[]{:S(2)}) collective-permute-start(bf16[64,5632]{1,0:T(8,128)(2,1)S(1)} %collective-permute-done.5.refs_4_), channel_id=1, source_target_pairs={{0,2},{1,3},{2,0},{3,1},{4,6},{5,7},{6,4},{7,5},{8,10},{9,11},{10,... | collective-permute-start | bytes 2162696 | tf_op jit(solution)/shard_map/ppermute | solution.py:244
  44.6 0.5 collective-permute-done.4.refs_3_
  45.1 0.1 collective-permute-start.9
  45.2 0.0 collective-permute-done.1.x
  45.2 14.2 %collective-permute-done.7.refs_0_.refs_6_ = bf16[64,5632]{1,0:T(8,128)(2,1)S(1)} collective-permute-done((bf16[64,5632]{1,0:T(8,128)(2,1)S(1)}, bf16[64,5632]{1,0:T(8,128)(2,1)S(1)}, u32[]{:S(2)}, u32[]{:S(2)}) %collective-permute-start.7) | collective-permute-done | bytes 720928 | tf_op jit(solution)/shard_map/ppermute | solution.py:244
  59.4 1.6 %collective-permute-start.8 = (bf16[32,5632]{1,0:T(8,128)(2,1)S(1)}, bf16[32,5632]{1,0:T(8,128)(2,1)S(1)}, u32[]{:S(2)}, u32[]{:S(2)}) collective-permute-start(bf16[32,5632]{1,0:T(8,128)(2,1)S(1)} %slice.6), channel_id=1, source_target_pairs={{0,2},{1,3},{2,0},{3,1},{4,6},{5,7},{6,4},{7,5},{8,10},{9,11},{10,... | collective-permute-start | bytes 1081352 | tf_op jit(solution)/shard_map/ppermute | solution.py:244
  61.0 0.0 collective-permute-done.6.refs_5_
  61.0 2.5 %project_early.1.early_ref = f32[3,128,256]{2,1,0:T(8,128)S(1)} custom-call(bf16[128,5760]{1,0:T(8,128)(2,1)S(1)} %get-tuple-element.22.own, bf16[128,5760]{1,0:T(8,128)(2,1)S(1)} %collective-permute-done.other, bf16[128,5760]{1,0:T(8,128)(2,1)S(1)} %collective-permute-done.1.x, bf16[64,5632]{1,0:T(8,128)(2,1)S(1)} %get-tuple-element.24.refs_0_, ...), custom_call_target="tpu_custom_call" | custom-call | tf_op jit(solution)/shard_map/project_early/pallas_call | solution.py:169
  63.5 3.5 %collective-permute-done.9.refs_2_.refs_8_ = bf16[32,5632]{1,0:T(8,128)(2,1)S(1)} collective-permute-done((bf16[32,5632]{1,0:T(8,128)(2,1)S(1)}, bf16[32,5632]{1,0:T(8,128)(2,1)S(1)}, u32[]{:S(2)}, u32[]{:S(2)}) %collective-permute-start.9) | collective-permute-done | bytes 360480 | tf_op jit(solution)/shard_map/ppermute | solution.py:244
  67.0 2.7 %collective-permute-done.8.refs_1_.refs_7_ = bf16[32,5632]{1,0:T(8,128)(2,1)S(1)} collective-permute-done((bf16[32,5632]{1,0:T(8,128)(2,1)S(1)}, bf16[32,5632]{1,0:T(8,128)(2,1)S(1)}, u32[]{:S(2)}, u32[]{:S(2)}) %collective-permute-start.8) | collective-permute-done | bytes 360480 | tf_op jit(solution)/shard_map/ppermute | solution.py:244
  69.7 1.4 %project_late.1 = (f32[128,256]{1,0:T(8,128)S(1)}, f32[128,256]{1,0:T(8,128)S(1)}, f32[128,256]{1,0:T(8,128)S(1)}) custom-call(bf16[128,5760]{1,0:T(8,128)(2,1)S(1)} %get-tuple-element.22.own, bf16[128,5760]{1,0:T(8,128)(2,1)S(1)} %collective-permute-done.other, bf16[128,5760]{1,0:T(8,128)(2,1)S(1)} %collective-permute-done.1.x, ...), custom_call_target="tpu_custom_call" | custom-call | tf_op jit(solution)/shard_map/project_late/pallas_call | solution.py:169
  71.1 0.1 collective-permute-start.10
  71.2 0.4 collective-permute-start.11
  71.6 0.0 collective-permute-done.12.xc
  71.6 0.0 copy-start.1
  71.6 0.0 copy-start
  71.6 1.7 %project_last.1 = f32[128,256]{1,0:T(8,128)S(1)} custom-call(bf16[128,5760]{1,0:T(8,128)(2,1)S(1)} %collective-permute-done.12.xc, bf16[64,5632]{1,0:T(8,128)(2,1)S(1)} %get-tuple-element.24.refs_0_, bf16[64,5632]{1,0:T(8,128)(2,1)S(1)} %collective-permute-done.2.refs_1_, bf16[64,5632]{1,0:T(8,128)(2,1)S(1)} %collective-permute-done.3.refs_2_, ...), custom_call_target="tpu_custom_call" | custom-call | tf_op jit(solution)/shard_map/project_last/pallas_call | solution.py:169
  73.3 1.5 %collective-permute-start.13 = (f32[128,256]{1,0:T(8,128)S(1)}, f32[128,256]{1,0:T(8,128)S(1)}, u32[]{:S(2)}, u32[]{:S(2)}) collective-permute-start(f32[128,256]{1,0:T(8,128)S(1)} %project_last.1), channel_id=1, source_target_pairs={{0,17},{1,16},{2,19},{3,18},{4,21},{5,20},{6,23},{7,22},{8,25},{9,... | collective-permute-start | bytes 393224 | tf_op jit(solution)/shard_map/ppermute | solution.py:244
  74.8 0.0 collective-permute-done.10.p1
  74.8 2.7 %collective-permute-done.11.p2 = f32[128,256]{1,0:T(8,128)S(1)} collective-permute-done((f32[128,256]{1,0:T(8,128)S(1)}, f32[128,256]{1,0:T(8,128)S(1)}, u32[]{:S(2)}, u32[]{:S(2)}) %collective-permute-start.11) | collective-permute-done | bytes 131104 | tf_op jit(solution)/shard_map/ppermute | solution.py:244
  77.5 1.9 %collective-permute-done.13.p3 = f32[128,256]{1,0:T(8,128)S(1)} collective-permute-done((f32[128,256]{1,0:T(8,128)S(1)}, f32[128,256]{1,0:T(8,128)S(1)}, u32[]{:S(2)}, u32[]{:S(2)}) %collective-permute-start.13) | collective-permute-done | bytes 131104 | tf_op jit(solution)/shard_map/ppermute | solution.py:244
  79.4 0.0 copy-done.1
  79.5 0.4 gram.1.refs_0_
  79.9 0.0 copy-done
  79.9 0.3 collective-permute-start.21
  80.2 3.3 %collective-permute-start.16 = (bf16[16,16,128]{2,1,0:T(8,128)(2,1)S(1)}, bf16[16,16,128]{2,1,0:T(8,128)(2,1)S(1)}, u32[]{:S(2)}, u32[]{:S(2)}) collective-permute-start(bf16[16,16,128]{2,1,0:T(8,128)(2,1)S(1)} %gram.1.refs_0_), channel_id=1, source_target_pairs={{0,12},{1,13},{2,14},{3,15},{4,8},{5,9},{6,10},{7,11},{8,4},{9,5},... | collective-permute-start | bytes 196616 | tf_op jit(solution)/shard_map/ppermute | solution.py:244
  83.6 0.0 collective-permute-start.15
  83.6 1.1 collective-permute-start.14
  84.6 1.5 %collective-permute-start.17 = (bf16[16,16,128]{2,1,0:T(8,128)(2,1)S(1)}, bf16[16,16,128]{2,1,0:T(8,128)(2,1)S(1)}, u32[]{:S(2)}, u32[]{:S(2)}) collective-permute-start(bf16[16,16,128]{2,1,0:T(8,128)(2,1)S(1)} %gram.1.refs_0_), channel_id=1, source_target_pairs={{0,2},{1,3},{2,0},{3,1},{4,6},{5,7},{6,4},{7,5},{8,10},{9,11},{10,... | collective-permute-start | bytes 196616 | tf_op jit(solution)/shard_map/ppermute | solution.py:244
  86.1 0.9 collective-permute-done.16.refs_3_
  87.1 1.5 %collective-permute-start.20 = (bf16[16,16,128]{2,1,0:T(8,128)(2,1)S(1)}, bf16[16,16,128]{2,1,0:T(8,128)(2,1)S(1)}, u32[]{:S(2)}, u32[]{:S(2)}) collective-permute-start(bf16[16,16,128]{2,1,0:T(8,128)(2,1)S(1)} %collective-permute-done.16.refs_3_), channel_id=1, source_target_pairs={{0,2},{1,3},{2,0},{3,1},{4,6},{5,7},{6,4},{7,5},{8,10},{9,11},{10,... | collective-permute-start | bytes 196616 | tf_op jit(solution)/shard_map/ppermute | solution.py:244
  88.6 1.2 %collective-permute-done.15.refs_2_ = bf16[16,16,128]{2,1,0:T(8,128)(2,1)S(1)} collective-permute-done((bf16[16,16,128]{2,1,0:T(8,128)(2,1)S(1)}, bf16[16,16,128]{2,1,0:T(8,128)(2,1)S(1)}, u32[]{:S(2)}, u32[]{:S(2)}) %collective-permute-start.15) | collective-permute-done | bytes 65568 | tf_op jit(solution)/shard_map/ppermute | solution.py:244
  89.8 1.5 %collective-permute-start.19 = (bf16[16,16,128]{2,1,0:T(8,128)(2,1)S(1)}, bf16[16,16,128]{2,1,0:T(8,128)(2,1)S(1)}, u32[]{:S(2)}, u32[]{:S(2)}) collective-permute-start(bf16[16,16,128]{2,1,0:T(8,128)(2,1)S(1)} %collective-permute-done.15.refs_2_), channel_id=1, source_target_pairs={{0,2},{1,3},{2,0},{3,1},{4,6},{5,7},{6,4},{7,5},{8,10},{9,11},{10,... | collective-permute-start | bytes 196616 | tf_op jit(solution)/shard_map/ppermute | solution.py:244
  91.3 0.0 collective-permute-done.14.refs_1_
  91.3 0.5 collective-permute-start.18
  91.8 0.0 collective-permute-done.17.refs_4_
  91.8 0.0 collective-permute-done.20.refs_7_
  91.8 2.7 %collective-permute-done.19.refs_6_ = bf16[16,16,128]{2,1,0:T(8,128)(2,1)S(1)} collective-permute-done((bf16[16,16,128]{2,1,0:T(8,128)(2,1)S(1)}, bf16[16,16,128]{2,1,0:T(8,128)(2,1)S(1)}, u32[]{:S(2)}, u32[]{:S(2)}) %collective-permute-start.19) | collective-permute-done | bytes 65568 | tf_op jit(solution)/shard_map/ppermute | solution.py:244
  94.5 1.0 collective-permute-done.18.refs_5_
  95.6 0.0 collective-permute-done.21.refs_9_
  95.6 0.7 precondition.1
  96.3 10.6 %all_to_all.9 = f32[8,8,512]{2,0,1:T(8,128)S(1)} all-to-all(f32[8,8,512]{2,0,1:T(8,128)S(1)} %bitcast.5), channel_id=1, replica_groups={{0,2,4,6,8,10,12,14},{1,3,5,7,9,11,13,15},{16,18,20,22,24,26,28,30},{17..., dimensions={1} | all-to-all | bytes 262144 | tf_op jit(solution)/shard_map/all_to_all | solution.py:369
  106.8 0.7 copy.8
  (2 shorter events, 0.0 us)
Async XLA Ops:
  2.0 26.0 %collective-permute-start = (bf16[128,5760]{1,0:T(8,128)(2,1)S(1)}, bf16[128,5760]{1,0:T(8,128)(2,1)S(1)}, u32[]{:S(2)}, u32[]{:S(2)}) collective-permute-start(bf16[128,5760]{1,0:T(8,128)(2,1)S(1)} %get-tuple-element.23), channel_id=1, source_target_pairs={{0,1},{1,0},{2,3},{3,2},{4,5},{5,4},{6,7},{7,6},{8,9},{9,8},{10,11... | collective-permute-start | bytes 4423688 | tf_op jit(solution)/shard_map/ppermute | solution.py:244
  2.6 19.3 %collective-permute-start.2 = (bf16[64,5632]{1,0:T(8,128)(2,1)S(1)}, bf16[64,5632]{1,0:T(8,128)(2,1)S(1)}, u32[]{:S(2)}, u32[]{:S(2)}) collective-permute-start(bf16[64,5632]{1,0:T(8,128)(2,1)S(1)} %get-tuple-element.24.refs_0_), channel_id=1, source_target_pairs={{0,2},{1,3},{2,0},{3,1},{4,6},{5,7},{6,4},{7,5},{8,10},{9,11},{10,... | collective-permute-start | bytes 2162696 | tf_op jit(solution)/shard_map/ppermute | solution.py:244
  5.2 40.0 %collective-permute-start.1 = (bf16[128,5760]{1,0:T(8,128)(2,1)S(1)}, bf16[128,5760]{1,0:T(8,128)(2,1)S(1)}, u32[]{:S(2)}, u32[]{:S(2)}) collective-permute-start(bf16[128,5760]{1,0:T(8,128)(2,1)S(1)} %get-tuple-element.20), channel_id=1, source_target_pairs={{0,16},{1,17},{2,18},{3,19},{4,20},{5,21},{6,22},{7,23},{8,24},{9,... | collective-permute-start | bytes 4423688 | tf_op jit(solution)/shard_map/ppermute | solution.py:244
  6.7 19.8 %collective-permute-start.3 = (bf16[64,5632]{1,0:T(8,128)(2,1)S(1)}, bf16[64,5632]{1,0:T(8,128)(2,1)S(1)}, u32[]{:S(2)}, u32[]{:S(2)}) collective-permute-start(bf16[64,5632]{1,0:T(8,128)(2,1)S(1)} %get-tuple-element.24.refs_0_), channel_id=1, source_target_pairs={{0,4},{1,5},{2,6},{3,7},{4,8},{5,9},{6,10},{7,11},{8,12},{9,13},{1... | collective-permute-start | bytes 2162696 | tf_op jit(solution)/shard_map/ppermute | solution.py:244
  21.9 49.7 %collective-permute-start.12 = (bf16[128,5760]{1,0:T(8,128)(2,1)S(1)}, bf16[128,5760]{1,0:T(8,128)(2,1)S(1)}, u32[]{:S(2)}, u32[]{:S(2)}) collective-permute-start(bf16[128,5760]{1,0:T(8,128)(2,1)S(1)} %get-tuple-element.32), channel_id=1, source_target_pairs={{0,17},{1,16},{2,19},{3,18},{4,21},{5,20},{6,23},{7,22},{8,25},{9,... | collective-permute-start | bytes 4423688 | tf_op jit(solution)/shard_map/ppermute | solution.py:244
  22.9 20.2 %collective-permute-start.5 = (bf16[64,5632]{1,0:T(8,128)(2,1)S(1)}, bf16[64,5632]{1,0:T(8,128)(2,1)S(1)}, u32[]{:S(2)}, u32[]{:S(2)}) collective-permute-start(bf16[64,5632]{1,0:T(8,128)(2,1)S(1)} %get-tuple-element.24.refs_0_), channel_id=1, source_target_pairs={{0,12},{1,13},{2,14},{3,15},{4,0},{5,1},{6,2},{7,3},{8,4},{9,5},{1... | collective-permute-start | bytes 2162696 | tf_op jit(solution)/shard_map/ppermute | solution.py:244
  26.5 18.6 %collective-permute-start.4 = (bf16[64,5632]{1,0:T(8,128)(2,1)S(1)}, bf16[64,5632]{1,0:T(8,128)(2,1)S(1)}, u32[]{:S(2)}, u32[]{:S(2)}) collective-permute-start(bf16[64,5632]{1,0:T(8,128)(2,1)S(1)} %collective-permute-done.3.refs_2_), channel_id=1, source_target_pairs={{0,2},{1,3},{2,0},{3,1},{4,6},{5,7},{6,4},{7,5},{8,10},{9,11},{10,... | collective-permute-start | bytes 2162696 | tf_op jit(solution)/shard_map/ppermute | solution.py:244
  28.0 31.4 %collective-permute-start.7 = (bf16[64,5632]{1,0:T(8,128)(2,1)S(1)}, bf16[64,5632]{1,0:T(8,128)(2,1)S(1)}, u32[]{:S(2)}, u32[]{:S(2)}) collective-permute-start(bf16[64,5632]{1,0:T(8,128)(2,1)S(1)} %collective-permute-done.3.refs_2_), channel_id=1, source_target_pairs={{0,4},{1,5},{2,6},{3,7},{4,8},{5,9},{6,10},{7,11},{8,12},{9,13},{1... | collective-permute-start | bytes 2162696 | tf_op jit(solution)/shard_map/ppermute | solution.py:244
  43.1 17.9 %collective-permute-start.6 = (bf16[64,5632]{1,0:T(8,128)(2,1)S(1)}, bf16[64,5632]{1,0:T(8,128)(2,1)S(1)}, u32[]{:S(2)}, u32[]{:S(2)}) collective-permute-start(bf16[64,5632]{1,0:T(8,128)(2,1)S(1)} %collective-permute-done.5.refs_4_), channel_id=1, source_target_pairs={{0,2},{1,3},{2,0},{3,1},{4,6},{5,7},{6,4},{7,5},{8,10},{9,11},{10,... | collective-permute-start | bytes 2162696 | tf_op jit(solution)/shard_map/ppermute | solution.py:244
  45.1 21.8 %collective-permute-start.9 = (bf16[32,5632]{1,0:T(8,128)(2,1)S(1)}, bf16[32,5632]{1,0:T(8,128)(2,1)S(1)}, u32[]{:S(2)}, u32[]{:S(2)}) collective-permute-start(bf16[32,5632]{1,0:T(8,128)(2,1)S(1)} %slice.8), channel_id=1, source_target_pairs={{0,4},{1,5},{2,6},{3,7},{4,8},{5,9},{6,10},{7,11},{8,12},{9,13},{1... | collective-permute-start | bytes 1081352 | tf_op jit(solution)/shard_map/ppermute | solution.py:244
  59.4 10.3 %collective-permute-start.8 = (bf16[32,5632]{1,0:T(8,128)(2,1)S(1)}, bf16[32,5632]{1,0:T(8,128)(2,1)S(1)}, u32[]{:S(2)}, u32[]{:S(2)}) collective-permute-start(bf16[32,5632]{1,0:T(8,128)(2,1)S(1)} %slice.6), channel_id=1, source_target_pairs={{0,2},{1,3},{2,0},{3,1},{4,6},{5,7},{6,4},{7,5},{8,10},{9,11},{10,... | collective-permute-start | bytes 1081352 | tf_op jit(solution)/shard_map/ppermute | solution.py:244
  71.1 3.7 %collective-permute-start.10 = (f32[128,256]{1,0:T(8,128)S(1)}, f32[128,256]{1,0:T(8,128)S(1)}, u32[]{:S(2)}, u32[]{:S(2)}) collective-permute-start(f32[128,256]{1,0:T(8,128)S(1)} %get-tuple-element.29), channel_id=1, source_target_pairs={{0,1},{1,0},{2,3},{3,2},{4,5},{5,4},{6,7},{7,6},{8,9},{9,8},{10,11... | collective-permute-start | bytes 393224 | tf_op jit(solution)/shard_map/ppermute | solution.py:244
  71.2 6.4 %collective-permute-start.11 = (f32[128,256]{1,0:T(8,128)S(1)}, f32[128,256]{1,0:T(8,128)S(1)}, u32[]{:S(2)}, u32[]{:S(2)}) collective-permute-start(f32[128,256]{1,0:T(8,128)S(1)} %get-tuple-element.30), channel_id=1, source_target_pairs={{0,16},{1,17},{2,18},{3,19},{4,20},{5,21},{6,22},{7,23},{8,24},{9,... | collective-permute-start | bytes 393224 | tf_op jit(solution)/shard_map/ppermute | solution.py:244
  71.6 7.9 %copy-start.1 = (s32[128,2]{0,1:T(2,128)S(1)}, s32[128,2]{0,1:T(2,128)}, u32[]{:S(2)}) copy-start(s32[128,2]{0,1:T(2,128)} %param.8) | copy-start | bytes 3076
  71.6 8.3 %copy-start = (bf16[4096,256]{1,0:T(8,128)(2,1)S(1)}, bf16[4096,256]{1,0:T(8,128)(2,1)}, u32[]{:S(2)}) copy-start(bf16[4096,256]{1,0:T(8,128)(2,1)} %refs_8_.1) | copy-start | bytes 6291460
  73.3 6.1 %collective-permute-start.13 = (f32[128,256]{1,0:T(8,128)S(1)}, f32[128,256]{1,0:T(8,128)S(1)}, u32[]{:S(2)}, u32[]{:S(2)}) collective-permute-start(f32[128,256]{1,0:T(8,128)S(1)} %project_last.1), channel_id=1, source_target_pairs={{0,17},{1,16},{2,19},{3,18},{4,21},{5,20},{6,23},{7,22},{8,25},{9,... | collective-permute-start | bytes 393224 | tf_op jit(solution)/shard_map/ppermute | solution.py:244
  79.9 15.7 %collective-permute-start.21 = (bf16[4096,256]{1,0:T(8,128)(2,1)S(1)}, bf16[4096,256]{1,0:T(8,128)(2,1)S(1)}, u32[]{:S(2)}, u32[]{:S(2)}) collective-permute-start(bf16[4096,256]{1,0:T(8,128)(2,1)S(1)} %copy-done), channel_id=1, source_target_pairs={{0,1},{1,0},{2,3},{3,2},{4,5},{5,4},{6,7},{7,6},{8,9},{9,8},{10,11... | collective-permute-start | bytes 6291464 | tf_op jit(solution)/shard_map/ppermute | solution.py:244
  80.2 6.8 %collective-permute-start.16 = (bf16[16,16,128]{2,1,0:T(8,128)(2,1)S(1)}, bf16[16,16,128]{2,1,0:T(8,128)(2,1)S(1)}, u32[]{:S(2)}, u32[]{:S(2)}) collective-permute-start(bf16[16,16,128]{2,1,0:T(8,128)(2,1)S(1)} %gram.1.refs_0_), channel_id=1, source_target_pairs={{0,12},{1,13},{2,14},{3,15},{4,8},{5,9},{6,10},{7,11},{8,4},{9,5},... | collective-permute-start | bytes 196616 | tf_op jit(solution)/shard_map/ppermute | solution.py:244
  83.6 6.2 %collective-permute-start.15 = (bf16[16,16,128]{2,1,0:T(8,128)(2,1)S(1)}, bf16[16,16,128]{2,1,0:T(8,128)(2,1)S(1)}, u32[]{:S(2)}, u32[]{:S(2)}) collective-permute-start(bf16[16,16,128]{2,1,0:T(8,128)(2,1)S(1)} %gram.1.refs_0_), channel_id=1, source_target_pairs={{0,8},{1,9},{2,10},{3,11},{4,12},{5,13},{6,14},{7,15},{8,0},{9,1},... | collective-permute-start | bytes 196616 | tf_op jit(solution)/shard_map/ppermute | solution.py:244
  83.6 7.7 %collective-permute-start.14 = (bf16[16,16,128]{2,1,0:T(8,128)(2,1)S(1)}, bf16[16,16,128]{2,1,0:T(8,128)(2,1)S(1)}, u32[]{:S(2)}, u32[]{:S(2)}) collective-permute-start(bf16[16,16,128]{2,1,0:T(8,128)(2,1)S(1)} %gram.1.refs_0_), channel_id=1, source_target_pairs={{0,4},{1,5},{2,6},{3,7},{4,0},{5,1},{6,2},{7,3},{8,12},{9,13},{10,... | collective-permute-start | bytes 196616 | tf_op jit(solution)/shard_map/ppermute | solution.py:244
  84.6 7.2 %collective-permute-start.17 = (bf16[16,16,128]{2,1,0:T(8,128)(2,1)S(1)}, bf16[16,16,128]{2,1,0:T(8,128)(2,1)S(1)}, u32[]{:S(2)}, u32[]{:S(2)}) collective-permute-start(bf16[16,16,128]{2,1,0:T(8,128)(2,1)S(1)} %gram.1.refs_0_), channel_id=1, source_target_pairs={{0,2},{1,3},{2,0},{3,1},{4,6},{5,7},{6,4},{7,5},{8,10},{9,11},{10,... | collective-permute-start | bytes 196616 | tf_op jit(solution)/shard_map/ppermute | solution.py:244
  87.1 4.7 %collective-permute-start.20 = (bf16[16,16,128]{2,1,0:T(8,128)(2,1)S(1)}, bf16[16,16,128]{2,1,0:T(8,128)(2,1)S(1)}, u32[]{:S(2)}, u32[]{:S(2)}) collective-permute-start(bf16[16,16,128]{2,1,0:T(8,128)(2,1)S(1)} %collective-permute-done.16.refs_3_), channel_id=1, source_target_pairs={{0,2},{1,3},{2,0},{3,1},{4,6},{5,7},{6,4},{7,5},{8,10},{9,11},{10,... | collective-permute-start | bytes 196616 | tf_op jit(solution)/shard_map/ppermute | solution.py:244
  89.8 4.8 %collective-permute-start.19 = (bf16[16,16,128]{2,1,0:T(8,128)(2,1)S(1)}, bf16[16,16,128]{2,1,0:T(8,128)(2,1)S(1)}, u32[]{:S(2)}, u32[]{:S(2)}) collective-permute-start(bf16[16,16,128]{2,1,0:T(8,128)(2,1)S(1)} %collective-permute-done.15.refs_2_), channel_id=1, source_target_pairs={{0,2},{1,3},{2,0},{3,1},{4,6},{5,7},{6,4},{7,5},{8,10},{9,11},{10,... | collective-permute-start | bytes 196616 | tf_op jit(solution)/shard_map/ppermute | solution.py:244
  91.3 4.3 %collective-permute-start.18 = (bf16[16,16,128]{2,1,0:T(8,128)(2,1)S(1)}, bf16[16,16,128]{2,1,0:T(8,128)(2,1)S(1)}, u32[]{:S(2)}, u32[]{:S(2)}) collective-permute-start(bf16[16,16,128]{2,1,0:T(8,128)(2,1)S(1)} %collective-permute-done.14.refs_1_), channel_id=1, source_target_pairs={{0,2},{1,3},{2,0},{3,1},{4,6},{5,7},{6,4},{7,5},{8,10},{9,11},{10,... | collective-permute-start | bytes 196616 | tf_op jit(solution)/shard_map/ppermute | solution.py:244
